TPU v7x, 32 devices: a whole 2x2x4 slice. The times are simulated.
32 devices in a mesh: dp: 8 (over y, x, core), seq: 4 (over z).
Axes of the slice: x: 2, y: 2, z: 4, core: 2. Of those that a mesh axis runs over, the one named last changes fastest.
Arguments:
- hidden_in: bfloat16 [16384, 2048], P(('dp', 'seq')), may hold values from -6 to 6
- out_grad: bfloat16 [16384, 2048], P(('dp', 'seq')), may hold values from -6 to 6
- seq_lengths: int32 [8, 2], P('dp'), may hold values from 0 to 2048, as said below
- seq_counts: int32 [8], P('dp'), may hold values from 1 to 2, as said below
- segment_ids: int32 [8, 2048], P('dp'), may hold values from 0 to 1, as said below
- qkv_weight: float32 [2048, 2560], P(('dp', 'seq')), may hold values from -0.125 to 0.125
- qkv_m: float32 [2048, 2560], P(('dp', 'seq'))
- qkv_v: float32 [2048, 2560], P(('dp', 'seq'))
- out_weight: float32 [2048, 2048], P(('dp', 'seq')), may hold values from -1 to 1
- out_m: float32 [2048, 2048], P(('dp', 'seq'))
- out_v: float32 [2048, 2048], P(('dp', 'seq'))
- gate_up_weight: float32 [2048, 11264], P(('dp', 'seq')), may hold values from -0.125 to 0.125
- gate_up_m: float32 [2048, 11264], P(('dp', 'seq'))
- gate_up_v: float32 [2048, 11264], P(('dp', 'seq'))
- down_weight: float32 [5632, 2048], P(('dp', 'seq')), may hold values from -0.078125 to 0.078125
- down_m: float32 [5632, 2048], P(('dp', 'seq'))
- down_v: float32 [5632, 2048], P(('dp', 'seq'))
- norm_gains: float32 [2, 2048], P(None, ('dp', 'seq')), may hold values from 0.4 to 3.2, as said below
- gain_m: float32 [2, 2048], P(None, ('dp', 'seq'))
- gain_v: float32 [2, 2048], P(None, ('dp', 'seq'))
Outputs:
- block_out: bfloat16 [16384, 2048], P(('dp', 'seq'))
- input_grad: float32 [16384, 2048], P(('dp', 'seq'))
- grad_norm: float32 [], replicated
- new_qkv: float32 [2048, 2560], P(('dp', 'seq'))
- new_qkv_m: float32 [2048, 2560], P(('dp', 'seq'))
- new_qkv_v: float32 [2048, 2560], P(('dp', 'seq'))
- new_out: float32 [2048, 2048], P(('dp', 'seq'))
- new_out_m: float32 [2048, 2048], P(('dp', 'seq'))
- new_out_v: float32 [2048, 2048], P(('dp', 'seq'))
- new_gate_up: float32 [2048, 11264], P(('dp', 'seq'))
- new_gate_up_m: float32 [2048, 11264], P(('dp', 'seq'))
- new_gate_up_v: float32 [2048, 11264], P(('dp', 'seq'))
- new_down: float32 [5632, 2048], P(('dp', 'seq'))
- new_down_m: float32 [5632, 2048], P(('dp', 'seq'))
- new_down_v: float32 [5632, 2048], P(('dp', 'seq'))
- new_gains: float32 [2, 2048], P(None, ('dp', 'seq'))
- new_gain_m: float32 [2, 2048], P(None, ('dp', 'seq'))
- new_gain_v: float32 [2, 2048], P(None, ('dp', 'seq'))
Inputs may be any that keep to these rules, and one draw needn't show every extreme that they name: `seq_lengths`: row g is (1024, 1024) for a group of two sequences and (2048, 0) for a group of one; every draw has groups of both kinds. `seq_counts`: agrees with seq_lengths: the number of its nonzero entries. `segment_ids`: agrees with seq_lengths: token t of group g lies in sequence j where the sum of seq_lengths[g, i] over i < j is at most t and t is below that sum plus seq_lengths[g, j]. `norm_gains`: Positive.
All inputs are finite; a program needn't handle non-finite values.
Results may differ from a plain program's by a relative error of at most 0.014.
The roundings to bfloat16 on the way count: a program that leaves them out, or rounds other values in their place, can miss the bound.
Values may be sent and summed in bfloat16 or wider, within the bound.
A program may use at most 448 MiB of HBM per device.

v0:
```python
import jax
import jax.numpy as jnp
from jax import lax
from jax.sharding import PartitionSpec as P

HEADS = 32
KV_HEADS = 4
HD = 64
FF = 5632
STEP = 10


NORM_EPS = 1e-05
ROPE_BASE = 10000.0
CLIP_NORM = 1.0
BETA_ONE = 0.9
BETA_TWO = 0.999
ADAM_EPS = 1e-08
WEIGHT_DECAY = 0.1
MASKED = -1e30


def matmul(left, right):
    return jnp.dot(left, right, preferred_element_type=jnp.float32)


def contract(left, right, left_dim, right_dim):
    return lax.dot_general(
        left, right, (((left_dim,), (right_dim,)), ((), ())), preferred_element_type=jnp.float32
    )


def rope_tables(positions):
    half_dim = HD // 2
    inverse = jnp.exp(-(2.0 * jnp.arange(half_dim, dtype=jnp.float32) / HD) * jnp.log(ROPE_BASE))
    angles = positions.astype(jnp.float32)[:, None] * inverse[None, :]
    return (jnp.cos(angles)[:, None, :], jnp.sin(angles)[:, None, :])


def rotate(vector, cos_table, sin_table):
    half_dim = vector.shape[-1] // 2
    first_half, second_half = (vector[..., :half_dim], vector[..., half_dim:])
    return jnp.concatenate(
        [
            first_half * cos_table - second_half * sin_table,
            second_half * cos_table + first_half * sin_table,
        ],
        -1,
    )


def unrotate(gradient, cos_table, sin_table):
    half_dim = gradient.shape[-1] // 2
    first_half, second_half = (gradient[..., :half_dim], gradient[..., half_dim:])
    return jnp.concatenate(
        [
            first_half * cos_table + second_half * sin_table,
            second_half * cos_table - first_half * sin_table,
        ],
        -1,
    )


def allowed_mask(row_ids, seg_rows, seg_all, seq_count):
    col_ids = jnp.arange(seg_all.shape[0], dtype=jnp.int32)
    earlier = (
        (col_ids[None, :] < row_ids[:, None])
        & (seg_all[None, :] == seg_rows[:, None])
        & (seg_all[None, :] < seq_count)
    )
    return earlier | (col_ids[None, :] == row_ids[:, None])


def norm_forward(rows_in, gain_row):
    inv_rms = lax.rsqrt(jnp.mean(rows_in * rows_in, axis=-1, keepdims=True) + NORM_EPS)
    return (inv_rms, rows_in * inv_rms * gain_row)


def norm_backward(rows_in, inv_rms, gain_row, gradient):
    weighted = gain_row * gradient
    back_rows = inv_rms * weighted - rows_in * inv_rms**3 * jnp.mean(
        weighted * rows_in, axis=-1, keepdims=True
    )
    return (back_rows, jnp.sum(gradient * rows_in * inv_rms, axis=0))


def head_scores(query_blk, key_one, row_start, block_rows, seg_all, seq_count):
    row_ids = row_start + jnp.arange(block_rows, dtype=jnp.int32)
    seg_rows = lax.dynamic_slice_in_dim(seg_all, row_start, block_rows, 0)
    scores = contract(query_blk, key_one, 1, 1) * HD ** (-0.5)
    return jnp.where(allowed_mask(row_ids, seg_rows, seg_all, seq_count), scores, MASKED)


def attend_forward(query_heads, kv_heads, seg_all, seq_count):
    group_size, per_dev = (query_heads.shape[0], query_heads.shape[1])
    head_share = per_dev // kv_heads.shape[1]
    block_rows = min(512, group_size)
    starts = jnp.arange(group_size // block_rows, dtype=jnp.int32) * block_rows

    def one_head(head_idx):
        query_one = lax.dynamic_index_in_dim(query_heads, head_idx, 1, keepdims=False)
        kv_one = lax.dynamic_index_in_dim(kv_heads, head_idx // head_share, 1, keepdims=False)
        key_one, value_one = (kv_one[:, :HD], kv_one[:, HD:])

        def one_block(row_start):
            query_blk = lax.dynamic_slice_in_dim(query_one, row_start, block_rows, 0)
            scores = head_scores(query_blk, key_one, row_start, block_rows, seg_all, seq_count)
            row_max = jnp.max(scores, -1, keepdims=True)
            exp_vals = jnp.exp(scores - row_max)
            exp_total = jnp.sum(exp_vals, -1, keepdims=True)
            probability = (exp_vals / exp_total).astype(jnp.bfloat16)
            return (matmul(probability, value_one), (row_max + jnp.log(exp_total))[:, 0])

        head_outs, log_sums = lax.map(one_block, starts)
        return (head_outs.reshape(group_size, HD), log_sums.reshape(group_size))

    return lax.map(one_head, jnp.arange(per_dev, dtype=jnp.int32))


def attend_backward(query_heads, kv_heads, grad_heads, log_sums, seg_all, seq_count):
    group_size, per_dev = (query_heads.shape[0], query_heads.shape[1])
    kv_dev = kv_heads.shape[1]
    head_share = per_dev // kv_dev
    block_rows = min(512, group_size)
    starts = jnp.arange(group_size // block_rows, dtype=jnp.int32) * block_rows

    def one_head(head_idx):
        query_one = lax.dynamic_index_in_dim(query_heads, head_idx, 1, keepdims=False)
        grad_one = lax.dynamic_index_in_dim(grad_heads, head_idx, 1, keepdims=False)
        kv_one = lax.dynamic_index_in_dim(kv_heads, head_idx // head_share, 1, keepdims=False)
        key_one, value_one = (kv_one[:, :HD], kv_one[:, HD:])
        lse_one = lax.dynamic_index_in_dim(log_sums, head_idx, 0, keepdims=False)

        def one_block(carry, row_start):
            d_key, d_value = carry
            query_blk = lax.dynamic_slice_in_dim(query_one, row_start, block_rows, 0)
            grad_blk = lax.dynamic_slice_in_dim(grad_one, row_start, block_rows, 0)
            lse_blk = lax.dynamic_slice_in_dim(lse_one, row_start, block_rows, 0)
            scores = head_scores(query_blk, key_one, row_start, block_rows, seg_all, seq_count)
            probability = jnp.exp(scores - lse_blk[:, None])
            d_prob = contract(grad_blk, value_one, 1, 1)
            centre = jnp.sum(probability * d_prob, -1, keepdims=True)
            d_score = (probability * (d_prob - centre) * HD ** (-0.5)).astype(jnp.bfloat16)
            d_query_blk = matmul(d_score, key_one)
            d_key = d_key + contract(d_score, query_blk, 0, 0)
            d_value = d_value + contract(probability.astype(jnp.bfloat16), grad_blk, 0, 0)
            return ((d_key, d_value), d_query_blk)

        zeros_init = jnp.zeros((group_size, HD), jnp.float32)
        (d_key, d_value), d_query = lax.scan(one_block, (zeros_init, zeros_init), starts)
        return (d_query.reshape(group_size, HD), d_key, d_value)

    d_query, d_key, d_value = lax.map(one_head, jnp.arange(per_dev, dtype=jnp.int32))
    d_key = d_key.reshape(kv_dev, head_share, group_size, HD).sum(1)
    d_value = d_value.reshape(kv_dev, head_share, group_size, HD).sum(1)
    return (d_query, jnp.concatenate([d_key, d_value], -1))


def adam_update(weight, first_mom, second_mom, gradient, clip_factor, rate, decay):
    step_grad = gradient * clip_factor
    first_new = BETA_ONE * first_mom + (1.0 - BETA_ONE) * step_grad
    second_new = BETA_TWO * second_mom + (1.0 - BETA_TWO) * step_grad * step_grad
    mean_hat = first_new / (1.0 - BETA_ONE**STEP)
    square_hat = second_new / (1.0 - BETA_TWO**STEP)
    weight_new = weight - rate * (mean_hat / (jnp.sqrt(square_hat) + ADAM_EPS) + decay * weight)
    return (weight_new, first_new, second_new)


def per_device(
    hidden_in,
    out_grad,
    seq_lengths,
    seq_counts,
    segment_ids,
    qkv_weight,
    qkv_m,
    qkv_v,
    out_weight,
    out_m,
    out_v,
    gate_up_weight,
    gate_up_m,
    gate_up_v,
    down_weight,
    down_m,
    down_v,
    norm_gains,
    gain_m,
    gain_v,
):
    tok_dev = hidden_in.shape[0]
    seq_size = lax.axis_size("seq")
    q_width = HEADS * HD
    kv_width = KV_HEADS * HD
    per_dev = HEADS // seq_size
    copies = max(1, seq_size // KV_HEADS)
    group_size = tok_dev * seq_size
    seg_all = segment_ids[0]
    seq_count = seq_counts[0]
    lengths = seq_lengths[0]
    offset = lax.axis_index("seq") * tok_dev
    seg_local = lax.dynamic_slice_in_dim(seg_all, offset, tok_dev, 0)
    starts = jnp.cumsum(lengths, dtype=jnp.int32) - lengths
    slot_ids = jnp.arange(lengths.shape[0], dtype=jnp.int32)
    seq_start = jnp.sum(
        jnp.where(seg_local[:, None] == slot_ids[None, :], starts[None, :], 0),
        axis=1,
        dtype=jnp.int32,
    )
    positions = offset + jnp.arange(tok_dev, dtype=jnp.int32) - seq_start
    cos_table, sin_table = rope_tables(positions)
    w_qkv, w_out, w_gain = (
        lax.all_gather(qkv_weight.astype(jnp.bfloat16), ("dp", "seq"), axis=0, tiled=True),
        lax.all_gather(out_weight.astype(jnp.bfloat16), ("dp", "seq"), axis=0, tiled=True),
        lax.all_gather(norm_gains.astype(jnp.bfloat16), ("dp", "seq"), axis=1, tiled=True),
    )
    gain_attn = w_gain[0].astype(jnp.float32)
    gain_mlp = w_gain[1].astype(jnp.float32)
    residual = hidden_in.astype(jnp.float32)
    inv_one, normed = norm_forward(residual, gain_attn)
    normed_low = normed.astype(jnp.bfloat16)
    qkv_out = matmul(normed_low, w_qkv)
    query_rot = rotate(
        qkv_out[:, :q_width].reshape(tok_dev, HEADS, HD), cos_table, sin_table
    ).astype(jnp.bfloat16)
    key_rot = rotate(
        qkv_out[:, q_width : q_width + kv_width].reshape(tok_dev, KV_HEADS, HD),
        cos_table,
        sin_table,
    ).astype(jnp.bfloat16)
    value_rows = (
        qkv_out[:, q_width + kv_width :].reshape(tok_dev, KV_HEADS, HD).astype(jnp.bfloat16)
    )
    kv_pairs = jnp.repeat(jnp.concatenate([key_rot, value_rows], -1), copies, axis=1)
    query_send = query_rot.reshape(tok_dev, seq_size, per_dev * HD)
    query_heads, kv_heads = (
        lax.all_to_all(query_send, "seq", split_axis=1, concat_axis=0, tiled=True),
        lax.all_to_all(kv_pairs, "seq", split_axis=1, concat_axis=0, tiled=True),
    )
    query_heads = query_heads.reshape(group_size, per_dev, HD)
    head_outs, log_sums = attend_forward(query_heads, kv_heads, seg_all, seq_count)
    back_send = (
        jnp.moveaxis(head_outs, 0, 1).astype(jnp.bfloat16).reshape(group_size, 1, per_dev * HD)
    )
    attended = lax.all_to_all(back_send, "seq", split_axis=0, concat_axis=1, tiled=True).reshape(
        tok_dev, q_width
    )
    mid_rows = residual + matmul(attended, w_out)
    w_gu, w_down = (
        lax.all_gather(gate_up_weight.astype(jnp.bfloat16), ("dp", "seq"), axis=0, tiled=True),
        lax.all_gather(down_weight.astype(jnp.bfloat16), ("dp", "seq"), axis=0, tiled=True),
    )
    inv_two, normed_two = norm_forward(mid_rows, gain_mlp)
    inner_rows = normed_two.astype(jnp.bfloat16)
    gate_up = matmul(inner_rows, w_gu)
    gate_vals, up_vals = (gate_up[:, :FF], gate_up[:, FF:])
    sigmoid_gate = jax.nn.sigmoid(gate_vals)
    hidden = (gate_vals * sigmoid_gate * up_vals).astype(jnp.bfloat16)
    block_out = (mid_rows + matmul(hidden, w_down)).astype(jnp.bfloat16)
    w_gu, w_down = (
        lax.all_gather(gate_up_weight.astype(jnp.bfloat16), ("dp", "seq"), axis=0, tiled=True),
        lax.all_gather(down_weight.astype(jnp.bfloat16), ("dp", "seq"), axis=0, tiled=True),
    )
    d_hidden = contract(out_grad, w_down, 1, 1)
    g_down = contract(hidden, out_grad, 0, 0)
    d_gate = d_hidden * up_vals * sigmoid_gate * (1.0 + gate_vals * (1.0 - sigmoid_gate))
    d_up = d_hidden * gate_vals * sigmoid_gate
    d_gu = jnp.concatenate([d_gate, d_up], -1).astype(jnp.bfloat16)
    d_inner = contract(d_gu, w_gu, 1, 1)
    g_gu = contract(inner_rows, d_gu, 0, 0)
    back_two, g_gain_two = norm_backward(mid_rows, inv_two, gain_mlp, d_inner)
    d_mid = out_grad.astype(jnp.float32) + back_two
    g_gu_own, g_down_own = (
        lax.psum_scatter(g_gu, ("dp", "seq"), scatter_dimension=0, tiled=True),
        lax.psum_scatter(g_down, ("dp", "seq"), scatter_dimension=0, tiled=True),
    )
    w_qkv, w_out, w_gain = (
        lax.all_gather(qkv_weight.astype(jnp.bfloat16), ("dp", "seq"), axis=0, tiled=True),
        lax.all_gather(out_weight.astype(jnp.bfloat16), ("dp", "seq"), axis=0, tiled=True),
        lax.all_gather(norm_gains.astype(jnp.bfloat16), ("dp", "seq"), axis=1, tiled=True),
    )
    gain_attn = w_gain[0].astype(jnp.float32)
    d_branch = d_mid.astype(jnp.bfloat16)
    g_out = contract(attended, d_branch, 0, 0)
    d_attended = contract(d_branch, w_out, 1, 1).astype(jnp.bfloat16)
    grad_heads = lax.all_to_all(
        d_attended.reshape(tok_dev, seq_size, per_dev * HD),
        "seq",
        split_axis=1,
        concat_axis=0,
        tiled=True,
    ).reshape(group_size, per_dev, HD)
    d_query, d_pairs = attend_backward(
        query_heads, kv_heads, grad_heads, log_sums, seg_all, seq_count
    )
    dq_send = jnp.moveaxis(d_query, 0, 1).reshape(group_size, 1, per_dev * HD)
    dkv_send = jnp.moveaxis(d_pairs, 0, 1)
    dq_back, dkv_back = (
        lax.all_to_all(dq_send, "seq", split_axis=0, concat_axis=1, tiled=True),
        lax.all_to_all(dkv_send, "seq", split_axis=0, concat_axis=1, tiled=True),
    )
    dq_back = dq_back.reshape(tok_dev, HEADS, HD)
    dkv_back = dkv_back.reshape(tok_dev, KV_HEADS, copies, 2 * HD).sum(2)
    d_query_raw = unrotate(dq_back, cos_table, sin_table).reshape(tok_dev, q_width)
    d_key_raw = unrotate(dkv_back[..., :HD], cos_table, sin_table).reshape(tok_dev, kv_width)
    d_value_raw = dkv_back[..., HD:].reshape(tok_dev, kv_width)
    d_qkv = jnp.concatenate([d_query_raw, d_key_raw, d_value_raw], -1).astype(jnp.bfloat16)
    d_normed = contract(d_qkv, w_qkv, 1, 1)
    g_qkv = contract(normed_low, d_qkv, 0, 0)
    back_one, g_gain_one = norm_backward(residual, inv_one, gain_attn, d_normed)
    input_grad = d_mid + back_one
    g_gains = jnp.stack([g_gain_one, g_gain_two], 0)
    g_qkv_own, g_out_own, g_gains_own = (
        lax.psum_scatter(g_qkv, ("dp", "seq"), scatter_dimension=0, tiled=True),
        lax.psum_scatter(g_out, ("dp", "seq"), scatter_dimension=0, tiled=True),
        lax.psum_scatter(g_gains, ("dp", "seq"), scatter_dimension=1, tiled=True),
    )
    local_sq = (
        jnp.sum(g_qkv_own * g_qkv_own)
        + jnp.sum(g_out_own * g_out_own)
        + jnp.sum(g_gu_own * g_gu_own)
        + jnp.sum(g_down_own * g_down_own)
        + jnp.sum(g_gains_own * g_gains_own)
    )
    total_sq = lax.psum(local_sq, ("dp", "seq"))
    grad_norm = jnp.sqrt(total_sq)
    clip_factor = jnp.minimum(1.0, CLIP_NORM / (grad_norm + 1e-06))
    new_qkv, new_qkv_m, new_qkv_v = adam_update(
        qkv_weight, qkv_m, qkv_v, g_qkv_own, clip_factor, 0.06, WEIGHT_DECAY
    )
    new_out, new_out_m, new_out_v = adam_update(
        out_weight, out_m, out_v, g_out_own, clip_factor, 0.4, WEIGHT_DECAY
    )
    new_gu, new_gu_m, new_gu_v = adam_update(
        gate_up_weight, gate_up_m, gate_up_v, g_gu_own, clip_factor, 0.06, WEIGHT_DECAY
    )
    new_down, new_down_m, new_down_v = adam_update(
        down_weight, down_m, down_v, g_down_own, clip_factor, 0.06, WEIGHT_DECAY
    )
    new_gains, new_gain_m, new_gain_v = adam_update(
        norm_gains, gain_m, gain_v, g_gains_own, clip_factor, 0.6, 0.0
    )
    return (
        block_out,
        input_grad,
        grad_norm,
        new_qkv,
        new_qkv_m,
        new_qkv_v,
        new_out,
        new_out_m,
        new_out_v,
        new_gu,
        new_gu_m,
        new_gu_v,
        new_down,
        new_down_m,
        new_down_v,
        new_gains,
        new_gain_m,
        new_gain_v,
    )


def solution(mesh):
    in_specs = (
        P(("dp", "seq"), None),
        P(("dp", "seq"), None),
        P("dp", None),
        P("dp"),
        P("dp", None),
        P(("dp", "seq"), None),
        P(("dp", "seq"), None),
        P(("dp", "seq"), None),
        P(("dp", "seq"), None),
        P(("dp", "seq"), None),
        P(("dp", "seq"), None),
        P(("dp", "seq"), None),
        P(("dp", "seq"), None),
        P(("dp", "seq"), None),
        P(("dp", "seq"), None),
        P(("dp", "seq"), None),
        P(("dp", "seq"), None),
        P(None, ("dp", "seq")),
        P(None, ("dp", "seq")),
        P(None, ("dp", "seq")),
    )
    out_specs = (
        P(("dp", "seq"), None),
        P(("dp", "seq"), None),
        P(),
        P(("dp", "seq"), None),
        P(("dp", "seq"), None),
        P(("dp", "seq"), None),
        P(("dp", "seq"), None),
        P(("dp", "seq"), None),
        P(("dp", "seq"), None),
        P(("dp", "seq"), None),
        P(("dp", "seq"), None),
        P(("dp", "seq"), None),
        P(("dp", "seq"), None),
        P(("dp", "seq"), None),
        P(("dp", "seq"), None),
        P(None, ("dp", "seq")),
        P(None, ("dp", "seq")),
        P(None, ("dp", "seq")),
    )
    return jax.shard_map(
        per_device, mesh=mesh, in_specs=in_specs, out_specs=out_specs, check_vma=False
    )
```

profile of v0, /device:TPU:0, one launch (start us, length us, event | category | flops | bytes accessed | tf_op | source)
XLA Modules:
  0.0 5651.1 jit_solution(14452878118659012048)
XLA Ops:
  14.3 69.9 %all-gather = bf16[32,64,2]{1,2,0:T(2,128)(2,1)S(1)} all-gather(bf16[1,64,2]{1,2,0:T(2,128)(2,1)S(1)} %convert_bitcast_fusion), channel_id=1, replica_groups=mesh['dp'=8,'seq'=4] {'dp','seq'}, dimensions={0}, use_global_device_ids=true | all-gather | bytes 8448 | tf_op jit(solution)/shard_map/all_gather | solution.py:215
  86.7 14.4 all-gather.6.cloned.1.call-done
  101.1 8.4 fusion.47
  121.4 5.4 copy.110
  142.5 75.5 %all-to-all-done = bf16[512,4,512]{0,2,1:T(8,128)(2,1)S(1)} async-done(((bf16[512,4,512]{0,2,1:T(8,128)(2,1)}), bf16[512,4,512]{0,2,1:T(8,128)(2,1)S(1)}, u32[]{:S(2)}, u32[]{:S(2)}) %all-to-all-start) | async-done | bytes 2097184 | tf_op jit(solution)/shard_map/all_to_all | solution.py:237
  227.3 306.9 %while.64 = (s32[]{:T(128)}, bf16[8,2048,64]{1,2,0:T(8,128)(2,1)}, f32[8,2048]{1,0:T(8,128)}, s32[8]{0:T(128)S(1)}, bf16[2048,8,64]{2,0,1:T(8,128)(2,1)}, /*inde...) while((s32[]{:T(128)}, bf16[8,2048,64]{1,2,0:T(8,128)(2,1)}, ...), condition=%wide.region_8.9_spmd.clone.clone, body=%wide.region_3.8_spmd.clone.sunk.clone | while | flops 283117568 | bytes 17123856 | solution.py:117
  231.2 31.8 while.63
  269.6 31.8 while.63
  307.9 31.7 while.63
  346.4 31.8 while.63
  384.8 31.7 while.63
  423.1 31.8 while.63
  461.4 31.8 while.63
  499.8 31.7 while.63
  545.7 104.4 %all_to_all.93 = bf16[4,2,131072]{2,1,0:T(2,128)(2,1)S(1)} all-to-all(bf16[4,2,131072]{2,1,0:T(2,128)(2,1)} %reshape.267), channel_id=1, replica_groups=mesh['dp'=8,'seq'=4] {'seq'}, dimensions={0} | all-to-all | bytes 4194304 | tf_op jit(solution)/shard_map/all_to_all | solution.py:245
  658.6 11.7 multiply_reduce_fusion.3
  670.4 33.2 fusion.56
  703.6 27.1 multiply_convert_fusion.2
  730.7 34.7 multiply_reduce_fusion.1
  772.0 8.2 convolution_convert_fusion
  786.5 43.4 all-to-all-done.3
  842.2 705.4 %while.66 = (s32[]{:T(128)}, f32[8,2048,64]{1,2,0:T(8,128)}, f32[8,2048,64]{1,2,0:T(8,128)}, f32[8,2048,64]{1,2,0:T(8,128)}, s32[8]{0:T(128)S(1)}, /*index=5*/bf...) while((s32[]{:T(128)}, f32[8,2048,64]{1,2,0:T(8,128)}, ...), condition=%wide.region_15.16_spmd.clone.clone, body=%wide.region_11.15_spmd.clone.sunk.clone | while | flops 688392192 | bytes 64414408 | solution.py:153
  850.5 76.2 %while.65 = (s32[]{:T(128)}, f32[2048,64]{0,1:T(8,128)}, f32[2048,64]{0,1:T(8,128)S(1)}, f32[4,512,64]{1,2,0:T(8,128)}, s32[4]{0:T(128)S(1)}, /*index=5*/s32[1,2...) while((s32[]{:T(128)}, f32[2048,64]{0,1:T(8,128)}, ...), condition=%wide.region_14.14_spmd.clone, body=%wide.region_12.13_spmd.clone.sunk | while | flops 688392192 | bytes 52338964 | solution.py:150
  938.7 76.2 %while.65 = (s32[]{:T(128)}, f32[2048,64]{0,1:T(8,128)}, f32[2048,64]{0,1:T(8,128)S(1)}, f32[4,512,64]{1,2,0:T(8,128)}, s32[4]{0:T(128)S(1)}, /*index=5*/s32[1,2...) while((s32[]{:T(128)}, f32[2048,64]{0,1:T(8,128)}, ...), condition=%wide.region_14.14_spmd.clone, body=%wide.region_12.13_spmd.clone.sunk | while | flops 688392192 | bytes 52338964 | solution.py:150
  1026.8 76.2 %while.65 = (s32[]{:T(128)}, f32[2048,64]{0,1:T(8,128)}, f32[2048,64]{0,1:T(8,128)S(1)}, f32[4,512,64]{1,2,0:T(8,128)}, s32[4]{0:T(128)S(1)}, /*index=5*/s32[1,2...) while((s32[]{:T(128)}, f32[2048,64]{0,1:T(8,128)}, ...), condition=%wide.region_14.14_spmd.clone, body=%wide.region_12.13_spmd.clone.sunk | while | flops 688392192 | bytes 52338964 | solution.py:150
  1115.1 76.2 %while.65 = (s32[]{:T(128)}, f32[2048,64]{0,1:T(8,128)}, f32[2048,64]{0,1:T(8,128)S(1)}, f32[4,512,64]{1,2,0:T(8,128)}, s32[4]{0:T(128)S(1)}, /*index=5*/s32[1,2...) while((s32[]{:T(128)}, f32[2048,64]{0,1:T(8,128)}, ...), condition=%wide.region_14.14_spmd.clone, body=%wide.region_12.13_spmd.clone.sunk | while | flops 688392192 | bytes 52338964 | solution.py:150
  1203.2 76.2 %while.65 = (s32[]{:T(128)}, f32[2048,64]{0,1:T(8,128)}, f32[2048,64]{0,1:T(8,128)S(1)}, f32[4,512,64]{1,2,0:T(8,128)}, s32[4]{0:T(128)S(1)}, /*index=5*/s32[1,2...) while((s32[]{:T(128)}, f32[2048,64]{0,1:T(8,128)}, ...), condition=%wide.region_14.14_spmd.clone, body=%wide.region_12.13_spmd.clone.sunk | while | flops 688392192 | bytes 52338964 | solution.py:150
  1291.4 76.2 %while.65 = (s32[]{:T(128)}, f32[2048,64]{0,1:T(8,128)}, f32[2048,64]{0,1:T(8,128)S(1)}, f32[4,512,64]{1,2,0:T(8,128)}, s32[4]{0:T(128)S(1)}, /*index=5*/s32[1,2...) while((s32[]{:T(128)}, f32[2048,64]{0,1:T(8,128)}, ...), condition=%wide.region_14.14_spmd.clone, body=%wide.region_12.13_spmd.clone.sunk | while | flops 688392192 | bytes 52338964 | solution.py:150
  1379.5 76.2 %while.65 = (s32[]{:T(128)}, f32[2048,64]{0,1:T(8,128)}, f32[2048,64]{0,1:T(8,128)S(1)}, f32[4,512,64]{1,2,0:T(8,128)}, s32[4]{0:T(128)S(1)}, /*index=5*/s32[1,2...) while((s32[]{:T(128)}, f32[2048,64]{0,1:T(8,128)}, ...), condition=%wide.region_14.14_spmd.clone, body=%wide.region_12.13_spmd.clone.sunk | while | flops 688392192 | bytes 52338964 | solution.py:150
  1467.7 76.2 %while.65 = (s32[]{:T(128)}, f32[2048,64]{0,1:T(8,128)}, f32[2048,64]{0,1:T(8,128)S(1)}, f32[4,512,64]{1,2,0:T(8,128)}, s32[4]{0:T(128)S(1)}, /*index=5*/s32[1,2...) while((s32[]{:T(128)}, f32[2048,64]{0,1:T(8,128)}, ...), condition=%wide.region_14.14_spmd.clone, body=%wide.region_12.13_spmd.clone.sunk | while | flops 688392192 | bytes 52338964 | solution.py:150
  1558.1 10.9 copy.126
  1569.0 14.3 all-to-all-done.5
  1588.7 92.1 %all-to-all-done.4 = f32[2048,1,512]{2,1,0:T(1,128)} async-done(((f32[2048,1,512]{2,1,0:T(1,128)}), f32[2048,1,512]{2,1,0:T(1,128)}, u32[]{:S(2)}, u32[]{:S(2)}) %all-to-all-start.4) | async-done | bytes 4194336 | tf_op jit(solution)/shard_map/all_to_all | solution.py:299
  1685.5 5.6 copy.127
  1694.5 13.2 fusion.37
  1709.1 13.2 fusion.42
  1722.3 12.0 fusion.40
  1734.4 24.2 fusion.65
  1759.3 40.3 fusion.27
  1799.6 19.8 add_convert_fusion
  1819.4 26.8 reduce-scatter.16.cloned.1.call-done
  1847.6 361.5 %reduce-scatter.10.cloned.1.call-done = f32[64,2048]{1,0:T(8,128)} async-done(((f32[2048,2048]{1,0:T(8,128)}), f32[64,2048]{1,0:T(8,128)}) %reduce-scatter.10.cloned.1.call-update) | async-done | bytes 524304 | tf_op jit(solution)/shard_map/reduce_scatter | solution.py:315
  2210.9 449.1 %reduce-scatter.8.cloned.1.call-done = f32[64,2560]{1,0:T(8,128)} async-done(((f32[2048,2560]{1,0:T(8,128)}), f32[64,2560]{1,0:T(8,128)}) %reduce-scatter.8.cloned.1.call-update) | async-done | bytes 655376 | tf_op jit(solution)/shard_map/reduce_scatter | solution.py:314
  2663.2 970.6 %reduce-scatter.14.cloned.1.call-done = f32[176,2048]{1,0:T(8,128)} async-done(((f32[5632,2048]{1,0:T(8,128)}), f32[176,2048]{1,0:T(8,128)}) %reduce-scatter.14.cloned.1.call-update) | async-done | bytes 1441808 | tf_op jit(solution)/shard_map/reduce_scatter | solution.py:275
  3636.1 1936.1 %reduce-scatter.12.cloned.1.call-done = f32[64,11264]{1,0:T(8,128)} async-done(((f32[2048,11264]{1,0:T(8,128)}), f32[64,11264]{1,0:T(8,128)}) %reduce-scatter.12.cloned.1.call-update) | async-done | bytes 2883600 | tf_op jit(solution)/shard_map/reduce_scatter | solution.py:274
  5577.4 6.6 fusion.34
  5584.0 40.8 psum.7
  5632.5 7.9 multiply_subtract_fusion
  (1111 shorter events, 991.0 us)
Async XLA Ops:
  7.2 7.1 copy-start.35
  7.2 77.1 %copy-start.39 = (s32[1,2]{1,0:T(1,128)S(1)}, s32[1,2]{1,0:T(1,128)}, u32[]{:S(2)}) copy-start(s32[1,2]{1,0:T(1,128)} %param.30) | copy-start | bytes 28
  7.2 77.3 %copy-start.5 = (s32[1,2048]{1,0:T(1,128)S(1)}, s32[1,2048]{1,0:T(1,128)}, u32[]{:S(2)}) copy-start(s32[1,2048]{1,0:T(1,128)} %param.32) | copy-start | bytes 24580
  7.2 77.4 %copy-start.10 = (bf16[512,2048]{1,0:T(8,128)(2,1)S(1)}, bf16[512,2048]{1,0:T(8,128)(2,1)}, u32[]{:S(2)}) copy-start(bf16[512,2048]{1,0:T(8,128)(2,1)} %param.28) | copy-start | bytes 6291460
  7.2 93.9 %all-gather.6.cloned.1.call-start = ((), (), s32[]{:S(2)}) async-start(), calls=%async_computation.11 | async-start | bytes 10813440 | tf_op jit(solution)/shard_map/all_gather | solution.py:213
  9.3 649.3 %all-gather.8.cloned.1.call-start = ((), (), s32[]{:S(2)}) async-start(), calls=%async_computation.12 | async-start | bytes 8650752 | tf_op jit(solution)/shard_map/all_gather | solution.py:214
  11.1 659.2 %all-gather.10.cloned.1.call-start = ((), (), s32[]{:S(2)}) async-start(), calls=%async_computation.13 | async-start | bytes 47579136 | tf_op jit(solution)/shard_map/all_gather | solution.py:250
  85.7 15.4 copy-start.31
  86.1 40.7 copy-start.18
  86.1 40.7 copy-start.20
  86.7 14.4 copy-start.28
  113.2 21.3 all-to-all-start.1
  134.4 83.6 %all-to-all-start = ((bf16[512,4,512]{0,2,1:T(8,128)(2,1)}), bf16[512,4,512]{0,2,1:T(8,128)(2,1)S(1)}, u32[]{:S(2)}, u32[]{:S(2)}) async-start(bf16[512,4,512]{0,2,1:T(8,128)(2,1)} %bitcast.11), calls=%async_computation | async-start | bytes 4194304 | tf_op jit(solution)/shard_map/all_to_all | solution.py:237
  138.1 565.5 %all-gather.12.cloned.1.call-start = ((), (), s32[]{:S(2)}) async-start(), calls=%async_computation.14 | async-start | bytes 23789568 | tf_op jit(solution)/shard_map/all_gather | solution.py:251
  534.2 7.0 copy-start.2
  658.6 11.7 copy-start.24
  670.3 95.0 %copy-start.26 = (f32[512]{0:T(512)}, f32[512]{0:T(512)S(1)}, u32[]{:S(2)}) copy-start(f32[512]{0:T(512)S(1)} %get-tuple-element.604) | copy-start | bytes 6148
  670.3 33.2 copy-start.17
  782.9 47.0 all-to-all-start.3
  837.3 4.9 copy-start.3
  837.3 4.9 copy-start.6
  926.7 3.7 copy-start.4
  1014.9 3.7 copy-start.4
  1103.1 3.8 copy-start.4
  1279.5 3.7 copy-start.4
  1554.6 28.7 all-to-all-start.5
  1569.0 19.6 copy-start.19
  1569.0 19.6 copy-start.21
  1583.3 97.5 %all-to-all-start.4 = ((f32[2048,1,512]{2,1,0:T(1,128)}), f32[2048,1,512]{2,1,0:T(1,128)}, u32[]{:S(2)}, u32[]{:S(2)}) async-start(f32[2048,1,512]{2,1,0:T(1,128)} %copy.126), calls=%async_computation.4 | async-start | bytes 8388608 | tf_op jit(solution)/shard_map/all_to_all | solution.py:299
  1588.2 258.0 %reduce-scatter.16.cloned.1.call-start = ((), (), s32[]{:S(2)}) async-start(), calls=%async_computation.19 | async-start | bytes 1081344
  1694.4 13.2 copy-start.16
  1694.4 13.2 copy-start.33
  1709.0 500.1 %reduce-scatter.10.cloned.1.call-start = ((), (), s32[]{:S(2)}) async-start(), calls=%async_computation.16 | async-start | bytes 17301504 | tf_op jit(solution)/shard_map/reduce_scatter | solution.py:315
  1722.3 937.7 %reduce-scatter.8.cloned.1.call-start = ((), (), s32[]{:S(2)}) async-start(), calls=%async_computation.15 | async-start | bytes 21626880 | tf_op jit(solution)/shard_map/reduce_scatter | solution.py:314
  1734.3 1899.4 %reduce-scatter.14.cloned.1.call-start = ((), (), s32[]{:S(2)}) async-start(), calls=%async_computation.18 | async-start | bytes 47579136 | tf_op jit(solution)/shard_map/reduce_scatter | solution.py:275
  1758.6 3813.6 %reduce-scatter.12.cloned.1.call-start = ((), (), s32[]{:S(2)}) async-start(), calls=%async_computation.17 | async-start | bytes 95158272 | tf_op jit(solution)/shard_map/reduce_scatter | solution.py:274
  1799.6 19.8 copy-start.34
  1819.4 3757.9 %copy-start.30 = (f32[512]{0:T(512)S(1)}, f32[512]{0:T(512)}, u32[]{:S(2)}) copy-start(f32[512]{0:T(512)} %get-tuple-element.601) | copy-start | bytes 6148
  5577.4 48.2 copy-start.36
  5577.4 48.2 copy-start.37
  5577.4 48.2 copy-start.38
  5577.4 48.8 copy-start.15
  5584.0 48.4 copy-start.8
  5625.6 6.9 copy-start.9
  5632.4 7.9 copy-start.12
  5632.4 7.9 copy-start.13
  5632.5 7.9 copy-start.22
  5632.5 7.9 copy-start.23
  (51 other events, 115.3 us)
Sparse Core Ops, SparseCore 0:
  11.5 89.5 all-gather.5
  104.6 115.7 all-gather.7
  223.8 254.3 all-gather.9
  481.4 181.1 all-gather.11
  1709.2 136.9 reduce-scatter.15
  1848.4 360.6 reduce-scatter.9
  2211.5 448.4 reduce-scatter.7
  2662.4 971.2 reduce-scatter.13
  3636.2 1935.9 reduce-scatter.11
where the time goes:
time: 5670 us; the launch traced here: 5650 us
  waiting for transfers between devices  3990 us (70%)
  matrix products  767 us (14%)
  local copies, waits for them, and re-layouts  291 us (5%)
  blocking collectives  215 us (4%)
  other arithmetic  193 us (3%)
  loops' own time  159 us (3%)
    reduce_scatter x1, waiting for transfers between devices, per_device(): lax.psum_scatter(g_gu, ('dp', 'seq'), scatter_dimension=0, tiled=True)  1940 us
    reduce_scatter x1, waiting for transfers between devices, per_device(): lax.psum_scatter(g_down, ('dp', 'seq'), scatter_dimension=0, tiled=True)  971 us
    dot_general x168, matrix products, contract(): lax.dot_general(left, right, (((left_dim,), (right_dim,)), ((), ())), pre...  580 us
    reduce_scatter x1, waiting for transfers between devices, per_device(): lax.psum_scatter(g_qkv, ('dp', 'seq'), scatter_dimension=0, tiled=True)  449 us
    reduce_scatter x1, waiting for transfers between devices, per_device(): lax.psum_scatter(g_out, ('dp', 'seq'), scatter_dimension=0, tiled=True)  361 us
    dot_general x68, matrix products, matmul(): return jnp.dot(left, right, preferred_element_type=jnp.float32)  187 us
  transfers between devices with their start and end apart: 14, of which 11 were waited for; matrix products, arithmetic and copies ran while one was open for 8% of the time, Pallas kernels for 0%

commit v1 on v0

v1 whole, which is shorter than its diff:
```python
import jax
import jax.numpy as jnp
from jax import lax
from jax.experimental import pallas as pl
from jax.experimental.pallas import tpu as pltpu
from jax.sharding import PartitionSpec as P

HEADS = 32
KV_HEADS = 4
HD = 64
FF = 5632
STEP = 10


NORM_EPS = 1e-05
ROPE_BASE = 10000.0
CLIP_NORM = 1.0
BETA_ONE = 0.9
BETA_TWO = 0.999
ADAM_EPS = 1e-08
WEIGHT_DECAY = 0.1
MASKED = -1e30


def matmul(left, right):
    return jnp.dot(left, right, preferred_element_type=jnp.float32)


def contract(left, right, left_dim, right_dim):
    return lax.dot_general(
        left, right, (((left_dim,), (right_dim,)), ((), ())), preferred_element_type=jnp.float32
    )


def rope_tables(positions):
    half_dim = HD // 2
    inverse = jnp.exp(-(2.0 * jnp.arange(half_dim, dtype=jnp.float32) / HD) * jnp.log(ROPE_BASE))
    angles = inverse[:, None] * positions.astype(jnp.float32)[None, :]
    return (jnp.cos(angles), jnp.sin(angles))


def rotate(rows, cos_table, sin_table):
    tokens = rows.shape[1]
    split = rows.reshape(-1, 2, HD // 2, tokens)
    first, second = (split[:, 0], split[:, 1])
    return jnp.stack(
        [first * cos_table - second * sin_table, second * cos_table + first * sin_table], 1
    ).reshape(rows.shape)


def norm_forward(rows_in, gain_row):
    inv_rms = lax.rsqrt(jnp.mean(rows_in * rows_in, axis=-1, keepdims=True) + NORM_EPS)
    return (inv_rms, rows_in * inv_rms * gain_row)


def norm_backward(rows_in, inv_rms, gain_row, gradient):
    weighted = gain_row * gradient
    back_rows = inv_rms * weighted - rows_in * inv_rms**3 * jnp.mean(
        weighted * rows_in, axis=-1, keepdims=True
    )
    return (back_rows, jnp.sum(gradient * rows_in * inv_rms, axis=0))


LOG2E = 1.4426950408889634
SCORE_SCALE = HD ** (-0.5)


def transposed(block):
    return block.astype(jnp.float32).T.astype(block.dtype)


def causal(tokens, valid):
    key_ids = lax.broadcasted_iota(jnp.int32, (tokens, tokens), 0)
    row_ids = lax.broadcasted_iota(jnp.int32, (tokens, tokens), 1)
    return (key_ids == row_ids) | ((key_ids < row_ids) & (valid > 0))


def forward_kernel(info, q_ref, k_ref, v_ref, o_ref, full_ref, lse_ref, k_rows):
    tokens = q_ref.shape[1]
    share = HEADS // KV_HEADS
    blocks, valid = (info[0], info[1])

    @pl.when(pl.program_id(0) % share == 0)
    def _():
        @pl.loop(0, blocks)
        def _(dist):
            k_rows[dist] = transposed(k_ref[dist])

    query = q_ref[...]

    def scores_of(dist):
        return matmul(k_rows[dist], query) * (SCORE_SCALE * LOG2E)

    scores = jnp.where(causal(tokens, valid), scores_of(0), MASKED)
    top = jnp.max(scores, 0, keepdims=True)
    weights = jnp.exp2(scores - top)
    total = jnp.sum(weights, 0, keepdims=True)
    acc = matmul(v_ref[0], weights.astype(jnp.bfloat16))

    def step(dist, carry):
        top, total, acc = carry
        scores = scores_of(dist)
        new_top = jnp.maximum(top, jnp.max(scores, 0, keepdims=True))
        weights = jnp.exp2(scores - new_top)
        fade = jnp.exp2(top - new_top)
        total = total * fade + jnp.sum(weights, 0, keepdims=True)
        acc = acc * fade + matmul(v_ref[dist], weights.astype(jnp.bfloat16))
        return (new_top, total, acc)

    top, total, acc = lax.fori_loop(1, blocks, step, (top, total, acc))
    out = acc / total
    o_ref[...] = out.astype(jnp.bfloat16)
    full_ref[...] = out
    lse_ref[0] = top + jnp.log2(total)


def backward_kernel(
    info, q_ref, k_ref, v_ref, full_ref, lse_ref, do_ref, dq_ref, dk_ref, dv_ref,
    k_rows, v_rows, dk_acc, dv_acc,
):
    tokens = q_ref.shape[1]
    share = HEADS // KV_HEADS
    blocks, valid = (info[0], info[1])

    @pl.when(pl.program_id(0) % share == 0)
    def _():
        dk_acc[...] = jnp.zeros_like(dk_acc)
        dv_acc[...] = jnp.zeros_like(dv_acc)

        @pl.loop(0, blocks)
        def _(dist):
            k_rows[dist] = transposed(k_ref[dist])
            v_rows[dist] = transposed(v_ref[dist])

    query, grad = (q_ref[...], do_ref[...])
    query_rows, grad_rows = (transposed(query), transposed(grad))
    lse = lse_ref[0]
    centre = jnp.sum(grad.astype(jnp.float32) * full_ref[...], 0, keepdims=True)

    def block(dist, mask):
        scores = matmul(k_rows[dist], query) * (SCORE_SCALE * LOG2E)
        prob = jnp.exp2(scores - lse)
        if mask is not None:
            prob = jnp.where(mask, prob, 0.0)
        d_prob = matmul(v_rows[dist], grad)
        d_score = (prob * (d_prob - centre) * SCORE_SCALE).astype(jnp.bfloat16)
        dv_acc[dist] += matmul(prob.astype(jnp.bfloat16), grad_rows)
        dk_acc[dist] += matmul(d_score, query_rows)
        return matmul(k_ref[dist], d_score)

    d_query = block(0, causal(tokens, valid))
    dq_ref[...] = lax.fori_loop(1, blocks, lambda dist, acc: acc + block(dist, None), d_query)

    @pl.when(pl.program_id(0) % share == share - 1)
    def _():
        @pl.loop(0, dk_acc.shape[0])
        def _(dist):
            dk_ref[dist] = dk_acc[dist].T
            dv_ref[dist] = dv_acc[dist].T


def head_block(tokens):
    return pl.BlockSpec((HD, tokens), lambda head, info: (head, 0))


def kv_block(reach, tokens):
    share = HEADS // KV_HEADS
    return pl.BlockSpec((reach, HD, tokens), lambda head, info: (0, head // share, 0))


def row_block(tokens):
    return pl.BlockSpec((1, 1, tokens), lambda head, info: (head, 0, 0))


def attend_forward(info, query, keys, values):
    tokens, reach = (query.shape[1], keys.shape[0])
    return pl.pallas_call(
        forward_kernel,
        grid_spec=pltpu.PrefetchScalarGridSpec(
            num_scalar_prefetch=1,
            grid=(HEADS,),
            in_specs=[head_block(tokens), kv_block(reach, tokens), kv_block(reach, tokens)],
            out_specs=[head_block(tokens), head_block(tokens), row_block(tokens)],
            scratch_shapes=[pltpu.VMEM((reach, tokens, HD), jnp.bfloat16)],
        ),
        out_shape=[
            jax.ShapeDtypeStruct(query.shape, jnp.bfloat16),
            jax.ShapeDtypeStruct(query.shape, jnp.float32),
            jax.ShapeDtypeStruct((HEADS, 1, tokens), jnp.float32),
        ],
        compiler_params=pltpu.CompilerParams(vmem_limit_bytes=40 * 2**20),
        cost_estimate=pl.CostEstimate(
            flops=HEADS * reach * tokens * tokens * 256 * 4,
            bytes_accessed=query.size * 8,
            transcendentals=HEADS * reach * tokens * tokens,
        ),
        name="attend_forward",
    )(info, query, keys, values)


def attend_backward(info, query, keys, values, full, lse, grad):
    tokens, reach = (query.shape[1], keys.shape[0])
    return pl.pallas_call(
        backward_kernel,
        grid_spec=pltpu.PrefetchScalarGridSpec(
            num_scalar_prefetch=1,
            grid=(HEADS,),
            in_specs=[
                head_block(tokens),
                kv_block(reach, tokens),
                kv_block(reach, tokens),
                head_block(tokens),
                row_block(tokens),
                head_block(tokens),
            ],
            out_specs=[head_block(tokens), kv_block(reach, tokens), kv_block(reach, tokens)],
            scratch_shapes=[
                pltpu.VMEM((reach, tokens, HD), jnp.bfloat16),
                pltpu.VMEM((reach, tokens, HD), jnp.bfloat16),
                pltpu.VMEM((reach, tokens, HD), jnp.float32),
                pltpu.VMEM((reach, tokens, HD), jnp.float32),
            ],
        ),
        out_shape=[
            jax.ShapeDtypeStruct(query.shape, jnp.float32),
            jax.ShapeDtypeStruct(keys.shape, jnp.float32),
            jax.ShapeDtypeStruct(keys.shape, jnp.float32),
        ],
        compiler_params=pltpu.CompilerParams(vmem_limit_bytes=40 * 2**20),
        cost_estimate=pl.CostEstimate(
            flops=HEADS * reach * tokens * tokens * 256 * 10,
            bytes_accessed=query.size * 14,
            transcendentals=HEADS * reach * tokens * tokens,
        ),
        name="attend_backward",
    )(info, query, keys, values, full, lse, grad)


def gather_earlier(block):
    size = lax.axis_size("seq")
    held = [block]
    for step in range(1, size):
        held.append(lax.ppermute(held[-1], "seq", [(i, i + 1) for i in range(step - 1, size - 1)]))
    return jnp.stack(held, 0)


def sum_to_owner(parts):
    size = lax.axis_size("seq")
    total = parts[size - 1]
    for step in range(size - 1, 0, -1):
        total = parts[step - 1] + lax.ppermute(
            total.astype(jnp.bfloat16), "seq", [(i, i - 1) for i in range(step, size)]
        ).astype(jnp.float32)
    return total


def adam_update(weight, first_mom, second_mom, gradient, clip_factor, rate, decay):
    step_grad = gradient * clip_factor
    first_new = BETA_ONE * first_mom + (1.0 - BETA_ONE) * step_grad
    second_new = BETA_TWO * second_mom + (1.0 - BETA_TWO) * step_grad * step_grad
    mean_hat = first_new / (1.0 - BETA_ONE**STEP)
    square_hat = second_new / (1.0 - BETA_TWO**STEP)
    weight_new = weight - rate * (mean_hat / (jnp.sqrt(square_hat) + ADAM_EPS) + decay * weight)
    return (weight_new, first_new, second_new)


def gathered(shard):
    return lax.all_gather(shard.astype(jnp.bfloat16), ("dp", "seq"), axis=0, tiled=True)


def scattered(partial):
    part = lax.psum_scatter(
        partial.astype(jnp.bfloat16), "dp", scatter_dimension=0, tiled=True
    )
    return lax.psum_scatter(part, "seq", scatter_dimension=0, tiled=True).astype(jnp.float32)


def per_device(
    hidden_in,
    out_grad,
    seq_lengths,
    seq_counts,
    segment_ids,
    qkv_weight,
    qkv_m,
    qkv_v,
    out_weight,
    out_m,
    out_v,
    gate_up_weight,
    gate_up_m,
    gate_up_v,
    down_weight,
    down_m,
    down_v,
    norm_gains,
    gain_m,
    gain_v,
):
    tok_dev = hidden_in.shape[0]
    q_width = HEADS * HD
    kv_width = KV_HEADS * HD
    seg_all = segment_ids[0]
    lengths = seq_lengths[0]
    seq_index = lax.axis_index("seq")
    offset = seq_index * tok_dev
    seg_local = lax.dynamic_slice_in_dim(seg_all, offset, tok_dev, 0)
    starts = jnp.cumsum(lengths, dtype=jnp.int32) - lengths
    slot_ids = jnp.arange(lengths.shape[0], dtype=jnp.int32)
    seq_start = jnp.sum(
        jnp.where(seg_local[:, None] == slot_ids[None, :], starts[None, :], 0),
        axis=1,
        dtype=jnp.int32,
    )
    positions = offset + jnp.arange(tok_dev, dtype=jnp.int32) - seq_start
    cos_table, sin_table = rope_tables(positions)
    valid = (seg_local[0] < seq_counts[0]).astype(jnp.int32)
    reach = jnp.where(valid > 0, seq_index - seq_start[0] // tok_dev + 1, 1)
    info = jnp.stack([reach, valid]).astype(jnp.int32)

    w_qkv = gathered(qkv_weight)
    w_gain = lax.all_gather(norm_gains.astype(jnp.bfloat16), ("dp", "seq"), axis=1, tiled=True)
    w_out = gathered(out_weight)
    w_down = gathered(down_weight)
    w_gu = gathered(gate_up_weight)
    gain_attn = w_gain[0].astype(jnp.float32)
    gain_mlp = w_gain[1].astype(jnp.float32)
    residual = hidden_in.astype(jnp.float32)
    inv_one, normed = norm_forward(residual, gain_attn)
    normed_low = normed.astype(jnp.bfloat16)
    qkv_out = contract(w_qkv, normed_low, 0, 1)
    query = rotate(qkv_out[:q_width], cos_table, sin_table).astype(jnp.bfloat16)
    key = rotate(qkv_out[q_width : q_width + kv_width], cos_table, sin_table).astype(jnp.bfloat16)
    value = qkv_out[q_width + kv_width :].astype(jnp.bfloat16)
    kv_all = gather_earlier(jnp.concatenate([key, value], 0))
    keys, values = (kv_all[:, :kv_width], kv_all[:, kv_width:])
    attended, attended_full, lse = attend_forward(info, query, keys, values)
    mid_rows = residual + contract(attended, w_out, 0, 0)
    inv_two, normed_two = norm_forward(mid_rows, gain_mlp)
    inner_rows = normed_two.astype(jnp.bfloat16)
    gate_up = matmul(inner_rows, w_gu)
    gate_vals, up_vals = (gate_up[:, :FF], gate_up[:, FF:])
    sigmoid_gate = jax.nn.sigmoid(gate_vals)
    hidden = (gate_vals * sigmoid_gate * up_vals).astype(jnp.bfloat16)
    block_out = (mid_rows + matmul(hidden, w_down)).astype(jnp.bfloat16)
    d_hidden = contract(out_grad, w_down, 1, 1)
    g_down = contract(hidden, out_grad, 0, 0)
    d_gate = d_hidden * up_vals * sigmoid_gate * (1.0 + gate_vals * (1.0 - sigmoid_gate))
    d_up = d_hidden * gate_vals * sigmoid_gate
    d_gu = jnp.concatenate([d_gate, d_up], -1).astype(jnp.bfloat16)
    d_inner = contract(d_gu, w_gu, 1, 1)
    g_gu = contract(inner_rows, d_gu, 0, 0)
    back_two, g_gain_two = norm_backward(mid_rows, inv_two, gain_mlp, d_inner)
    d_mid = out_grad.astype(jnp.float32) + back_two
    g_down_own = scattered(g_down)
    g_gu_own = scattered(g_gu)
    d_branch = d_mid.astype(jnp.bfloat16)
    g_out = matmul(attended, d_branch)
    g_out_own = scattered(g_out)
    d_attended = contract(w_out, d_branch, 1, 1).astype(jnp.bfloat16)
    d_query, d_keys, d_values = attend_backward(
        info, query, keys, values, attended_full, lse, d_attended
    )
    d_kv = sum_to_owner(jnp.concatenate([d_keys, d_values], 1))
    d_qkv = jnp.concatenate(
        [
            rotate(d_query, cos_table, -sin_table),
            rotate(d_kv[:kv_width], cos_table, -sin_table),
            d_kv[kv_width:],
        ],
        0,
    ).astype(jnp.bfloat16)
    d_normed = contract(d_qkv, w_qkv, 0, 1)
    g_qkv = contract(normed_low, d_qkv, 0, 1)
    back_one, g_gain_one = norm_backward(residual, inv_one, gain_attn, d_normed)
    input_grad = d_mid + back_one
    g_gains = jnp.stack([g_gain_one, g_gain_two], 0)
    g_qkv_own = scattered(g_qkv)
    g_gains_own = lax.psum_scatter(g_gains, ("dp", "seq"), scatter_dimension=1, tiled=True)
    local_sq = (
        jnp.sum(g_qkv_own * g_qkv_own)
        + jnp.sum(g_out_own * g_out_own)
        + jnp.sum(g_gu_own * g_gu_own)
        + jnp.sum(g_down_own * g_down_own)
        + jnp.sum(g_gains_own * g_gains_own)
    )
    total_sq = lax.psum(local_sq, ("dp", "seq"))
    grad_norm = jnp.sqrt(total_sq)
    clip_factor = jnp.minimum(1.0, CLIP_NORM / (grad_norm + 1e-06))
    new_qkv, new_qkv_m, new_qkv_v = adam_update(
        qkv_weight, qkv_m, qkv_v, g_qkv_own, clip_factor, 0.06, WEIGHT_DECAY
    )
    new_out, new_out_m, new_out_v = adam_update(
        out_weight, out_m, out_v, g_out_own, clip_factor, 0.4, WEIGHT_DECAY
    )
    new_gu, new_gu_m, new_gu_v = adam_update(
        gate_up_weight, gate_up_m, gate_up_v, g_gu_own, clip_factor, 0.06, WEIGHT_DECAY
    )
    new_down, new_down_m, new_down_v = adam_update(
        down_weight, down_m, down_v, g_down_own, clip_factor, 0.06, WEIGHT_DECAY
    )
    new_gains, new_gain_m, new_gain_v = adam_update(
        norm_gains, gain_m, gain_v, g_gains_own, clip_factor, 0.6, 0.0
    )
    return (
        block_out,
        input_grad,
        grad_norm,
        new_qkv,
        new_qkv_m,
        new_qkv_v,
        new_out,
        new_out_m,
        new_out_v,
        new_gu,
        new_gu_m,
        new_gu_v,
        new_down,
        new_down_m,
        new_down_v,
        new_gains,
        new_gain_m,
        new_gain_v,
    )


def solution(mesh):
    in_specs = (
        P(("dp", "seq"), None),
        P(("dp", "seq"), None),
        P("dp", None),
        P("dp"),
        P("dp", None),
        P(("dp", "seq"), None),
        P(("dp", "seq"), None),
        P(("dp", "seq"), None),
        P(("dp", "seq"), None),
        P(("dp", "seq"), None),
        P(("dp", "seq"), None),
        P(("dp", "seq"), None),
        P(("dp", "seq"), None),
        P(("dp", "seq"), None),
        P(("dp", "seq"), None),
        P(("dp", "seq"), None),
        P(("dp", "seq"), None),
        P(None, ("dp", "seq")),
        P(None, ("dp", "seq")),
        P(None, ("dp", "seq")),
    )
    out_specs = (
        P(("dp", "seq"), None),
        P(("dp", "seq"), None),
        P(),
        P(("dp", "seq"), None),
        P(("dp", "seq"), None),
        P(("dp", "seq"), None),
        P(("dp", "seq"), None),
        P(("dp", "seq"), None),
        P(("dp", "seq"), None),
        P(("dp", "seq"), None),
        P(("dp", "seq"), None),
        P(("dp", "seq"), None),
        P(("dp", "seq"), None),
        P(("dp", "seq"), None),
        P(("dp", "seq"), None),
        P(None, ("dp", "seq")),
        P(None, ("dp", "seq")),
        P(None, ("dp", "seq")),
    )
    return jax.shard_map(
        per_device, mesh=mesh, in_specs=in_specs, out_specs=out_specs, check_vma=False
    )
```

time: 5670 us -> 1790 us (0.32)
  waiting for transfers between devices: 3990 us -> 1290 us
  matrix products: 767 us -> 227 us
  local copies, waits for them, and re-layouts: 291 us -> 17.9 us
  loops' own time: 159 us -> 0 us
  other arithmetic: 193 us -> 48.4 us
  blocking collectives: 215 us -> 111 us
    reduce_scatter x4 -> x7, waiting for transfers between devices: 3720 us -> 374 us  [the longest x4 212 us: scattered(): lax.psum_scatter(part, 'seq', scatter_dimension=0, tiled=True)]
    dot_general x168 -> x9, matrix products: 580 us -> 167 us  [contract(): lax.dot_general(left, right, (((left_dim,), (right_dim,)), ((), ())), pre...]
    all_gather x4, waiting for transfers between devices: 14.4 us -> 399 us  [gathered(): lax.all_gather(shard.astype(jnp.bfloat16), ('dp', 'seq'), axis=0, tiled=T...]
    unnamed x10 -> x15, waiting for transfers between devices: 26.9 us -> 387 us
    all_to_all x5 -> x0, waiting for transfers between devices: 229 us -> none  [the longest x1 92.1 us: per_device(): lax.all_to_all(dq_send, 'seq', split_axis=0, concat_axis=1, tiled=True)]
    another operation x18 -> x0, loops' own time: 159 us -> none  [the longest x8 63.8 us: one_head(): head_outs, log_sums = lax.map(one_block, starts)]
    ppermute x0 -> x6, waiting for transfers between devices: none -> 127 us  [the longest x3 112 us: sum_to_owner(): lax.ppermute(total.astype(jnp.bfloat16), 'seq', [(i, i - 1) for i in rang...]
    dot_general x68 -> x3, matrix products: 187 us -> 59.9 us  [matmul(): return jnp.dot(left, right, preferred_element_type=jnp.float32)]
  transfers between devices with their start and end apart: 14 -> 19, of which waited for: 11 -> 14; matrix products, arithmetic and copies ran while one was open for 8% -> 10% of each run, Pallas kernels for 0% -> 3%
where the time goes in v1:
time: 1790 us; the launch traced here: 1780 us
  waiting for transfers between devices  1290 us (72%)
  matrix products  227 us (13%)
  blocking collectives  111 us (6%)
  Pallas kernels  55.8 us (3%)
  other arithmetic  48.4 us (3%)
  between operations  24.2 us (1%)
    all_gather x4, waiting for transfers between devices, gathered(): lax.all_gather(shard.astype(jnp.bfloat16), ('dp', 'seq'), axis=0, tiled=T...  399 us
    unnamed x15, waiting for transfers between devices  387 us
    reduce_scatter x4, waiting for transfers between devices, scattered(): lax.psum_scatter(part, 'seq', scatter_dimension=0, tiled=True)  212 us
    dot_general x9, matrix products, contract(): lax.dot_general(left, right, (((left_dim,), (right_dim,)), ((), ())), pre...  167 us
    reduce_scatter x3, waiting for transfers between devices, scattered(): lax.psum_scatter(partial.astype(jnp.bfloat16), 'dp', scatter_dimension=0,...  162 us
    ppermute x3, waiting for transfers between devices, sum_to_owner(): lax.ppermute(total.astype(jnp.bfloat16), 'seq', [(i, i - 1) for i in rang...  112 us
    all_gather x1, blocking collectives, per_device(): lax.all_gather(norm_gains.astype(jnp.bfloat16), ('dp', 'seq'), axis=1, ti...  70 us
    dot_general x3, matrix products, matmul(): return jnp.dot(left, right, preferred_element_type=jnp.float32)  59.9 us
  transfers between devices with their start and end apart: 19, of which 14 were waited for; matrix products, arithmetic and copies ran while one was open for 10% of the time, Pallas kernels for 3%

profile of v1, /device:TPU:0, one launch (start us, length us, event | category | flops | bytes accessed | tf_op | source)
XLA Modules:
  0.0 1780.9 jit_solution(4581637427573561547)
XLA Ops:
  7.3 1.9 convert_element_type.112
  9.3 1.8 convert_element_type.116
  11.2 3.2 convert_element_type.118
  15.7 70.0 %all-gather = bf16[32,64,2]{1,2,0:T(2,128)(2,1)S(1)} all-gather(bf16[1,64,2]{1,2,0:T(2,128)(2,1)S(1)} %convert_bitcast_fusion), channel_id=1, replica_groups=mesh['dp'=8,'seq'=4] {'dp','seq'}, dimensions={0}, use_global_device_ids=true | all-gather | bytes 8448 | tf_op jit(solution)/shard_map/all_gather | solution.py:322
  88.0 12.8 all-gather.6.cloned.1.call-done
  100.8 8.8 convolution_bitcast_fusion
  109.6 2.2 copy-done.11
  112.1 3.3 collective-permute-start
  115.4 15.2 collective-permute-done
  137.2 2.2 slice-done
  141.8 20.2 %attend_forward.1 = (bf16[2048,512]{1,0:T(8,128)(2,1)S(1)}, f32[2048,512]{1,0:T(8,128)S(1)}, f32[32,1,512]{2,1,0:T(1,128)S(1)}) custom-call(s32[2]{0:T(128)S(1)} %pad_add_fusion.info, bf16[2048,512]{1,0:T(8,128)(2,1)S(1)} %bitcast.72, bf16[4,256,512]{2,1,0:T(8,128)(2,1)S(1)} %get-tuple-element.57.k_ref, bf16[4,256,512]{2,1,0:T(8,128)(2,1)S(1)} %get-tuple-element.56.v_ref), custom_call_target="tpu_custom_call" | custom-call | flops 34359738368 | bytes 8388608 | tf_op jit(solution)/shard_map/attend_forward/pallas_call | solution.py:177
  164.0 2.1 copy-done.10
  166.0 18.2 %all-gather.8.cloned.1.call-done = bf16[2048,2048]{1,0:T(8,128)(2,1)} async-done(((bf16[64,2048]{1,0:T(8,128)(2,1)}), bf16[2048,2048]{1,0:T(8,128)(2,1)}) %all-gather.8.cloned.1.call-update) | async-done | bytes 8388624 | tf_op jit(solution)/shard_map/all_gather | solution.py:268
  184.3 10.0 multiply_reduce_fusion.2
  194.2 255.3 %all-gather.10.cloned.1.call-done = bf16[2048,11264]{1,0:T(8,128)(2,1)} async-done(((bf16[64,11264]{1,0:T(8,128)(2,1)}), bf16[2048,11264]{1,0:T(8,128)(2,1)}) %all-gather.10.cloned.1.call-update) | async-done | bytes 46137360 | tf_op jit(solution)/shard_map/all_gather | solution.py:268
  449.6 33.3 %fusion.46 = f32[512,11264]{1,0:T(8,128)} fusion(bf16[2048,11264]{1,0:T(8,128)(2,1)} %all-gather.10.cloned.1.call-done, f32[512,2048]{1,0:T(8,128)} %get-tuple-element.74, f32[2048]{0:T(1024)S(1)} %bitcast.92, f32[512]{0:T(512)S(1)} %get-tuple-element.72), kind=kOutput, calls=%fused_computation.129 | convolution fusion | flops 23625465856 | bytes 73410560 | tf_op jit(solution)/shard_map/dot_general | solution.py:26
  482.9 112.7 %all-gather.12.cloned.1.call-done = bf16[5632,2048]{1,0:T(8,128)(2,1)} async-done(((bf16[176,2048]{1,0:T(8,128)(2,1)}), bf16[5632,2048]{1,0:T(8,128)(2,1)}) %all-gather.12.cloned.1.call-update) | async-done | bytes 23068688 | tf_op jit(solution)/shard_map/all_gather | solution.py:268
  595.7 28.1 %multiply_convert_fusion.1 = (bf16[512,5632]{1,0:T(8,128)(2,1)}, bf16[512,5632]{1,0:T(8,128)(2,1)}, bf16[512,5632]{1,0:T(8,128)(2,1)}) fusion(f32[512,11264]{1,0:T(8,128)} %fusion.46, bf16[512,2048]{1,0:T(8,128)(2,1)} %param.21, bf16[5632,2048]{1,0:T(8,128)(2,1)} %all-gather.12.cloned.1.call-done), kind=kOutput, calls=%fused_computation.4 | convolution fusion | flops 11857297408 | bytes 65536000 | tf_op jit(solution)/shard_map/dot_general | solution.py:30
  623.8 35.3 %multiply_reduce_fusion = (f32[2048]{0:T(1024)}, f32[512]{0:T(512)S(1)}, f32[512,2048]{1,0:T(8,128)}) fusion(f32[512,2048]{1,0:T(8,128)} %get-tuple-element.74, f32[512]{0:T(512)S(1)} %get-tuple-element.72, f32[2048]{0:T(1024)S(1)} %bitcast.93, bf16[2048,11264]{1,0:T(8,128)(2,1)} %all-gather.10.cloned.1.call-done, bf16[512,5632]{1,0:T(8,128)(2,1)} %get-tuple-element.50, ...), kind=kOutput, calls=%fused_computation.27 | convolution fusion | flops 23651678208 | bytes 66080768 | tf_op jit(solution)/shard_map/dot_general | solution.py:30
  659.1 5.2 subtract_add_fusion
  664.3 2.0 copy-done.12
  666.3 6.7 convolution_convert_fusion.3
  673.6 10.2 fusion.14.do_ref
  683.9 35.6 %attend_backward.1 = (f32[2048,512]{1,0:T(8,128)}, f32[4,256,512]{2,1,0:T(8,128)S(1)}, f32[4,256,512]{2,1,0:T(8,128)S(1)}) custom-call(s32[2]{0:T(128)S(1)} %copy-done.9, bf16[2048,512]{1,0:T(8,128)(2,1)S(1)} %bitcast.73, bf16[4,256,512]{2,1,0:T(8,128)(2,1)S(1)} %copy-done.7, bf16[4,256,512]{2,1,0:T(8,128)(2,1)S(1)} %copy-done.5, f32[2048,512]{1,0:T(8,128)} %copy-done.10, ...), custom_call_target="tpu_custom_call" | custom-call | flops 85899345920 | bytes 14680064 | tf_op jit(solution)/shard_map/attend_backward/pallas_call | solution.py:203
  724.4 112.3 %collective-permute-done.5 = bf16[512,512]{1,0:T(8,128)(2,1)S(1)} collective-permute-done((bf16[512,512]{1,0:T(8,128)(2,1)S(1)}, bf16[512,512]{1,0:T(8,128)(2,1)S(1)}, u32[]{:S(2)}, u32[]{:S(2)}) %collective-permute-start.5) | collective-permute-done | bytes 524320 | tf_op jit(solution)/shard_map/ppermute | solution.py:251
  837.1 9.8 convolution_convert_fusion.2
  847.0 19.7 %convolution_convert_fusion.1 = bf16[5632,2048]{1,0:T(8,128)(2,1)} fusion(bf16[512,5632]{1,0:T(8,128)(2,1)} %get-tuple-element.51, bf16[512,2048]{1,0:T(8,128)(2,1)} %param.21), kind=kOutput, calls=%fused_computation.1 | convolution fusion | flops 11822694400 | bytes 30932992 | tf_op jit(solution)/shard_map/dot_general | solution.py:30
  867.4 32.8 %convolution_convert_fusion = bf16[2048,11264]{1,0:T(8,128)(2,1)} fusion(bf16[512,5632]{1,0:T(8,128)(2,1)} %get-tuple-element.50, bf16[512,5632]{1,0:T(8,128)(2,1)} %get-tuple-element.49, f32[512,2048]{1,0:T(8,128)} %get-tuple-element.74, f32[2048]{0:T(1024)S(1)} %bitcast.95, f32[512]{0:T(512)S(1)} %copy-done.39), kind=kOutput, calls=%fused_computation | convolution fusion | flops 23671603200 | bytes 61876224 | tf_op jit(solution)/shard_map/dot_general | solution.py:30
  900.3 12.3 fusion.9
  914.6 12.4 reduce-scatter.14.cloned.1.call-done
  927.1 149.9 %reduce-scatter.24.cloned.1.call-done = bf16[704,2048]{1,0:T(8,128)(2,1)} async-done(((bf16[5632,2048]{1,0:T(8,128)(2,1)}), bf16[704,2048]{1,0:T(8,128)(2,1)}) %reduce-scatter.24.cloned.1.call-update) | async-done | bytes 2883600 | tf_op jit(solution)/shard_map/reduce_scatter | solution.py:272
  1077.3 268.1 %reduce-scatter.30.cloned.1.call-done = bf16[256,11264]{1,0:T(8,128)(2,1)} async-done(((bf16[2048,11264]{1,0:T(8,128)(2,1)}), bf16[256,11264]{1,0:T(8,128)(2,1)}) %reduce-scatter.30.cloned.1.call-update) | async-done | bytes 5767184
  1345.4 19.8 %add_convert_fusion = bf16[512,2048]{1,0:T(8,128)(2,1)} fusion(f32[512,2048]{1,0:T(8,128)} %get-tuple-element.74, bf16[512,5632]{1,0:T(8,128)(2,1)} %get-tuple-element.51, bf16[5632,2048]{1,0:T(8,128)(2,1)} %all-gather.12.cloned.1.call-done), kind=kOutput, calls=%fused_computation.30 | convolution fusion | flops 11813257216 | bytes 35127296 | tf_op jit(solution)/shard_map/dot_general | solution.py:26
  1365.3 118.2 %reduce-scatter.28.cloned.1.call-done = f32[64,2]{1,0:T(8,128)} async-done(((f32[2048,2]{1,0:T(8,128)}), f32[64,2]{1,0:T(8,128)}) %reduce-scatter.28.cloned.1.call-update) | async-done | bytes 528
  1485.0 24.7 %reduce-scatter.20.cloned.1.call-done = bf16[64,2048]{1,0:T(8,128)(2,1)} async-done(((bf16[256,2048]{1,0:T(8,128)(2,1)}), bf16[64,2048]{1,0:T(8,128)(2,1)}) %reduce-scatter.20.cloned.1.call-update) | async-done | bytes 262160 | tf_op jit(solution)/shard_map/reduce_scatter | solution.py:275
  1509.7 1.7 fusion.35
  1511.4 30.6 %reduce-scatter.16.cloned.1.call-done = bf16[64,2560]{1,0:T(8,128)(2,1)} async-done(((bf16[256,2560]{1,0:T(8,128)(2,1)}), bf16[64,2560]{1,0:T(8,128)(2,1)}) %reduce-scatter.16.cloned.1.call-update) | async-done | bytes 327696 | tf_op jit(solution)/shard_map/reduce_scatter | solution.py:275
  1541.9 1.7 fusion.29
  1545.0 54.1 %reduce-scatter.26.cloned.1.call-done = bf16[176,2048]{1,0:T(8,128)(2,1)} async-done(((bf16[704,2048]{1,0:T(8,128)(2,1)}), bf16[176,2048]{1,0:T(8,128)(2,1)}) %reduce-scatter.26.cloned.1.call-update) | async-done | bytes 720912 | tf_op jit(solution)/shard_map/reduce_scatter | solution.py:275
  1599.1 2.1 fusion.17
  1601.2 102.4 %reduce-scatter.22.cloned.1.call-done = bf16[64,11264]{1,0:T(8,128)(2,1)} async-done(((bf16[256,11264]{1,0:T(8,128)(2,1)}), bf16[64,11264]{1,0:T(8,128)(2,1)}) %reduce-scatter.22.cloned.1.call-update) | async-done | bytes 1441808 | tf_op jit(solution)/shard_map/reduce_scatter | solution.py:275
  1703.5 2.7 fusion.12
  1708.3 6.7 fusion.6
  1714.9 40.7 %psum.7 = f32[]{:T(128)} all-reduce(f32[]{:T(128)S(6)} %add.214), channel_id=1, replica_groups=mesh['dp'=8,'seq'=4] {'dp','seq'}, use_global_device_ids=true, to_apply=%region_22.23 | all-reduce | flops 1 | bytes 8 | tf_op jit(solution)/shard_map/psum | solution.py:387
  1757.0 2.9 multiply_subtract_fusion.3
  1759.9 3.1 multiply_subtract_fusion.2
  1763.1 2.8 multiply_subtract_fusion.1
  1767.8 4.9 multiply_subtract_fusion
  (172 shorter events, 23.7 us)
Async XLA Ops:
  7.2 78.6 %copy-start = (s32[1,2048]{1,0:T(1,128)S(1)}, s32[1,2048]{1,0:T(1,128)}, u32[]{:S(2)}) copy-start(s32[1,2048]{1,0:T(1,128)} %param.24) | copy-start | bytes 24580
  7.2 7.2 copy-start.16
  7.2 93.6 %all-gather.6.cloned.1.call-start = ((), (), s32[]{:S(2)}) async-start(), calls=%async_computation.9 | async-start | bytes 10813440 | tf_op jit(solution)/shard_map/all_gather | solution.py:268
  9.2 175.0 %all-gather.8.cloned.1.call-start = ((), (), s32[]{:S(2)}) async-start(), calls=%async_computation.10 | async-start | bytes 8650752 | tf_op jit(solution)/shard_map/all_gather | solution.py:268
  11.1 74.8 %copy-start.14 = (bf16[512,2048]{1,0:T(8,128)(2,1)S(1)}, bf16[512,2048]{1,0:T(8,128)(2,1)}, u32[]{:S(2)}) copy-start(bf16[512,2048]{1,0:T(8,128)(2,1)} %param.20) | copy-start | bytes 6291460
  11.1 438.5 %all-gather.10.cloned.1.call-start = ((), (), s32[]{:S(2)}) async-start(), calls=%async_computation.11 | async-start | bytes 47579136 | tf_op jit(solution)/shard_map/all_gather | solution.py:268
  14.4 581.3 %all-gather.12.cloned.1.call-start = ((), (), s32[]{:S(2)}) async-start(), calls=%async_computation.12 | async-start | bytes 23789568 | tf_op jit(solution)/shard_map/all_gather | solution.py:268
  15.4 898.6 %reduce-scatter.18.cloned.1.call-start = ((), (), s32[]{:S(2)}) async-start(), calls=%async_computation.15 | async-start | bytes 9437184 | tf_op jit(solution)/shard_map/reduce_scatter | solution.py:272
  87.0 22.5 %copy-start.36 = (f32[512]{0:T(512)}, f32[512]{0:T(512)S(1)}, u32[]{:S(2)}) copy-start(f32[512]{0:T(512)S(1)} %get-tuple-element.70) | copy-start | bytes 6148
  87.9 49.3 %copy-start.26 = (f32[32,512]{1,0:T(8,128)}, f32[32,512]{1,0:T(8,128)S(1)}, u32[]{:S(2)}) copy-start(f32[32,512]{1,0:T(8,128)S(1)} %get-tuple-element.68) | copy-start | bytes 196612
  88.0 21.6 %copy-start.31 = (f32[1,2048]{1,0:T(1,128)}, f32[1,2048]{1,0:T(1,128)S(1)}, u32[]{:S(2)}) copy-start(f32[1,2048]{1,0:T(1,128)S(1)} %get-tuple-element.65) | copy-start | bytes 24580
  88.0 571.1 %copy-start.33 = (f32[1,2048]{1,0:T(1,128)}, f32[1,2048]{1,0:T(1,128)S(1)}, u32[]{:S(2)}) copy-start(f32[1,2048]{1,0:T(1,128)S(1)} %get-tuple-element.64) | copy-start | bytes 24580
  112.1 18.5 %collective-permute-start = (bf16[512,512]{1,0:T(8,128)(2,1)S(1)}, bf16[512,512]{1,0:T(8,128)(2,1)S(1)}, u32[]{:S(2)}, u32[]{:S(2)}) collective-permute-start(bf16[512,512]{1,0:T(8,128)(2,1)S(1)} %get-tuple-element.63), channel_id=1, source_target_pairs={{0,1},{1,2},{2,3},{4,5},{5,6},{6,7},{8,9},{9,10},{10,11},{12,13},{... | collective-permute-start | bytes 1572872 | tf_op jit(solution)/shard_map/ppermute | solution.py:243
  130.5 5.7 collective-permute-start.1
  136.2 4.2 collective-permute-start.2
  194.2 464.8 %copy-start.38 = (f32[512]{0:T(512)}, f32[512]{0:T(512)S(1)}, u32[]{:S(2)}) copy-start(f32[512]{0:T(512)S(1)} %get-tuple-element.72) | copy-start | bytes 6148
  673.1 10.8 copy-start.3
  673.1 10.8 copy-start.5
  673.1 10.8 copy-start.9
  673.1 253.9 %reduce-scatter.14.cloned.1.call-start = ((), (), s32[]{:S(2)}) async-start(), calls=%async_computation.13 | async-start | bytes 11796480 | tf_op jit(solution)/shard_map/reduce_scatter | solution.py:272
  673.6 10.3 copy-start.7
  720.0 0.8 collective-permute-start.3
  721.0 0.7 collective-permute-start.4
  721.9 114.8 %collective-permute-start.5 = (bf16[512,512]{1,0:T(8,128)(2,1)S(1)}, bf16[512,512]{1,0:T(8,128)(2,1)S(1)}, u32[]{:S(2)}, u32[]{:S(2)}) collective-permute-start(bf16[512,512]{1,0:T(8,128)(2,1)S(1)} %fusion.23), channel_id=1, source_target_pairs={{1,0},{2,1},{3,2},{5,4},{6,5},{7,6},{9,8},{10,9},{11,10},{13,12},{... | collective-permute-start | bytes 1572872 | tf_op jit(solution)/shard_map/ppermute | solution.py:251
  724.1 112.9 %copy-start.15 = (bf16[512,2048]{1,0:T(8,128)(2,1)S(1)}, bf16[512,2048]{1,0:T(8,128)(2,1)}, u32[]{:S(2)}) copy-start(bf16[512,2048]{1,0:T(8,128)(2,1)} %param.20) | copy-start | bytes 6291460
  724.1 112.9 %copy-start.32 = (f32[1,2048]{1,0:T(1,128)S(1)}, f32[1,2048]{1,0:T(1,128)}, u32[]{:S(2)}) copy-start(f32[1,2048]{1,0:T(1,128)} %copy-done.31) | copy-start | bytes 24580
  724.2 112.9 %copy-start.37 = (f32[512]{0:T(512)S(1)}, f32[512]{0:T(512)}, u32[]{:S(2)}) copy-start(f32[512]{0:T(512)} %copy-done.36) | copy-start | bytes 6148
  724.4 112.7 %copy-start.24 = (bf16[32,2,32,512]{3,2,1,0:T(8,128)(2,1)}, bf16[32,2,32,512]{3,2,1,0:T(8,128)(2,1)S(1)}, u32[]{:S(2)}) copy-start(bf16[32,2,32,512]{3,2,1,0:T(8,128)(2,1)S(1)} %pad_maximum_fusion.6) | copy-start | bytes 6291460
  846.9 230.1 %reduce-scatter.24.cloned.1.call-start = ((), (), s32[]{:S(2)}) async-start(), calls=%async_computation.18 | async-start | bytes 25952256 | tf_op jit(solution)/shard_map/reduce_scatter | solution.py:272
  866.7 478.7 %reduce-scatter.30.cloned.1.call-start = ((), (), s32[]{:S(2)}) async-start(), calls=%async_computation.21 | async-start | bytes 51904512
  900.2 12.4 copy-start.40
  900.2 583.3 %reduce-scatter.28.cloned.1.call-start = ((), (), s32[]{:S(2)}) async-start(), calls=%async_computation.20 | async-start | bytes 1081344
  914.0 595.7 %reduce-scatter.20.cloned.1.call-start = ((), (), s32[]{:S(2)}) async-start(), calls=%async_computation.16 | async-start | bytes 1310720 | tf_op jit(solution)/shard_map/reduce_scatter | solution.py:275
  914.6 627.3 %reduce-scatter.16.cloned.1.call-start = ((), (), s32[]{:S(2)}) async-start(), calls=%async_computation.14 | async-start | bytes 1638400 | tf_op jit(solution)/shard_map/reduce_scatter | solution.py:275
  927.0 672.1 %reduce-scatter.26.cloned.1.call-start = ((), (), s32[]{:S(2)}) async-start(), calls=%async_computation.19 | async-start | bytes 3604480 | tf_op jit(solution)/shard_map/reduce_scatter | solution.py:275
  1077.0 626.5 %reduce-scatter.22.cloned.1.call-start = ((), (), s32[]{:S(2)}) async-start(), calls=%async_computation.17 | async-start | bytes 7208960 | tf_op jit(solution)/shard_map/reduce_scatter | solution.py:275
  1345.4 362.8 %copy-start.35 = (f32[512]{0:T(512)S(1)}, f32[512]{0:T(512)}, u32[]{:S(2)}) copy-start(f32[512]{0:T(512)} %get-tuple-element.69) | copy-start | bytes 6148
  1708.2 48.1 %copy-start.42 = (f32[2,64]{1,0:T(2,128)S(1)}, f32[2,64]{1,0:T(2,128)}, u32[]{:S(2)}) copy-start(f32[2,64]{1,0:T(2,128)} %param.37) | copy-start | bytes 1540
  1708.2 48.1 %copy-start.43 = (f32[2,64]{1,0:T(2,128)S(1)}, f32[2,64]{1,0:T(2,128)}, u32[]{:S(2)}) copy-start(f32[2,64]{1,0:T(2,128)} %param.38) | copy-start | bytes 1540
  1708.2 48.1 %copy-start.44 = (f32[2,64]{1,0:T(2,128)S(1)}, f32[2,64]{1,0:T(2,128)}, u32[]{:S(2)}) copy-start(f32[2,64]{1,0:T(2,128)} %param.39) | copy-start | bytes 1540
  1708.2 48.7 %copy-start.25 = (f32[64,2048]{1,0:T(8,128)S(1)}, f32[64,2048]{1,0:T(8,128)}, u32[]{:S(2)}) copy-start(f32[64,2048]{1,0:T(8,128)} %param.28) | copy-start | bytes 1572868
  1708.3 51.7 %copy-start.23 = (f32[64,2560]{1,0:T(8,128)S(1)}, f32[64,2560]{1,0:T(8,128)}, u32[]{:S(2)}) copy-start(f32[64,2560]{1,0:T(8,128)} %param.25) | copy-start | bytes 1966084
  1714.9 48.2 %copy-start.17 = (f32[176,2048]{1,0:T(8,128)S(1)}, f32[176,2048]{1,0:T(8,128)}, u32[]{:S(2)}) copy-start(f32[176,2048]{1,0:T(8,128)} %param.34) | copy-start | bytes 4325380
  1714.9 48.2 %copy-start.20 = (bf16[176,2048]{1,0:T(8,128)(2,1)S(1)}, bf16[176,2048]{1,0:T(8,128)(2,1)}, u32[]{:S(2)}) copy-start(bf16[176,2048]{1,0:T(8,128)(2,1)} %reduce-scatter.26.cloned.1.call-done) | copy-start | bytes 2162692
  1756.4 6.7 copy-start.28
  1756.4 6.7 copy-start.29
  1759.9 6.0 copy-start.22
  1767.8 5.0 copy-start.1
  (18 other events, 48.3 us)
Sparse Core Ops, SparseCore 0:
  11.5 89.2 all-gather.5
  104.3 79.9 all-gather.7
  187.7 261.8 all-gather.9
  452.8 142.7 all-gather.11
  673.2 69.4 reduce-scatter.17
  847.0 79.9 reduce-scatter.13
  931.1 145.9 reduce-scatter.23
  1081.1 264.2 reduce-scatter.29
  1348.2 135.2 reduce-scatter.27
  1485.8 23.8 reduce-scatter.19
  1512.0 29.8 reduce-scatter.15
  1544.1 54.9 reduce-scatter.25
  1601.4 102.1 reduce-scatter.21

commit v2 on v1

v2 whole, which is shorter than its diff:
```python
import functools

import jax
import jax.numpy as jnp
from jax import lax
from jax.experimental import pallas as pl
from jax.experimental.pallas import tpu as pltpu
from jax.sharding import PartitionSpec as P

HEADS = 32
KV_HEADS = 4
HD = 64
FF = 5632
STEP = 10


NORM_EPS = 1e-05
ROPE_BASE = 10000.0
CLIP_NORM = 1.0
BETA_ONE = 0.9
BETA_TWO = 0.999
ADAM_EPS = 1e-08
WEIGHT_DECAY = 0.1
MASKED = -1e30


def matmul(left, right):
    return jnp.dot(left, right, preferred_element_type=jnp.float32)


def contract(left, right, left_dim, right_dim):
    return lax.dot_general(
        left, right, (((left_dim,), (right_dim,)), ((), ())), preferred_element_type=jnp.float32
    )


def rope_tables(positions):
    half_dim = HD // 2
    inverse = jnp.exp(-(2.0 * jnp.arange(half_dim, dtype=jnp.float32) / HD) * jnp.log(ROPE_BASE))
    angles = inverse[:, None] * positions.astype(jnp.float32)[None, :]
    return (jnp.cos(angles), jnp.sin(angles))


def rotate(rows, cos_table, sin_table):
    tokens = rows.shape[1]
    split = rows.reshape(-1, 2, HD // 2, tokens)
    first, second = (split[:, 0], split[:, 1])
    return jnp.stack(
        [first * cos_table - second * sin_table, second * cos_table + first * sin_table], 1
    ).reshape(rows.shape)


def norm_forward(rows_in, gain_row):
    inv_rms = lax.rsqrt(jnp.mean(rows_in * rows_in, axis=-1, keepdims=True) + NORM_EPS)
    return (inv_rms, rows_in * inv_rms * gain_row)


def norm_backward(rows_in, inv_rms, gain_row, gradient):
    weighted = gain_row * gradient
    back_rows = inv_rms * weighted - rows_in * inv_rms**3 * jnp.mean(
        weighted * rows_in, axis=-1, keepdims=True
    )
    return (back_rows, jnp.sum(gradient * rows_in * inv_rms, axis=0))


LOG2E = 1.4426950408889634
SCORE_SCALE = HD ** (-0.5)
SHARE = HEADS // KV_HEADS


def transposed(block):
    return block.astype(jnp.float32).T.astype(block.dtype)


def causal(tokens, valid):
    key_ids = lax.broadcasted_iota(jnp.int32, (tokens, tokens), 0)
    row_ids = lax.broadcasted_iota(jnp.int32, (tokens, tokens), 1)
    return (key_ids == row_ids) | ((key_ids < row_ids) & (valid > 0))


def attend_head(head, blocks, reach, valid, q_ref, kv_ref, group, k_rows, o_ref, full_ref, lse_ref):
    tokens = q_ref.shape[1]
    rows = pl.ds(pl.multiple_of(head * HD, HD), HD)
    query = q_ref[rows, :]

    def scores_of(dist):
        return matmul(k_rows[dist], query) * (SCORE_SCALE * LOG2E)

    def values_of(dist):
        return kv_ref[dist, group, HD:, :]

    scores = jnp.where(causal(tokens, valid), scores_of(0), MASKED)
    top = jnp.max(scores, 0, keepdims=True)
    weights = jnp.exp2(scores - top)
    total = jnp.sum(weights, 0, keepdims=True)
    acc = matmul(values_of(0), weights.astype(jnp.bfloat16))

    def step(dist, carry):
        top, total, acc = carry
        scores = jnp.where(dist < reach, scores_of(dist), MASKED)
        new_top = jnp.maximum(top, jnp.max(scores, 0, keepdims=True))
        weights = jnp.exp2(scores - new_top)
        fade = jnp.exp2(top - new_top)
        total = total * fade + jnp.sum(weights, 0, keepdims=True)
        acc = acc * fade + matmul(values_of(dist), weights.astype(jnp.bfloat16))
        return (new_top, total, acc)

    top, total, acc = lax.fori_loop(1, blocks, step, (top, total, acc))
    out = acc / total
    o_ref[rows, :] = out.astype(jnp.bfloat16)
    full_ref[rows, :] = out
    lse_ref[head] = top + jnp.log2(total)


def backward_kernel(
    info, q_ref, kv_ref, full_ref, lse_ref, do_ref, dq_ref, dkv_ref, k_rows, v_rows, dk_acc, dv_acc
):
    tokens = q_ref.shape[1]
    blocks, valid = (info[0], info[1])

    @pl.when(pl.program_id(0) % SHARE == 0)
    def _():
        dk_acc[...] = jnp.zeros_like(dk_acc)
        dv_acc[...] = jnp.zeros_like(dv_acc)

        @pl.loop(0, blocks)
        def _(dist):
            k_rows[dist] = transposed(kv_ref[dist, 0, :HD, :])
            v_rows[dist] = transposed(kv_ref[dist, 0, HD:, :])

    query, grad = (q_ref[...], do_ref[...])
    query_rows, grad_rows = (transposed(query), transposed(grad))
    lse = lse_ref[0]
    centre = jnp.sum(grad.astype(jnp.float32) * full_ref[...], 0, keepdims=True)

    def block(dist, mask):
        scores = matmul(k_rows[dist], query) * (SCORE_SCALE * LOG2E)
        prob = jnp.exp2(scores - lse)
        if mask is not None:
            prob = jnp.where(mask, prob, 0.0)
        d_prob = matmul(v_rows[dist], grad)
        d_score = (prob * (d_prob - centre) * SCORE_SCALE).astype(jnp.bfloat16)
        dv_acc[dist] += matmul(prob.astype(jnp.bfloat16), grad_rows)
        dk_acc[dist] += matmul(d_score, query_rows)
        return matmul(kv_ref[dist, 0, :HD, :], d_score)

    d_query = block(0, causal(tokens, valid))
    dq_ref[...] = lax.fori_loop(1, blocks, lambda dist, acc: acc + block(dist, None), d_query)

    @pl.when(pl.program_id(0) % SHARE == SHARE - 1)
    def _():
        @pl.loop(0, dk_acc.shape[0])
        def _(dist):
            dkv_ref[dist, 0, :HD, :] = dk_acc[dist].T
            dkv_ref[dist, 0, HD:, :] = dv_acc[dist].T


def attend_backward(info, query, kv, full, lse, grad, first, heads):
    tokens, reach = (query.shape[1], kv.shape[0])

    def head_block():
        return pl.BlockSpec((HD, tokens), lambda head, info: (head + first, 0))

    def row_block():
        return pl.BlockSpec((1, 1, tokens), lambda head, info: (head + first, 0, 0))

    return pl.pallas_call(
        backward_kernel,
        grid_spec=pltpu.PrefetchScalarGridSpec(
            num_scalar_prefetch=1,
            grid=(heads,),
            in_specs=[
                head_block(),
                pl.BlockSpec(
                    (reach, 1, 2 * HD, tokens),
                    lambda head, info: (0, (head + first) // SHARE, 0, 0),
                ),
                head_block(),
                row_block(),
                head_block(),
            ],
            out_specs=[
                pl.BlockSpec((HD, tokens), lambda head, info: (head, 0)),
                pl.BlockSpec(
                    (reach, 1, 2 * HD, tokens), lambda head, info: (0, head // SHARE, 0, 0)
                ),
            ],
            scratch_shapes=[
                pltpu.VMEM((reach, tokens, HD), jnp.bfloat16),
                pltpu.VMEM((reach, tokens, HD), jnp.bfloat16),
                pltpu.VMEM((reach, tokens, HD), jnp.float32),
                pltpu.VMEM((reach, tokens, HD), jnp.float32),
            ],
        ),
        out_shape=[
            jax.ShapeDtypeStruct((heads * HD, tokens), jnp.float32),
            jax.ShapeDtypeStruct((reach, heads // SHARE, 2 * HD, tokens), jnp.float32),
        ],
        compiler_params=pltpu.CompilerParams(vmem_limit_bytes=40 * 2**20),
        cost_estimate=pl.CostEstimate(
            flops=heads * reach * tokens * tokens * 256 * 10,
            bytes_accessed=query.size * 14,
            transcendentals=heads * reach * tokens * tokens,
        ),
        name="attend_backward",
    )(info, query, kv, full, lse, grad)


def sum_to_owner(parts):
    size = lax.axis_size("seq")
    total = parts[size - 1]
    for step in range(size - 1, 0, -1):
        total = parts[step - 1] + lax.ppermute(
            total.astype(jnp.bfloat16), "seq", [(i, i - 1) for i in range(step, size)]
        ).astype(jnp.float32)
    return total


def adam_update(weight, first_mom, second_mom, gradient, clip_factor, rate, decay):
    step_grad = gradient * clip_factor
    first_new = BETA_ONE * first_mom + (1.0 - BETA_ONE) * step_grad
    second_new = BETA_TWO * second_mom + (1.0 - BETA_TWO) * step_grad * step_grad
    mean_hat = first_new / (1.0 - BETA_ONE**STEP)
    square_hat = second_new / (1.0 - BETA_TWO**STEP)
    weight_new = weight - rate * (mean_hat / (jnp.sqrt(square_hat) + ADAM_EPS) + decay * weight)
    return (weight_new, first_new, second_new)


MESH = pl.DeviceIdType.MESH


def flipped(index, bit):
    return index + (1 << bit) * (1 - 2 * ((index // (1 << bit)) % 2))


WHOLE, ROWS, BLOCKS = range(3)


class Gather:
    ahead = 3

    def __init__(self, kinds, pieces, shards, fulls, local_sems, send_sems, recv_sems):
        self.kinds, self.pieces, self.shards, self.fulls = (kinds, pieces, shards, fulls)
        self.local_sems, self.send_sems, self.recv_sems = (local_sems, send_sems, recv_sems)
        self.dp, self.seq = (lax.axis_index("dp"), lax.axis_index("seq"))
        self.dp_size, self.seq_size = (lax.axis_size("dp"), lax.axis_size("seq"))
        self.bits = self.dp_size.bit_length() - 1
        up = list(range(1, self.bits))
        self.orders = (up + [0], up[::-1] + [0])
        self.started = []
        self.local = {}
        self.done = set()

    def along(self, step):
        return {"seq": lax.rem(self.seq + step, self.seq_size)}

    def across(self, bit):
        return {"dp": flipped(self.dp, bit)}

    def barrier(self):
        barrier = pltpu.get_barrier_semaphore()
        others = [self.along(step) for step in range(1, self.seq_size)]
        others += [self.across(bit) for bit in range(self.bits)]
        for other in others:
            pl.semaphore_signal(barrier, inc=1, device_id=other, device_id_type=MESH)
        pl.semaphore_wait(barrier, len(others))

    def columns(self, piece, side):
        _, low, middle, high = self.pieces[piece]
        return (pl.ds(low, middle - low), pl.ds(middle, high - middle))[side]

    def sides(self, piece):
        return (0, 1) if self.pieces[piece][3] > self.pieces[piece][2] else (0,)

    def own_rows(self, weight):
        depth = self.shards[weight].shape[0]
        index = {
            WHOLE: self.dp * self.seq_size + self.seq, ROWS: self.seq, BLOCKS: self.dp
        }[self.kinds[weight]]
        return pl.ds(pl.multiple_of(index * depth, depth), depth)

    def seq_copy(self, piece, side, step):
        weight = self.pieces[piece][0]
        cols = self.columns(piece, side)
        return pltpu.make_async_remote_copy(
            src_ref=self.shards[weight].at[:, cols],
            dst_ref=self.fulls[weight].at[self.own_rows(weight), cols],
            send_sem=self.send_sems.at[piece, side, self.dp_size + step],
            recv_sem=self.recv_sems.at[piece, side, self.dp_size + step],
            device_id=self.along(step),
            device_id_type=MESH,
        )

    def block_copy(self, piece, side, held, bit):
        weight = self.pieces[piece][0]
        depth = self.fulls[weight].shape[0] // self.dp_size
        owner = self.dp
        for position in range(self.bits):
            if held >> position & 1:
                owner = flipped(owner, position)
        window = (pl.ds(pl.multiple_of(owner * depth, depth), depth), self.columns(piece, side))
        source = self.fulls[weight].at[window]
        if not held and self.kinds[weight] == BLOCKS:
            source = self.shards[weight].at[:, self.columns(piece, side)]
        return pltpu.make_async_remote_copy(
            src_ref=source,
            dst_ref=self.fulls[weight].at[window],
            send_sem=self.send_sems.at[piece, side, held | 1 << bit],
            recv_sem=self.recv_sems.at[piece, side, held | 1 << bit],
            device_id=self.across(bit),
            device_id_type=MESH,
        )

    def start(self, copy):
        copy.start()
        self.started.append(copy)

    def begin(self):
        for weight, shard in enumerate(self.shards):
            self.local[weight] = pltpu.make_async_copy(
                shard, self.fulls[weight].at[self.own_rows(weight)], self.local_sems.at[weight]
            )
            self.local[weight].start()
        for piece in range(min(self.ahead, len(self.pieces))):
            self.send_rows(piece)

    def send_rows(self, piece):
        if self.kinds[self.pieces[piece][0]] == BLOCKS:
            return
        for step in range(1, self.seq_size):
            for side in self.sides(piece):
                self.start(self.seq_copy(piece, side, step))

    def advance(self, piece, stage):
        if (piece, stage) in self.done:
            return
        self.done.add((piece, stage))
        weight = self.pieces[piece][0]
        kind = self.kinds[weight]
        if stage and kind == ROWS:
            return
        if stage == 0 and kind == WHOLE and weight in self.local:
            self.local.pop(weight).wait()
        for side in self.sides(piece):
            order = self.orders[side] if kind != ROWS else []
            if stage == 0:
                if kind != BLOCKS:
                    for step in range(1, self.seq_size):
                        self.seq_copy(piece, side, step).wait_recv()
                held = [0]
            else:
                reached = [0]
                for bit in order[: stage - 1]:
                    reached += [block | 1 << bit for block in reached]
                held = [block | 1 << order[stage - 1] for block in reached]
                for block in reached:
                    self.block_copy(piece, side, block, order[stage - 1]).wait_recv()
            for bit in order[stage:]:
                for block in held:
                    self.start(self.block_copy(piece, side, block, bit))
        if stage == 0 and piece + self.ahead < len(self.pieces):
            self.send_rows(piece + self.ahead)

    def finish(self):
        for turn in range(len(self.pieces) + self.bits):
            for piece in range(len(self.pieces)):
                if 0 <= turn - piece <= self.bits:
                    self.advance(piece, turn - piece)
        for copy in self.local.values():
            copy.wait()
        for copy in self.started:
            copy.wait_send()


def gather_scratch(count, pieces):
    slots = lax.axis_size("dp") + lax.axis_size("seq")
    return [
        pltpu.SemaphoreType.DMA((count,)),
        pltpu.SemaphoreType.DMA((pieces, 2, slots)),
        pltpu.SemaphoreType.DMA((pieces, 2, slots)),
    ]


def gather_shapes(kinds, shards):
    dp_size, seq_size = (lax.axis_size("dp"), lax.axis_size("seq"))
    factor = {WHOLE: dp_size * seq_size, ROWS: seq_size, BLOCKS: dp_size}
    return [
        jax.ShapeDtypeStruct((s.shape[0] * factor[kind], s.shape[1]), s.dtype)
        for kind, s in zip(kinds, shards)
    ]


def gather_kernel(kinds, pieces, *refs):
    count = len(kinds)
    gather = Gather(kinds, pieces, refs[:count], refs[count : 2 * count], *refs[2 * count :])
    gather.barrier()
    gather.begin()
    gather.finish()


def gather_all(kinds, shards, pieces, collective_id):
    count = len(shards)
    return pl.pallas_call(
        functools.partial(gather_kernel, kinds, pieces),
        out_shape=gather_shapes(kinds, shards),
        in_specs=[pl.BlockSpec(memory_space=pl.ANY)] * count,
        out_specs=[pl.BlockSpec(memory_space=pl.ANY)] * count,
        scratch_shapes=gather_scratch(count, len(pieces)),
        compiler_params=pltpu.CompilerParams(collective_id=collective_id, has_side_effects=True),
        name="gather",
    )(*shards)


def attend_kernel(kinds, pieces, info, q_ref, kv_ref, *refs):
    count = len(kinds)
    shards = refs[:count]
    o_ref, full_ref, lse_ref, kv_all_ref = refs[count : count + 4]
    fulls = refs[count + 4 : 2 * count + 4]
    k_rows, slots, kv_send, kv_recv = refs[2 * count + 4 : 2 * count + 8]
    gather = Gather(kinds, pieces, shards, fulls, *refs[2 * count + 8 :])
    seq, seq_size = (gather.seq, gather.seq_size)
    reach, valid = (info[0], info[1])
    gather.barrier()

    def kv_copy(group, step):
        return pltpu.make_async_remote_copy(
            src_ref=kv_ref.at[group],
            dst_ref=slots.at[step, group],
            send_sem=kv_send.at[step, group],
            recv_sem=kv_recv.at[step, group],
            device_id=gather.along(step),
            device_id_type=MESH,
        )

    for group in range(KV_HEADS):
        for step in range(1, seq_size):

            @pl.when(seq + step < seq_size)
            def _():
                kv_copy(group, step).start()

    gather.begin()
    gather.advance(0, 0)
    slots[0] = kv_ref[...]
    beside = {1: [(0, 1)], 3: [(0, 2)], 5: [(1, 0)], 7: [(0, 3), (1, 1), (2, 0)]}
    for group in range(KV_HEADS):
        k_rows[0] = transposed(kv_ref[group, :HD, :])
        for step in range(1, seq_size):

            @pl.when(seq >= step)
            def _():
                kv_copy(group, step).wait_recv()
                k_rows[step] = transposed(slots[step, group, :HD, :])

        for part in range(2):

            @pl.loop(group * SHARE + part * SHARE // 2, group * SHARE + (part + 1) * SHARE // 2)
            def _(head):
                attend_head(
                    head, seq + 1, reach, valid, q_ref, slots, group, k_rows, o_ref, full_ref, lse_ref
                )

            for event in beside.get(group * 2 + part, []):
                gather.advance(*event)
    for step in range(seq_size):

        @pl.when(seq >= step)
        def _():
            kv_all_ref[step] = slots[step]

        @pl.when(seq < step)
        def _():
            kv_all_ref[step] = jnp.zeros_like(kv_ref)

    for group in range(KV_HEADS):
        for step in range(1, seq_size):

            @pl.when(seq + step < seq_size)
            def _():
                kv_copy(group, step).wait_send()

    gather.finish()


def attend_forward(info, query, kv, kinds, shards, pieces, collective_id):
    tokens = query.shape[1]
    seq_size = lax.axis_size("seq")
    count = len(shards)
    vmem = pl.BlockSpec(memory_space=pltpu.VMEM)
    hbm = pl.BlockSpec(memory_space=pl.ANY)
    out = pl.pallas_call(
        functools.partial(attend_kernel, kinds, pieces),
        out_shape=[
            jax.ShapeDtypeStruct(query.shape, jnp.bfloat16),
            jax.ShapeDtypeStruct(query.shape, jnp.float32),
            jax.ShapeDtypeStruct((HEADS, 1, tokens), jnp.float32),
            jax.ShapeDtypeStruct((seq_size, *kv.shape), kv.dtype),
            *gather_shapes(kinds, shards),
        ],
        in_specs=[pl.BlockSpec(memory_space=pltpu.SMEM), vmem, vmem] + [hbm] * count,
        out_specs=[vmem] * 4 + [hbm] * count,
        scratch_shapes=[
            pltpu.VMEM((seq_size, tokens, HD), jnp.bfloat16),
            pltpu.VMEM((seq_size, *kv.shape), kv.dtype),
            pltpu.SemaphoreType.DMA((seq_size, KV_HEADS)),
            pltpu.SemaphoreType.DMA((seq_size, KV_HEADS)),
            *gather_scratch(count, len(pieces)),
        ],
        compiler_params=pltpu.CompilerParams(
            collective_id=collective_id, has_side_effects=True, vmem_limit_bytes=48 * 2**20
        ),
        name="attend_forward",
    )(info, query, kv, *shards)
    return (out[:4], out[4:])


def total_kernel(x_ref, o_ref, slots, send_sems, recv_sems):
    dp, seq = (lax.axis_index("dp"), lax.axis_index("seq"))
    dp_size, seq_size = (lax.axis_size("dp"), lax.axis_size("seq"))
    devices = dp_size * seq_size
    me = dp * seq_size + seq

    def device(step):
        other = lax.rem(me + step, devices)
        return (other // seq_size, lax.rem(other, seq_size))

    def copy(step):
        return pltpu.make_async_remote_copy(
            src_ref=x_ref,
            dst_ref=slots.at[step],
            send_sem=send_sems.at[step],
            recv_sem=recv_sems.at[step],
            device_id=device(step),
            device_id_type=MESH,
        )

    barrier = pltpu.get_barrier_semaphore()

    @pl.loop(1, devices)
    def _(step):
        pl.semaphore_signal(barrier, inc=1, device_id=device(step), device_id_type=MESH)

    pl.semaphore_wait(barrier, devices - 1)

    @pl.loop(1, devices)
    def _(step):
        copy(step).start()

    @pl.loop(1, devices)
    def _(step):
        copy(step).wait()

    o_ref[...] = x_ref[...] + jnp.sum(slots[1:], 0)


def total_of(value, collective_id):
    devices = lax.axis_size("dp") * lax.axis_size("seq")
    return pl.pallas_call(
        total_kernel,
        out_shape=jax.ShapeDtypeStruct((8, 128), jnp.float32),
        in_specs=[pl.BlockSpec(memory_space=pltpu.VMEM)],
        out_specs=pl.BlockSpec(memory_space=pltpu.VMEM),
        scratch_shapes=[
            pltpu.VMEM((devices, 8, 128), jnp.float32),
            pltpu.SemaphoreType.DMA((devices,)),
            pltpu.SemaphoreType.DMA((devices,)),
        ],
        compiler_params=pltpu.CompilerParams(collective_id=collective_id, has_side_effects=True),
        name="total",
    )(jnp.full((8, 128), value, jnp.float32))[0, 0]


PARTS = 4


def swapped(block, axis, mask):
    return lax.ppermute(block, axis, [(i, i ^ mask) for i in range(lax.axis_size(axis))])


def by_distance(rows):
    size = lax.axis_size("dp")
    index = lax.axis_index("dp")
    depth = rows.shape[0] // size
    pick = lambda j: lax.dynamic_slice_in_dim(rows, (index ^ j) * depth, depth, 0)
    return (
        jnp.concatenate([pick(j) for j in range(0, size, 2)], 0),
        jnp.concatenate([pick(j) for j in range(1, size, 2)], 0),
    )


def owner_sum(total, split, dtype=jnp.bfloat16):
    size = total.shape[0]
    depth = total.shape[1]
    low, high = (total[..., :split], total[..., split:])
    bits = size.bit_length() - 1

    def plus(kept, got):
        return (kept.astype(jnp.float32) + got.astype(jnp.float32)).astype(dtype)

    for step in range(bits):
        half = low.shape[0] // 2
        low_pair = low.reshape(half, 2, depth, low.shape[-1])
        low_got, high_got = yield [
            ("dp", 2 << step, low_pair[:, 1].reshape(half * depth, -1)),
            ("dp", 1 << (bits - step), high[half:].reshape(half * depth, -1)),
        ]
        low = plus(low_pair[:, 0], low_got.reshape(half, depth, -1))
        high = plus(high[:half], high_got.reshape(half, depth, -1))
    total = jnp.concatenate([low[0], high[0]], -1)
    index = lax.axis_index("seq")
    mask = lax.axis_size("seq") // 2
    while mask:
        half = total.shape[0] // 2
        upper = ((index // mask) % 2) * half
        send = lax.dynamic_slice_in_dim(total, half - upper, half, 0)
        (got,) = yield [("seq", mask, send)]
        kept = lax.dynamic_slice_in_dim(total, upper, half, 0)
        mask //= 2
        total = plus(kept, got) if mask else kept.astype(jnp.float32) + got.astype(jnp.float32)
    return total


class Sums:
    def __init__(self):
        self.results = []
        self.ready = []
        self.arrived = []

    def step(self, place, generator, answer):
        try:
            self.ready.append((place, generator, generator.send(answer)))
        except StopIteration as stop:
            self.results[place] = stop.value

    def add(self, total, split, dtype=jnp.bfloat16):
        self.results.append(None)
        self.step(len(self.results) - 1, owner_sum(total, split, dtype), None)

    def absorb(self):
        arrived, self.arrived = (self.arrived, [])
        for place, generator, answer in arrived:
            self.step(place, generator, answer)

    def round(self, work, inputs, prompt=True):
        if prompt:
            self.absorb()
        sending, self.ready = (self.ready, [])
        blocks = [[block for _, _, block in wanted] for _, _, wanted in sending]
        came = [answer for _, _, answer in self.arrived]
        inputs, blocks, came = lax.optimization_barrier((inputs, blocks, came))
        self.arrived = [(p, g, a) for (p, g, _), a in zip(self.arrived, came)]
        self.absorb()
        answers = [
            [swapped(block, axis, mask) for (axis, mask, _), block in zip(wanted, group)]
            for (_, _, wanted), group in zip(sending, blocks)
        ]
        outputs = work(*inputs)
        later = [[block for _, _, block in wanted] for _, _, wanted in self.ready]
        outputs, answers, later = lax.optimization_barrier((outputs, answers, later))
        self.ready = [
            (p, g, [(axis, mask, block) for (axis, mask, _), block in zip(wanted, group)])
            for (p, g, wanted), group in zip(self.ready, later)
        ]
        self.arrived = [(p, g, a) for (p, g, _), a in zip(sending, answers)]
        return outputs


def weight_gradient(left, right, right_dim):
    left_own, left_other = left
    other = contract(left_other, right, 1, right_dim).astype(jnp.bfloat16)
    got = swapped(other, "dp", 1)
    total = contract(left_own, right, 1, right_dim) + got.astype(jnp.float32)
    size = lax.axis_size("dp") // 2
    return total.astype(jnp.bfloat16).reshape(size, total.shape[0] // size, total.shape[1])


def per_device(
    hidden_in,
    out_grad,
    seq_lengths,
    seq_counts,
    segment_ids,
    qkv_weight,
    qkv_m,
    qkv_v,
    out_weight,
    out_m,
    out_v,
    gate_up_weight,
    gate_up_m,
    gate_up_v,
    down_weight,
    down_m,
    down_v,
    norm_gains,
    gain_m,
    gain_v,
):
    tok_dev = hidden_in.shape[0]
    q_width = HEADS * HD
    kv_width = KV_HEADS * HD
    seg_all = segment_ids[0]
    lengths = seq_lengths[0]
    seq_index = lax.axis_index("seq")
    offset = seq_index * tok_dev
    seg_local = lax.dynamic_slice_in_dim(seg_all, offset, tok_dev, 0)
    starts = jnp.cumsum(lengths, dtype=jnp.int32) - lengths
    slot_ids = jnp.arange(lengths.shape[0], dtype=jnp.int32)
    seq_start = jnp.sum(
        jnp.where(seg_local[:, None] == slot_ids[None, :], starts[None, :], 0),
        axis=1,
        dtype=jnp.int32,
    )
    positions = offset + jnp.arange(tok_dev, dtype=jnp.int32) - seq_start
    cos_table, sin_table = rope_tables(positions)
    valid = (seg_local[0] < seq_counts[0]).astype(jnp.int32)
    reach = jnp.where(valid > 0, seq_index - seq_start[0] // tok_dev + 1, 1)
    info = jnp.stack([reach, valid]).astype(jnp.int32)

    devices = lax.axis_size("dp") * lax.axis_size("seq")
    own = norm_gains.shape[1]
    gain_rows = jnp.pad(norm_gains.astype(jnp.bfloat16), ((0, 14), (0, 128 - own)))
    width = qkv_weight.shape[1] // 4
    part = FF // PARTS
    gu_shards = [
        jnp.concatenate(
            [
                gate_up_weight[:, p * part : (p + 1) * part],
                gate_up_weight[:, FF + p * part : FF + (p + 1) * part],
            ],
            1,
        ).astype(jnp.bfloat16)
        for p in range(PARTS)
    ]
    w_qkv, gain_rows, gu_shards[0] = gather_all(
        [WHOLE, WHOLE, ROWS],
        [qkv_weight.astype(jnp.bfloat16), gain_rows, gu_shards[0]],
        [
            (1, 0, 128, 128),
            (0, 0, width, 2 * width),
            (0, 2 * width, 3 * width, 4 * width),
            (2, 0, part, 2 * part),
        ],
        1,
    )
    w_gain = jnp.moveaxis(gain_rows.reshape(devices, 16, 128)[:, :2, :own], 1, 0).reshape(2, -1)
    gain_attn = w_gain[0].astype(jnp.float32)
    gain_mlp = w_gain[1].astype(jnp.float32)
    residual = hidden_in.astype(jnp.float32)
    inv_one, normed = norm_forward(residual, gain_attn)
    normed_low = normed.astype(jnp.bfloat16)
    qkv_out = contract(w_qkv, normed_low, 0, 1)
    query = rotate(qkv_out[:q_width], cos_table, sin_table).astype(jnp.bfloat16)
    key = rotate(qkv_out[q_width : q_width + kv_width], cos_table, sin_table).astype(jnp.bfloat16)
    value = qkv_out[q_width + kv_width :].astype(jnp.bfloat16)
    kv_own = jnp.concatenate(
        [key.reshape(KV_HEADS, HD, tok_dev), value.reshape(KV_HEADS, HD, tok_dev)], 1
    )
    down_depth = down_weight.shape[0]
    spare = -down_depth % 16
    shards = [
        out_weight.astype(jnp.bfloat16),
        jnp.pad(down_weight.astype(jnp.bfloat16), ((0, spare), (0, 0))),
        *gu_shards,
    ]
    kinds = [WHOLE, WHOLE, BLOCKS] + [WHOLE] * (PARTS - 1)
    model = out_weight.shape[1]
    near = part // 256 * 128 + 128
    pieces = [(2, 0, part, 2 * part), (0, 0, model // 2, model)]
    pieces += [(1, low, low + model // 4, low + model // 2) for low in (0, model // 2)]
    pieces += [(2 + p, 0, part, 2 * part) for p in range(1, PARTS - 1)]
    pieces += [(1 + PARTS, 0, near, part), (1 + PARTS, part, 2 * part - near, 2 * part)]
    (attended, attended_full, lse, kv_all), (w_out, w_down, *w_gu) = attend_forward(
        info, query, kv_own, kinds, shards, pieces, 2
    )
    if spare:
        w_down = w_down.reshape(devices, -1, model)[:, :down_depth].reshape(-1, model)
    mid_rows = residual + contract(attended, w_out, 0, 0)
    inv_two, normed_two = norm_forward(mid_rows, gain_mlp)
    inner_rows = normed_two.astype(jnp.bfloat16)

    inner_blocks = by_distance(inner_rows.T)

    def mlp_part(inner_rows, inner_blocks, out_grad, w_gu_part, w_down_part):
        gate_up = matmul(inner_rows, w_gu_part)
        gate_vals, up_vals = (gate_up[:, :part], gate_up[:, part:])
        d_hidden = contract(out_grad, w_down_part, 1, 1)
        sigmoid_gate = jax.nn.sigmoid(gate_vals)
        hidden = (gate_vals * sigmoid_gate * up_vals).astype(jnp.bfloat16)
        d_gate = d_hidden * up_vals * sigmoid_gate * (1.0 + gate_vals * (1.0 - sigmoid_gate))
        d_up = d_hidden * gate_vals * sigmoid_gate
        d_gu = jnp.concatenate([d_gate, d_up], -1).astype(jnp.bfloat16)
        return (hidden, d_gu, weight_gradient(inner_blocks, d_gu, 0))

    def down_rows(p):
        return w_down[p * part : (p + 1) * part]

    sums = Sums()
    hidden_parts, d_gu_parts = ([], [])
    out = mlp_part(inner_rows, inner_blocks, out_grad, w_gu[0], down_rows(0))
    for p in range(1, PARTS + 1):
        hidden_parts.append(out[0])
        d_gu_parts.append(out[1])
        sums.add(out[2], part)
        if p < PARTS:
            out = sums.round(
                mlp_part, (inner_rows, inner_blocks, out_grad, w_gu[p], down_rows(p)), prompt=False
            )

    half = out_grad.shape[1] // 2

    def finish_mlp(hidden_parts, d_gu_parts, w_gu, out_grad, mid_rows, w_out):
        hidden = jnp.concatenate(hidden_parts, -1)
        d_inner = sum(contract(d, w, 1, 1) for d, w in zip(d_gu_parts, w_gu))
        back_two, g_gain_two = norm_backward(mid_rows, inv_two, gain_mlp, d_inner)
        d_mid = out_grad.astype(jnp.float32) + back_two
        d_branch = d_mid.astype(jnp.bfloat16)
        d_attended = contract(w_out, d_branch, 1, 1).astype(jnp.bfloat16)
        hidden_blocks = by_distance(hidden.T)
        g_down = weight_gradient(hidden_blocks, out_grad[:, :half], 0)
        return (hidden, hidden_blocks, g_gain_two, d_mid, d_branch, d_attended, g_down)

    hidden, hidden_blocks, g_gain_two, d_mid, d_branch, d_attended, g_down = sums.round(
        finish_mlp, (hidden_parts, d_gu_parts, w_gu, out_grad, mid_rows, w_out)
    )
    sums.add(g_down, half // 2)

    def attention_part(first):
        def work(d_attended, hidden_blocks, right):
            grads = attend_backward(
                info, query, kv_all, attended_full, lse, d_attended, first, HEADS // 2
            )
            return (grads, weight_gradient(hidden_blocks, right, 0))

        return work

    early, g_down = sums.round(
        attention_part(0), (d_attended, hidden_blocks, out_grad[:, half:])
    )
    sums.add(g_down, half // 2)
    late, g_out = sums.round(
        attention_part(HEADS // 2), (d_attended, by_distance(attended), d_branch)
    )
    sums.add(g_out, half)

    def finish_attention(early, late, normed_low):
        d_query = jnp.concatenate([early[0], late[0]], 0)
        d_kv = sum_to_owner(jnp.concatenate([early[1], late[1]], 1))
        d_qkv = jnp.concatenate(
            [
                rotate(d_query, cos_table, -sin_table),
                rotate(d_kv[:, :HD].reshape(kv_width, tok_dev), cos_table, -sin_table),
                d_kv[:, HD:].reshape(kv_width, tok_dev),
            ],
            0,
        ).astype(jnp.bfloat16)
        d_normed = contract(d_qkv, w_qkv, 0, 1)
        g_qkv = weight_gradient(by_distance(normed_low.T), d_qkv, 1)
        g_gain_one = jnp.sum(d_normed * residual * inv_one, axis=0)
        g_gains = jnp.stack([g_gain_one, g_gain_two], 0).reshape(2, devices, own)
        g_gains = by_distance(jnp.moveaxis(g_gains, 0, 1).reshape(devices, 2 * own))
        g_gains = (g_gains[0] + swapped(g_gains[1], "dp", 1)).reshape(
            lax.axis_size("dp") // 2, -1, 2 * own
        )
        return (d_normed, g_qkv, g_gains)

    d_normed, g_qkv, g_gains = sums.round(finish_attention, (early, late, normed_low))
    sums.add(g_qkv, g_qkv.shape[-1] // 2)
    sums.add(g_gains, own, jnp.float32)

    (input_grad,) = sums.round(
        lambda d_normed, d_mid: (
            d_mid + norm_backward(residual, inv_one, gain_attn, d_normed)[0],
        ),
        (d_normed, d_mid),
    )
    (block_out,) = sums.round(
        lambda hidden, mid_rows: ((mid_rows + matmul(hidden, w_down)).astype(jnp.bfloat16),),
        (hidden, mid_rows),
    )
    while sums.ready or sums.arrived:
        sums.round(lambda: (), ())
    summed = sums.results
    g_gu_own = jnp.concatenate(
        [s[:, :part] for s in summed[:PARTS]] + [s[:, part:] for s in summed[:PARTS]], 1
    )
    g_down_own = jnp.concatenate(summed[PARTS : PARTS + 2], 1)
    g_out_own, g_qkv_own, g_gains_own = summed[PARTS + 2 :]
    g_gains_own = g_gains_own.reshape(2, own)
    local_sq = (
        jnp.sum(g_qkv_own * g_qkv_own)
        + jnp.sum(g_out_own * g_out_own)
        + jnp.sum(g_gu_own * g_gu_own)
        + jnp.sum(g_down_own * g_down_own)
        + jnp.sum(g_gains_own * g_gains_own)
    )
    total_sq = total_of(local_sq, 3)
    grad_norm = jnp.sqrt(total_sq)
    clip_factor = jnp.minimum(1.0, CLIP_NORM / (grad_norm + 1e-06))
    new_qkv, new_qkv_m, new_qkv_v = adam_update(
        qkv_weight, qkv_m, qkv_v, g_qkv_own, clip_factor, 0.06, WEIGHT_DECAY
    )
    new_out, new_out_m, new_out_v = adam_update(
        out_weight, out_m, out_v, g_out_own, clip_factor, 0.4, WEIGHT_DECAY
    )
    new_gu, new_gu_m, new_gu_v = adam_update(
        gate_up_weight, gate_up_m, gate_up_v, g_gu_own, clip_factor, 0.06, WEIGHT_DECAY
    )
    new_down, new_down_m, new_down_v = adam_update(
        down_weight, down_m, down_v, g_down_own, clip_factor, 0.06, WEIGHT_DECAY
    )
    new_gains, new_gain_m, new_gain_v = adam_update(
        norm_gains, gain_m, gain_v, g_gains_own, clip_factor, 0.6, 0.0
    )
    return (
        block_out,
        input_grad,
        grad_norm,
        new_qkv,
        new_qkv_m,
        new_qkv_v,
        new_out,
        new_out_m,
        new_out_v,
        new_gu,
        new_gu_m,
        new_gu_v,
        new_down,
        new_down_m,
        new_down_v,
        new_gains,
        new_gain_m,
        new_gain_v,
    )


def solution(mesh):
    in_specs = (
        P(("dp", "seq"), None),
        P(("dp", "seq"), None),
        P("dp", None),
        P("dp"),
        P("dp", None),
        P(("dp", "seq"), None),
        P(("dp", "seq"), None),
        P(("dp", "seq"), None),
        P(("dp", "seq"), None),
        P(("dp", "seq"), None),
        P(("dp", "seq"), None),
        P(("dp", "seq"), None),
        P(("dp", "seq"), None),
        P(("dp", "seq"), None),
        P(("dp", "seq"), None),
        P(("dp", "seq"), None),
        P(("dp", "seq"), None),
        P(None, ("dp", "seq")),
        P(None, ("dp", "seq")),
        P(None, ("dp", "seq")),
    )
    out_specs = (
        P(("dp", "seq"), None),
        P(("dp", "seq"), None),
        P(),
        P(("dp", "seq"), None),
        P(("dp", "seq"), None),
        P(("dp", "seq"), None),
        P(("dp", "seq"), None),
        P(("dp", "seq"), None),
        P(("dp", "seq"), None),
        P(("dp", "seq"), None),
        P(("dp", "seq"), None),
        P(("dp", "seq"), None),
        P(("dp", "seq"), None),
        P(("dp", "seq"), None),
        P(("dp", "seq"), None),
        P(None, ("dp", "seq")),
        P(None, ("dp", "seq")),
        P(None, ("dp", "seq")),
    )
    return jax.shard_map(
        per_device, mesh=mesh, in_specs=in_specs, out_specs=out_specs, check_vma=False
    )
```

time: 1790 us -> 1410 us (0.79)
  waiting for transfers between devices: 1290 us -> 294 us
  Pallas kernels: 55.8 us -> 463 us
  blocking collectives: 111 us -> 0 us
  starting transfers between devices: 9.32 us -> 116 us
  local copies, waits for them, and re-layouts: 17.9 us -> 115 us
  other arithmetic: 48.4 us -> 120 us
  matrix products: 227 us -> 271 us
    pallas_call x1 -> x3, Pallas kernels: 20.2 us -> 426 us  [the longest x1 342 us: attend_forward(): pl.pallas_call(functools.partial(attend_kernel, kinds, pieces), out_shape...]
    all_gather x4 -> x0, waiting for transfers between devices: 399 us -> none  [gathered(): lax.all_gather(shard.astype(jnp.bfloat16), ('dp', 'seq'), axis=0, tiled=T...]
    unnamed x15 -> x0, waiting for transfers between devices: 387 us -> none
    reduce_scatter x7 -> x0, waiting for transfers between devices: 374 us -> none  [the longest x4 212 us: scattered(): lax.psum_scatter(part, 'seq', scatter_dimension=0, tiled=True)]
    ppermute x3 -> x63, waiting for transfers between devices: 15.2 us -> 241 us  [swapped(): lax.ppermute(block, axis, [(i, i ^ mask) for i in range(lax.axis_size(axi...]
    ppermute x3 -> x63, starting transfers between devices: 4.88 us -> 113 us  [swapped(): lax.ppermute(block, axis, [(i, i ^ mask) for i in range(lax.axis_size(axi...]
    all_gather x1 -> x0, blocking collectives: 70 us -> none  [per_device(): lax.all_gather(norm_gains.astype(jnp.bfloat16), ('dp', 'seq'), axis=1, ti...]
    ppermute x3, waiting for transfers between devices: 112 us -> 53.5 us  [sum_to_owner(): lax.ppermute(total.astype(jnp.bfloat16), 'seq', [(i, i - 1) for i in rang...]
  transfers between devices with their start and end apart: 19 -> 66, of which waited for: 14 -> 24; matrix products, arithmetic and copies ran while one was open for 10% -> 16% of each run, Pallas kernels for 3% -> 3%
where the time goes in v2:
time: 1410 us; the launch traced here: 1390 us
  Pallas kernels  463 us (33%)
  waiting for transfers between devices  294 us (21%)
  matrix products  271 us (19%)
  other arithmetic  120 us (9%)
  starting transfers between devices  116 us (8%)
  local copies, waits for them, and re-layouts  115 us (8%)
    pallas_call x1, Pallas kernels, attend_forward(): pl.pallas_call(functools.partial(attend_kernel, kinds, pieces), out_shape...  342 us
    ppermute x63, waiting for transfers between devices, swapped(): lax.ppermute(block, axis, [(i, i ^ mask) for i in range(lax.axis_size(axi...  241 us
    dot_general x28, matrix products, contract(): lax.dot_general(left, right, (((left_dim,), (right_dim,)), ((), ())), pre...  209 us
    ppermute x63, starting transfers between devices, swapped(): lax.ppermute(block, axis, [(i, i ^ mask) for i in range(lax.axis_size(axi...  113 us
    pallas_call x1, Pallas kernels, gather_all(): pl.pallas_call(functools.partial(gather_kernel, kinds, pieces), out_shape...  73.7 us
    dot_general x5, matrix products, matmul(): return jnp.dot(left, right, preferred_element_type=jnp.float32)  62 us
    ppermute x3, waiting for transfers between devices, sum_to_owner(): lax.ppermute(total.astype(jnp.bfloat16), 'seq', [(i, i - 1) for i in rang...  53.5 us
    pallas_call x2, Pallas kernels, attend_backward(): pl.pallas_call(backward_kernel, grid_spec=pltpu.PrefetchScalarGridSpec(nu...  36.9 us
  transfers between devices with their start and end apart: 66, of which 24 were waited for; matrix products, arithmetic and copies ran while one was open for 16% of the time, Pallas kernels for 3%

profile of v2, /device:TPU:0, one launch (start us, length us, event | category | flops | bytes accessed | tf_op | source)
XLA Modules:
  0.0 1392.0 jit_solution(17006771795893963185)
XLA Ops:
  13.7 73.7 %gather.1 = (bf16[2048,2560]{1,0:T(8,128)(2,1)}, bf16[512,128]{1,0:T(8,128)(2,1)}, bf16[256,2816]{1,0:T(8,128)(2,1)}) custom-call(bf16[64,2560]{1,0:T(8,128)(2,1)} %convert_element_type.908.refs_0_, bf16[16,128]{1,0:T(8,128)(2,1)} %pad.4.refs_1_, bf16[64,2816]{1,0:T(8,128)(2,1)} %get-tuple-element.544.refs_2_), custom_call_target="tpu_custom_call" | custom-call | tf_op jit(solution)/shard_map/gather/pallas_call | solution.py:403
  89.0 9.1 fusion.129
  111.5 341.6 %attend_forward.1 = (bf16[2048,512]{1,0:T(8,128)(2,1)S(1)}, f32[2048,512]{1,0:T(8,128)}, f32[32,1,512]{2,1,0:T(1,128)S(1)}, bf16[4,4,128,512]{3,2,1,0:T(8,128)(2...) custom-call(s32[2]{0:T(128)S(1)} %pad_add_fusion.info, ...), custom_call_target="tpu_custom_call" | custom-call | tf_op jit(solution)/shard_map/attend_forward/pallas_call | solution.py:491
  453.2 10.3 multiply_reduce_fusion.2
  466.9 11.3 fusion.130
  479.4 8.0 multiply_convert_fusion.11
  488.4 7.3 convolution_convert_fusion.5
  500.5 6.7 fusion.127
  507.2 7.0 add_convert_fusion.5
  515.7 11.7 fusion.131
  527.4 7.9 multiply_convert_fusion.8
  550.7 6.6 add_convert_fusion.4
  557.4 17.8 %collective-permute-done.2 = bf16[512,1408]{1,0:T(8,128)(2,1)S(1)} collective-permute-done((bf16[512,1408]{1,0:T(8,128)(2,1)S(1)}, bf16[512,1408]{1,0:T(8,128)(2,1)S(1)}, u32[]{:S(2)}, u32[]{:S(2)}) %collective-permute-start.2) | collective-permute-done | bytes 1441824 | tf_op jit(solution)/shard_map/ppermute | solution.py:577
  578.7 11.7 fusion.132
  590.4 8.0 multiply_convert_fusion.5
  618.7 19.3 %collective-permute-done.5 = bf16[512,1408]{1,0:T(8,128)(2,1)S(1)} collective-permute-done((bf16[512,1408]{1,0:T(8,128)(2,1)}, bf16[512,1408]{1,0:T(8,128)(2,1)S(1)}, u32[]{:S(2)}, u32[]{:S(2)}) %collective-permute-start.5) | collective-permute-done | bytes 1441824 | tf_op jit(solution)/shard_map/ppermute | solution.py:577
  644.2 9.7 fusion.133
  687.4 33.6 %collective-permute-done.8 = bf16[256,1408]{1,0:T(8,128)(2,1)S(1)} collective-permute-done((bf16[256,1408]{1,0:T(8,128)(2,1)S(1)}, bf16[256,1408]{1,0:T(8,128)(2,1)S(1)}, u32[]{:S(2)}, u32[]{:S(2)}) %collective-permute-start.8) | collective-permute-done | bytes 720928 | tf_op jit(solution)/shard_map/ppermute | solution.py:577
  736.9 6.7 dynamic-slice_bitcast_fusion
  743.6 6.3 concatenate.126
  749.8 7.9 convolution_convert_fusion.1
  757.7 10.5 fusion.134
  768.2 10.4 fusion.135
  778.7 7.7 fusion.136
  786.4 14.9 %multiply_reduce_fusion = (f32[512]{0:T(512)S(1)}, f32[2048]{0:T(1024)}, f32[512,2048]{1,0:T(8,128)}) fusion(f32[512,2048]{1,0:T(8,128)S(1)} %copy-done.18, f32[2048]{0:T(1024)S(1)} %copy-done.165, f32[512]{0:T(512)S(1)} %copy-done.170, bf16[512,2816]{1,0:T(8,128)(2,1)} %pad_maximum_fusion.4, bf16[2048,2816]{1,0:T(8,128)(2,1)} %get-tuple-element.301, ...), kind=kOutput, calls=%fused_computation.36 | convolution fusion | flops 5915014656 | bytes 35409920 | tf_op jit(solution)/shard_map/dot_general | solution.py:32
  806.2 9.9 convolution_convert_fusion.8.do_ref
  822.0 26.4 %collective-permute-start.17 = (bf16[128,2816]{1,0:T(8,128)(2,1)}, bf16[128,2816]{1,0:T(8,128)(2,1)S(1)}, u32[]{:S(2)}, u32[]{:S(2)}) collective-permute-start(bf16[128,2816]{1,0:T(8,128)(2,1)} %fusion.92), channel_id=1, source_target_pairs={{0,2},{1,3},{2,0},{3,1},{4,6},{5,7},{6,4},{7,5},{8,10},{9,11},{10,... | collective-permute-start | bytes 2162696 | tf_op jit(solution)/shard_map/ppermute | solution.py:577
  850.3 7.0 add_convert_fusion.1
  857.4 8.0 collective-permute-done.17
  891.3 20.7 %collective-permute-start.26 = (bf16[64,2816]{1,0:T(8,128)(2,1)}, bf16[64,2816]{1,0:T(8,128)(2,1)}, u32[]{:S(2)}, u32[]{:S(2)}) collective-permute-start(bf16[64,2816]{1,0:T(8,128)(2,1)} %constant_dynamic-slice_fusion.28), channel_id=1, source_target_pairs={{0,1},{1,0},{2,3},{3,2},{4,5},{5,4},{6,7},{7,6},{8,9},{9,8},{10,11... | collective-permute-start | bytes 1081352 | tf_op jit(solution)/shard_map/ppermute | solution.py:577
  914.5 18.1 %attend_backward.2 = (f32[1024,512]{1,0:T(8,128)S(1)}, f32[4,2,128,512]{3,2,1,0:T(8,128)S(1)}) custom-call(s32[2]{0:T(128)S(1)} %pad_add_fusion.info, bf16[2048,512]{1,0:T(8,128)(2,1)S(1)} %bitcast.399, bf16[4,4,128,512]{3,2,1,0:T(8,128)(2,1)S(1)} %copy-done.11, f32[2048,512]{1,0:T(8,128)} %get-tuple-element.314.full_ref, ...), custom_call_target="tpu_custom_call" | custom-call | flops 42949672960 | bytes 14680064 | tf_op jit(solution)/shard_map/attend_backward/pallas_call | solution.py:167
  933.8 13.1 collective-permute-done.23
  947.6 13.1 collective-permute-start.27
  966.0 26.6 %collective-permute-done.27 = bf16[128,2816]{1,0:T(8,128)(2,1)S(1)} collective-permute-done((bf16[128,2816]{1,0:T(8,128)(2,1)}, bf16[128,2816]{1,0:T(8,128)(2,1)S(1)}, u32[]{:S(2)}, u32[]{:S(2)}) %collective-permute-start.27) | collective-permute-done | bytes 720928 | tf_op jit(solution)/shard_map/ppermute | solution.py:577
  1012.6 8.8 collective-permute-done.33
  1023.6 11.2 collective-permute-done.35
  1038.7 18.8 %attend_backward.3 = (f32[1024,512]{1,0:T(8,128)S(1)}, f32[4,2,128,512]{3,2,1,0:T(8,128)S(1)}) custom-call(s32[2]{0:T(128)S(1)} %pad_add_fusion.info, bf16[2048,512]{1,0:T(8,128)(2,1)S(1)} %bitcast.400, bf16[4,4,128,512]{3,2,1,0:T(8,128)(2,1)S(1)} %copy-done.12, f32[2048,512]{1,0:T(8,128)} %get-tuple-element.314.full_ref, ...), custom_call_target="tpu_custom_call" | custom-call | flops 42949672960 | bytes 14680064 | tf_op jit(solution)/shard_map/attend_backward/pallas_call | solution.py:167
  1092.3 53.5 %collective-permute-done.38 = bf16[4,128,512]{2,1,0:T(8,128)(2,1)S(1)} collective-permute-done((bf16[4,128,512]{2,1,0:T(8,128)(2,1)S(1)}, bf16[4,128,512]{2,1,0:T(8,128)(2,1)S(1)}, u32[]{:S(2)}, u32[]{:S(2)}) %collective-permute-start.38) | collective-permute-done | bytes 524320 | tf_op jit(solution)/shard_map/ppermute | solution.py:213
  1146.2 6.5 convolution_convert_fusion.6
  1164.2 10.3 fusion.6
  1184.3 6.6 add_convert_fusion.6
  1190.9 8.9 collective-permute-done.44
  1199.8 17.6 %collective-permute-done.45 = bf16[352,1024]{1,0:T(8,128)(2,1)S(1)} collective-permute-done((bf16[352,1024]{1,0:T(8,128)(2,1)}, bf16[352,1024]{1,0:T(8,128)(2,1)S(1)}, u32[]{:S(2)}, u32[]{:S(2)}) %collective-permute-start.45) | collective-permute-done | bytes 720928 | tf_op jit(solution)/shard_map/ppermute | solution.py:577
  1244.1 30.1 %collective-permute-done.51 = bf16[256,1024]{1,0:T(8,128)(2,1)S(1)} collective-permute-done((bf16[256,1024]{1,0:T(8,128)(2,1)S(1)}, bf16[256,1024]{1,0:T(8,128)(2,1)S(1)}, u32[]{:S(2)}, u32[]{:S(2)}) %collective-permute-start.51) | collective-permute-done | bytes 524320 | tf_op jit(solution)/shard_map/ppermute | solution.py:577
  1290.1 17.7 %add_convert_fusion.8 = bf16[512,2048]{1,0:T(8,128)(2,1)} fusion(f32[512,2048]{1,0:T(8,128)S(1)} %copy-done.19, bf16[512,5632]{1,0:T(8,128)(2,1)S(1)} %bitcast.420, bf16[5632,2048]{1,0:T(8,128)(2,1)} %get-tuple-element.236), kind=kOutput, calls=%fused_computation.34 | convolution fusion | flops 11813257216 | bytes 35127296 | tf_op jit(solution)/shard_map/dot_general | solution.py:28
  1322.9 21.2 %collective-permute-done.62 = f32[2,128]{1,0:T(2,128)S(1)} collective-permute-done((f32[2,128]{1,0:T(2,128)S(1)}, f32[2,128]{1,0:T(2,128)S(1)}, u32[]{:S(2)}, u32[]{:S(2)}) %collective-permute-start.62) | collective-permute-done | bytes 1056 | tf_op jit(solution)/shard_map/ppermute | solution.py:577
  1359.3 10.7 total.1
  1383.1 6.9 multiply_subtract_fusion
  (734 shorter events, 342.0 us)
Async XLA Ops:
  541.2 34.0 %collective-permute-start.2 = (bf16[512,1408]{1,0:T(8,128)(2,1)S(1)}, bf16[512,1408]{1,0:T(8,128)(2,1)S(1)}, u32[]{:S(2)}, u32[]{:S(2)}) collective-permute-start(bf16[512,1408]{1,0:T(8,128)(2,1)S(1)} %bitcast.472), channel_id=1, source_target_pairs={{0,8},{4,12},{8,0},{12,4},{16,24},{20,28},{24,16},{28,20},{1,9},{5... | collective-permute-start | bytes 4325384 | tf_op jit(solution)/shard_map/ppermute | solution.py:577
  542.3 33.6 %collective-permute-start.3 = (bf16[512,1408]{1,0:T(8,128)(2,1)S(1)}, bf16[512,1408]{1,0:T(8,128)(2,1)S(1)}, u32[]{:S(2)}, u32[]{:S(2)}) collective-permute-start(bf16[512,1408]{1,0:T(8,128)(2,1)S(1)} %bitcast.471), channel_id=1, source_target_pairs={{0,16},{4,20},{8,24},{12,28},{16,0},{20,4},{24,8},{28,12},{1,17},{... | collective-permute-start | bytes 4325384 | tf_op jit(solution)/shard_map/ppermute | solution.py:577
  603.8 34.2 %collective-permute-start.5 = (bf16[512,1408]{1,0:T(8,128)(2,1)}, bf16[512,1408]{1,0:T(8,128)(2,1)S(1)}, u32[]{:S(2)}, u32[]{:S(2)}) collective-permute-start(bf16[512,1408]{1,0:T(8,128)(2,1)} %bitcast.29), channel_id=1, source_target_pairs={{0,8},{4,12},{8,0},{12,4},{16,24},{20,28},{24,16},{28,20},{1,9},{5... | collective-permute-start | bytes 4325384 | tf_op jit(solution)/shard_map/ppermute | solution.py:577
  604.9 33.9 %collective-permute-start.6 = (bf16[512,1408]{1,0:T(8,128)(2,1)}, bf16[512,1408]{1,0:T(8,128)(2,1)S(1)}, u32[]{:S(2)}, u32[]{:S(2)}) collective-permute-start(bf16[512,1408]{1,0:T(8,128)(2,1)} %bitcast.30), channel_id=1, source_target_pairs={{0,16},{4,20},{8,24},{12,28},{16,0},{20,4},{24,8},{28,12},{1,17},{... | collective-permute-start | bytes 4325384 | tf_op jit(solution)/shard_map/ppermute | solution.py:577
  671.0 50.1 %collective-permute-start.10 = (bf16[512,1408]{1,0:T(8,128)(2,1)S(1)}, bf16[512,1408]{1,0:T(8,128)(2,1)S(1)}, u32[]{:S(2)}, u32[]{:S(2)}) collective-permute-start(bf16[512,1408]{1,0:T(8,128)(2,1)S(1)} %bitcast.461), channel_id=1, source_target_pairs={{0,8},{4,12},{8,0},{12,4},{16,24},{20,28},{24,16},{28,20},{1,9},{5... | collective-permute-start | bytes 4325384 | tf_op jit(solution)/shard_map/ppermute | solution.py:577
  672.0 49.1 %collective-permute-start.11 = (bf16[512,1408]{1,0:T(8,128)(2,1)S(1)}, bf16[512,1408]{1,0:T(8,128)(2,1)S(1)}, u32[]{:S(2)}, u32[]{:S(2)}) collective-permute-start(bf16[512,1408]{1,0:T(8,128)(2,1)S(1)} %bitcast.458), channel_id=1, source_target_pairs={{0,16},{4,20},{8,24},{12,28},{16,0},{20,4},{24,8},{28,12},{1,17},{... | collective-permute-start | bytes 4325384 | tf_op jit(solution)/shard_map/ppermute | solution.py:577
  679.1 42.0 %collective-permute-start.8 = (bf16[256,1408]{1,0:T(8,128)(2,1)S(1)}, bf16[256,1408]{1,0:T(8,128)(2,1)S(1)}, u32[]{:S(2)}, u32[]{:S(2)}) collective-permute-start(bf16[256,1408]{1,0:T(8,128)(2,1)S(1)} %copy-done.149), channel_id=1, source_target_pairs={{0,16},{4,20},{8,24},{12,28},{16,0},{20,4},{24,8},{28,12},{1,17},{... | collective-permute-start | bytes 2162696 | tf_op jit(solution)/shard_map/ppermute | solution.py:577
  680.1 40.9 %collective-permute-start.9 = (bf16[256,1408]{1,0:T(8,128)(2,1)S(1)}, bf16[256,1408]{1,0:T(8,128)(2,1)S(1)}, u32[]{:S(2)}, u32[]{:S(2)}) collective-permute-start(bf16[256,1408]{1,0:T(8,128)(2,1)S(1)} %copy-done.150), channel_id=1, source_target_pairs={{0,8},{4,12},{8,0},{12,4},{16,24},{20,28},{24,16},{28,20},{1,9},{5... | collective-permute-start | bytes 2162696 | tf_op jit(solution)/shard_map/ppermute | solution.py:577
  731.1 90.8 %collective-permute-start.13 = (bf16[256,1408]{1,0:T(8,128)(2,1)}, bf16[256,1408]{1,0:T(8,128)(2,1)}, u32[]{:S(2)}, u32[]{:S(2)}) collective-permute-start(bf16[256,1408]{1,0:T(8,128)(2,1)} %slice_bitcast_fusion.26), channel_id=1, source_target_pairs={{0,16},{4,20},{8,24},{12,28},{16,0},{20,4},{24,8},{28,12},{1,17},{... | collective-permute-start | bytes 2162696 | tf_op jit(solution)/shard_map/ppermute | solution.py:577
  732.1 116.3 %collective-permute-start.14 = (bf16[256,1408]{1,0:T(8,128)(2,1)}, bf16[256,1408]{1,0:T(8,128)(2,1)}, u32[]{:S(2)}, u32[]{:S(2)}) collective-permute-start(bf16[256,1408]{1,0:T(8,128)(2,1)} %slice_bitcast_fusion.25), channel_id=1, source_target_pairs={{0,8},{4,12},{8,0},{12,4},{16,24},{20,28},{24,16},{28,20},{1,9},{5... | collective-permute-start | bytes 2162696 | tf_op jit(solution)/shard_map/ppermute | solution.py:577
  733.4 134.4 %collective-permute-start.15 = (bf16[512,1408]{1,0:T(8,128)(2,1)}, bf16[512,1408]{1,0:T(8,128)(2,1)}, u32[]{:S(2)}, u32[]{:S(2)}) collective-permute-start(bf16[512,1408]{1,0:T(8,128)(2,1)} %bitcast.47), channel_id=1, source_target_pairs={{0,8},{4,12},{8,0},{12,4},{16,24},{20,28},{24,16},{28,20},{1,9},{5... | collective-permute-start | bytes 4325384 | tf_op jit(solution)/shard_map/ppermute | solution.py:577
  734.1 133.6 %collective-permute-start.16 = (bf16[512,1408]{1,0:T(8,128)(2,1)}, bf16[512,1408]{1,0:T(8,128)(2,1)}, u32[]{:S(2)}, u32[]{:S(2)}) collective-permute-start(bf16[512,1408]{1,0:T(8,128)(2,1)} %bitcast.48), channel_id=1, source_target_pairs={{0,16},{4,20},{8,24},{12,28},{16,0},{20,4},{24,8},{28,12},{1,17},{... | collective-permute-start | bytes 4325384 | tf_op jit(solution)/shard_map/ppermute | solution.py:577
  757.7 91.9 %collective-permute-start.12 = (bf16[2816,1024]{1,0:T(8,128)(2,1)}, bf16[2816,1024]{1,0:T(8,128)(2,1)}, u32[]{:S(2)}, u32[]{:S(2)}) collective-permute-start(bf16[2816,1024]{1,0:T(8,128)(2,1)} %convolution_convert_fusion.1), channel_id=1, source_target_pairs={{0,4},{4,0},{8,12},{12,8},{16,20},{20,16},{24,28},{28,24},{1,5},{5... | collective-permute-start | bytes 17301512 | tf_op jit(solution)/shard_map/ppermute | solution.py:577
  822.0 43.4 %collective-permute-start.17 = (bf16[128,2816]{1,0:T(8,128)(2,1)}, bf16[128,2816]{1,0:T(8,128)(2,1)S(1)}, u32[]{:S(2)}, u32[]{:S(2)}) collective-permute-start(bf16[128,2816]{1,0:T(8,128)(2,1)} %fusion.92), channel_id=1, source_target_pairs={{0,2},{1,3},{2,0},{3,1},{4,6},{5,7},{6,4},{7,5},{8,10},{9,11},{10,... | collective-permute-start | bytes 2162696 | tf_op jit(solution)/shard_map/ppermute | solution.py:577
  888.9 58.7 %collective-permute-start.20 = (bf16[2816,1024]{1,0:T(8,128)(2,1)}, bf16[2816,1024]{1,0:T(8,128)(2,1)}, u32[]{:S(2)}, u32[]{:S(2)}) collective-permute-start(bf16[2816,1024]{1,0:T(8,128)(2,1)} %convolution_convert_fusion), channel_id=1, source_target_pairs={{0,4},{4,0},{8,12},{12,8},{16,20},{20,16},{24,28},{28,24},{1,5},{5... | collective-permute-start | bytes 17301512 | tf_op jit(solution)/shard_map/ppermute | solution.py:577
  891.3 41.3 %collective-permute-start.26 = (bf16[64,2816]{1,0:T(8,128)(2,1)}, bf16[64,2816]{1,0:T(8,128)(2,1)}, u32[]{:S(2)}, u32[]{:S(2)}) collective-permute-start(bf16[64,2816]{1,0:T(8,128)(2,1)} %constant_dynamic-slice_fusion.28), channel_id=1, source_target_pairs={{0,1},{1,0},{2,3},{3,2},{4,5},{5,4},{6,7},{7,6},{8,9},{9,8},{10,11... | collective-permute-start | bytes 1081352 | tf_op jit(solution)/shard_map/ppermute | solution.py:577
  911.9 34.9 %collective-permute-start.23 = (bf16[128,2816]{1,0:T(8,128)(2,1)}, bf16[128,2816]{1,0:T(8,128)(2,1)}, u32[]{:S(2)}, u32[]{:S(2)}) collective-permute-start(bf16[128,2816]{1,0:T(8,128)(2,1)} %fusion.90), channel_id=1, source_target_pairs={{0,2},{1,3},{2,0},{3,1},{4,6},{5,7},{6,4},{7,5},{8,10},{9,11},{10,... | collective-permute-start | bytes 2162696 | tf_op jit(solution)/shard_map/ppermute | solution.py:577
  912.3 80.4 %collective-permute-start.21 = (bf16[1408,512]{1,0:T(8,128)(2,1)}, bf16[1408,512]{1,0:T(8,128)(2,1)S(1)}, u32[]{:S(2)}, u32[]{:S(2)}) collective-permute-start(bf16[1408,512]{1,0:T(8,128)(2,1)} %bitcast.67), channel_id=1, source_target_pairs={{0,8},{4,12},{8,0},{12,4},{16,24},{20,28},{24,16},{28,20},{1,9},{5... | collective-permute-start | bytes 4325384 | tf_op jit(solution)/shard_map/ppermute | solution.py:577
  913.5 79.2 %collective-permute-start.22 = (bf16[1408,512]{1,0:T(8,128)(2,1)}, bf16[1408,512]{1,0:T(8,128)(2,1)}, u32[]{:S(2)}, u32[]{:S(2)}) collective-permute-start(bf16[1408,512]{1,0:T(8,128)(2,1)} %bitcast.68), channel_id=1, source_target_pairs={{0,16},{4,20},{8,24},{12,28},{16,0},{20,4},{24,8},{28,12},{1,17},{... | collective-permute-start | bytes 4325384 | tf_op jit(solution)/shard_map/ppermute | solution.py:577
  932.6 33.4 %collective-permute-start.24 = (bf16[256,1408]{1,0:T(8,128)(2,1)}, bf16[256,1408]{1,0:T(8,128)(2,1)S(1)}, u32[]{:S(2)}, u32[]{:S(2)}) collective-permute-start(bf16[256,1408]{1,0:T(8,128)(2,1)} %slice_bitcast_fusion.20), channel_id=1, source_target_pairs={{0,16},{4,20},{8,24},{12,28},{16,0},{20,4},{24,8},{28,12},{1,17},{... | collective-permute-start | bytes 2162696 | tf_op jit(solution)/shard_map/ppermute | solution.py:577
  947.6 45.1 %collective-permute-start.27 = (bf16[128,2816]{1,0:T(8,128)(2,1)}, bf16[128,2816]{1,0:T(8,128)(2,1)S(1)}, u32[]{:S(2)}, u32[]{:S(2)}) collective-permute-start(bf16[128,2816]{1,0:T(8,128)(2,1)} %fusion.88), channel_id=1, source_target_pairs={{0,2},{1,3},{2,0},{3,1},{4,6},{5,7},{6,4},{7,5},{8,10},{9,11},{10,... | collective-permute-start | bytes 2162696 | tf_op jit(solution)/shard_map/ppermute | solution.py:577
  1009.8 25.3 %collective-permute-start.28 = (bf16[1024,2048]{1,0:T(8,128)(2,1)}, bf16[1024,2048]{1,0:T(8,128)(2,1)}, u32[]{:S(2)}, u32[]{:S(2)}) collective-permute-start(bf16[1024,2048]{1,0:T(8,128)(2,1)} %convolution_convert_fusion.7), channel_id=1, source_target_pairs={{0,4},{4,0},{8,12},{12,8},{16,20},{20,16},{24,28},{28,24},{1,5},{5... | collective-permute-start | bytes 12582920 | tf_op jit(solution)/shard_map/ppermute | solution.py:577
  1010.7 24.0 %collective-permute-start.35 = (bf16[64,2816]{1,0:T(8,128)(2,1)S(1)}, bf16[64,2816]{1,0:T(8,128)(2,1)}, u32[]{:S(2)}, u32[]{:S(2)}) collective-permute-start(bf16[64,2816]{1,0:T(8,128)(2,1)S(1)} %constant_dynamic-slice_fusion.18), channel_id=1, source_target_pairs={{0,1},{1,0},{2,3},{3,2},{4,5},{5,4},{6,7},{7,6},{8,9},{9,8},{10,11... | collective-permute-start | bytes 1081352 | tf_op jit(solution)/shard_map/ppermute | solution.py:577
  1011.9 51.0 %collective-permute-start.31 = (bf16[704,512]{1,0:T(8,128)(2,1)}, bf16[704,512]{1,0:T(8,128)(2,1)S(1)}, u32[]{:S(2)}, u32[]{:S(2)}) collective-permute-start(bf16[704,512]{1,0:T(8,128)(2,1)} %slice_bitcast_fusion.17), channel_id=1, source_target_pairs={{0,16},{4,20},{8,24},{12,28},{16,0},{20,4},{24,8},{28,12},{1,17},{... | collective-permute-start | bytes 2162696 | tf_op jit(solution)/shard_map/ppermute | solution.py:577
  1012.2 50.6 %collective-permute-start.32 = (bf16[704,512]{1,0:T(8,128)(2,1)}, bf16[704,512]{1,0:T(8,128)(2,1)S(1)}, u32[]{:S(2)}, u32[]{:S(2)}) collective-permute-start(bf16[704,512]{1,0:T(8,128)(2,1)} %slice_bitcast_fusion.16), channel_id=1, source_target_pairs={{0,8},{4,12},{8,0},{12,4},{16,24},{20,28},{24,16},{28,20},{1,9},{5... | collective-permute-start | bytes 2162696 | tf_op jit(solution)/shard_map/ppermute | solution.py:577
  1021.4 41.5 %collective-permute-start.34 = (bf16[128,2816]{1,0:T(8,128)(2,1)}, bf16[128,2816]{1,0:T(8,128)(2,1)S(1)}, u32[]{:S(2)}, u32[]{:S(2)}) collective-permute-start(bf16[128,2816]{1,0:T(8,128)(2,1)} %fusion.86), channel_id=1, source_target_pairs={{0,2},{1,3},{2,0},{3,1},{4,6},{5,7},{6,4},{7,5},{8,10},{9,11},{10,... | collective-permute-start | bytes 2162696 | tf_op jit(solution)/shard_map/ppermute | solution.py:577
  1034.8 33.4 %collective-permute-start.29 = (bf16[1408,512]{1,0:T(8,128)(2,1)}, bf16[1408,512]{1,0:T(8,128)(2,1)S(1)}, u32[]{:S(2)}, u32[]{:S(2)}) collective-permute-start(bf16[1408,512]{1,0:T(8,128)(2,1)} %bitcast.463), channel_id=1, source_target_pairs={{0,8},{4,12},{8,0},{12,4},{16,24},{20,28},{24,16},{28,20},{1,9},{5... | collective-permute-start | bytes 4325384 | tf_op jit(solution)/shard_map/ppermute | solution.py:577
  1035.1 33.1 %collective-permute-start.30 = (bf16[1408,512]{1,0:T(8,128)(2,1)}, bf16[1408,512]{1,0:T(8,128)(2,1)S(1)}, u32[]{:S(2)}, u32[]{:S(2)}) collective-permute-start(bf16[1408,512]{1,0:T(8,128)(2,1)} %bitcast.462), channel_id=1, source_target_pairs={{0,16},{4,20},{8,24},{12,28},{16,0},{20,4},{24,8},{28,12},{1,17},{... | collective-permute-start | bytes 4325384 | tf_op jit(solution)/shard_map/ppermute | solution.py:577
  1088.8 57.0 %collective-permute-start.38 = (bf16[4,128,512]{2,1,0:T(8,128)(2,1)S(1)}, bf16[4,128,512]{2,1,0:T(8,128)(2,1)S(1)}, u32[]{:S(2)}, u32[]{:S(2)}) collective-permute-start(bf16[4,128,512]{2,1,0:T(8,128)(2,1)S(1)} %fusion.49), channel_id=1, source_target_pairs={{1,0},{2,1},{3,2},{5,4},{6,5},{7,6},{9,8},{10,9},{11,10},{13,12},{... | collective-permute-start | bytes 1572872 | tf_op jit(solution)/shard_map/ppermute | solution.py:213
  1152.8 30.1 %collective-permute-start.39 = (bf16[1024,2560]{1,0:T(8,128)(2,1)}, bf16[1024,2560]{1,0:T(8,128)(2,1)}, u32[]{:S(2)}, u32[]{:S(2)}) collective-permute-start(bf16[1024,2560]{1,0:T(8,128)(2,1)} %convolution_convert_fusion.6), channel_id=1, source_target_pairs={{0,4},{4,0},{8,12},{12,8},{16,20},{20,16},{24,28},{28,24},{1,5},{5... | collective-permute-start | bytes 15728648 | tf_op jit(solution)/shard_map/ppermute | solution.py:577
  1155.7 25.1 %collective-permute-start.46 = (bf16[64,2816]{1,0:T(8,128)(2,1)}, bf16[64,2816]{1,0:T(8,128)(2,1)}, u32[]{:S(2)}, u32[]{:S(2)}) collective-permute-start(bf16[64,2816]{1,0:T(8,128)(2,1)} %constant_dynamic-slice_fusion.17), channel_id=1, source_target_pairs={{0,1},{1,0},{2,3},{3,2},{4,5},{5,4},{6,7},{7,6},{8,9},{9,8},{10,11... | collective-permute-start | bytes 1081352 | tf_op jit(solution)/shard_map/ppermute | solution.py:577
  1157.7 33.2 %collective-permute-start.43 = (bf16[704,512]{1,0:T(8,128)(2,1)}, bf16[704,512]{1,0:T(8,128)(2,1)}, u32[]{:S(2)}, u32[]{:S(2)}) collective-permute-start(bf16[704,512]{1,0:T(8,128)(2,1)} %slice_bitcast_fusion.14), channel_id=1, source_target_pairs={{0,16},{4,20},{8,24},{12,28},{16,0},{20,4},{24,8},{28,12},{1,17},{... | collective-permute-start | bytes 2162696 | tf_op jit(solution)/shard_map/ppermute | solution.py:577
  1159.3 58.1 %collective-permute-start.41 = (bf16[512,1024]{1,0:T(8,128)(2,1)}, bf16[512,1024]{1,0:T(8,128)(2,1)}, u32[]{:S(2)}, u32[]{:S(2)}) collective-permute-start(bf16[512,1024]{1,0:T(8,128)(2,1)} %bitcast.94), channel_id=1, source_target_pairs={{0,8},{4,12},{8,0},{12,4},{16,24},{20,28},{24,16},{28,20},{1,9},{5... | collective-permute-start | bytes 3145736 | tf_op jit(solution)/shard_map/ppermute | solution.py:577
  1180.6 36.9 %collective-permute-start.42 = (bf16[512,1024]{1,0:T(8,128)(2,1)}, bf16[512,1024]{1,0:T(8,128)(2,1)S(1)}, u32[]{:S(2)}, u32[]{:S(2)}) collective-permute-start(bf16[512,1024]{1,0:T(8,128)(2,1)} %bitcast.476), channel_id=1, source_target_pairs={{0,16},{4,20},{8,24},{12,28},{16,0},{20,4},{24,8},{28,12},{1,17},{... | collective-permute-start | bytes 3145736 | tf_op jit(solution)/shard_map/ppermute | solution.py:577
  1182.9 34.5 %collective-permute-start.45 = (bf16[352,1024]{1,0:T(8,128)(2,1)}, bf16[352,1024]{1,0:T(8,128)(2,1)S(1)}, u32[]{:S(2)}, u32[]{:S(2)}) collective-permute-start(bf16[352,1024]{1,0:T(8,128)(2,1)} %fusion.84), channel_id=1, source_target_pairs={{0,2},{1,3},{2,0},{3,1},{4,6},{5,7},{6,4},{7,5},{8,10},{9,11},{10,... | collective-permute-start | bytes 2162696 | tf_op jit(solution)/shard_map/ppermute | solution.py:577
  1231.5 42.7 %collective-permute-start.47 = (bf16[512,1280]{1,0:T(8,128)(2,1)S(1)}, bf16[512,1280]{1,0:T(8,128)(2,1)S(1)}, u32[]{:S(2)}, u32[]{:S(2)}) collective-permute-start(bf16[512,1280]{1,0:T(8,128)(2,1)S(1)} %bitcast.473), channel_id=1, source_target_pairs={{0,8},{4,12},{8,0},{12,4},{16,24},{20,28},{24,16},{28,20},{1,9},{5... | collective-permute-start | bytes 3932168 | tf_op jit(solution)/shard_map/ppermute | solution.py:577
  1233.1 42.1 %collective-permute-start.48 = (bf16[512,1280]{1,0:T(8,128)(2,1)}, bf16[512,1280]{1,0:T(8,128)(2,1)}, u32[]{:S(2)}, u32[]{:S(2)}) collective-permute-start(bf16[512,1280]{1,0:T(8,128)(2,1)} %bitcast.127), channel_id=1, source_target_pairs={{0,16},{4,20},{8,24},{12,28},{16,0},{20,4},{24,8},{28,12},{1,17},{... | collective-permute-start | bytes 3932168 | tf_op jit(solution)/shard_map/ppermute | solution.py:577
  1237.4 36.7 %collective-permute-start.51 = (bf16[256,1024]{1,0:T(8,128)(2,1)S(1)}, bf16[256,1024]{1,0:T(8,128)(2,1)S(1)}, u32[]{:S(2)}, u32[]{:S(2)}) collective-permute-start(bf16[256,1024]{1,0:T(8,128)(2,1)S(1)} %slice_bitcast_fusion.34), channel_id=1, source_target_pairs={{0,16},{4,20},{8,24},{12,28},{16,0},{20,4},{24,8},{28,12},{1,17},{... | collective-permute-start | bytes 1572872 | tf_op jit(solution)/shard_map/ppermute | solution.py:577
  1239.1 35.1 %collective-permute-start.52 = (bf16[256,1024]{1,0:T(8,128)(2,1)S(1)}, bf16[256,1024]{1,0:T(8,128)(2,1)S(1)}, u32[]{:S(2)}, u32[]{:S(2)}) collective-permute-start(bf16[256,1024]{1,0:T(8,128)(2,1)S(1)} %slice_bitcast_fusion.33), channel_id=1, source_target_pairs={{0,8},{4,12},{8,0},{12,4},{16,24},{20,28},{24,16},{28,20},{1,9},{5... | collective-permute-start | bytes 1572872 | tf_op jit(solution)/shard_map/ppermute | solution.py:577
  1241.1 33.1 %collective-permute-start.53 = (bf16[352,1024]{1,0:T(8,128)(2,1)S(1)}, bf16[352,1024]{1,0:T(8,128)(2,1)S(1)}, u32[]{:S(2)}, u32[]{:S(2)}) collective-permute-start(bf16[352,1024]{1,0:T(8,128)(2,1)S(1)} %fusion.82), channel_id=1, source_target_pairs={{0,2},{1,3},{2,0},{3,1},{4,6},{5,7},{6,4},{7,5},{8,10},{9,11},{10,... | collective-permute-start | bytes 2162696 | tf_op jit(solution)/shard_map/ppermute | solution.py:577
  1283.2 24.6 %collective-permute-start.58 = (f32[4,64]{1,0:T(4,128)}, f32[4,64]{1,0:T(4,128)S(1)}, u32[]{:S(2)}, u32[]{:S(2)}) collective-permute-start(f32[4,64]{1,0:T(4,128)} %slice_bitcast_fusion.38), channel_id=1, source_target_pairs={{0,8},{4,12},{8,0},{12,4},{16,24},{20,28},{24,16},{28,20},{1,9},{5... | collective-permute-start | bytes 3080 | tf_op jit(solution)/shard_map/ppermute | solution.py:577
  1284.5 23.4 %collective-permute-start.60 = (bf16[176,1024]{1,0:T(8,128)(2,1)S(1)}, bf16[176,1024]{1,0:T(8,128)(2,1)}, u32[]{:S(2)}, u32[]{:S(2)}) collective-permute-start(bf16[176,1024]{1,0:T(8,128)(2,1)S(1)} %constant_dynamic-slice_fusion.7), channel_id=1, source_target_pairs={{0,1},{1,0},{2,3},{3,2},{4,5},{5,4},{6,7},{7,6},{8,9},{9,8},{10,11... | collective-permute-start | bytes 1081352 | tf_op jit(solution)/shard_map/ppermute | solution.py:577
  1285.4 25.3 %collective-permute-start.59 = (bf16[128,2048]{1,0:T(8,128)(2,1)}, bf16[128,2048]{1,0:T(8,128)(2,1)}, u32[]{:S(2)}, u32[]{:S(2)}) collective-permute-start(bf16[128,2048]{1,0:T(8,128)(2,1)} %fusion.102), channel_id=1, source_target_pairs={{0,2},{1,3},{2,0},{3,1},{4,6},{5,7},{6,4},{7,5},{8,10},{9,11},{10,... | collective-permute-start | bytes 1572872 | tf_op jit(solution)/shard_map/ppermute | solution.py:577
  1287.9 22.8 %collective-permute-start.55 = (bf16[256,1280]{1,0:T(8,128)(2,1)}, bf16[256,1280]{1,0:T(8,128)(2,1)}, u32[]{:S(2)}, u32[]{:S(2)}) collective-permute-start(bf16[256,1280]{1,0:T(8,128)(2,1)} %slice_bitcast_fusion.31), channel_id=1, source_target_pairs={{0,16},{4,20},{8,24},{12,28},{16,0},{20,4},{24,8},{28,12},{1,17},{... | collective-permute-start | bytes 1966088 | tf_op jit(solution)/shard_map/ppermute | solution.py:577
  1289.6 21.2 %collective-permute-start.56 = (bf16[256,1280]{1,0:T(8,128)(2,1)S(1)}, bf16[256,1280]{1,0:T(8,128)(2,1)}, u32[]{:S(2)}, u32[]{:S(2)}) collective-permute-start(bf16[256,1280]{1,0:T(8,128)(2,1)S(1)} %slice_bitcast_fusion.30), channel_id=1, source_target_pairs={{0,8},{4,12},{8,0},{12,4},{16,24},{20,28},{24,16},{28,20},{1,9},{5... | collective-permute-start | bytes 1966088 | tf_op jit(solution)/shard_map/ppermute | solution.py:577
  1314.8 29.4 %collective-permute-start.61 = (bf16[128,2560]{1,0:T(8,128)(2,1)S(1)}, bf16[128,2560]{1,0:T(8,128)(2,1)S(1)}, u32[]{:S(2)}, u32[]{:S(2)}) collective-permute-start(bf16[128,2560]{1,0:T(8,128)(2,1)S(1)} %fusion.95), channel_id=1, source_target_pairs={{0,2},{1,3},{2,0},{3,1},{4,6},{5,7},{6,4},{7,5},{8,10},{9,11},{10,... | collective-permute-start | bytes 1966088 | tf_op jit(solution)/shard_map/ppermute | solution.py:577
  1315.6 28.5 %collective-permute-start.63 = (bf16[64,2048]{1,0:T(8,128)(2,1)S(1)}, bf16[64,2048]{1,0:T(8,128)(2,1)S(1)}, u32[]{:S(2)}, u32[]{:S(2)}) collective-permute-start(bf16[64,2048]{1,0:T(8,128)(2,1)S(1)} %constant_dynamic-slice_fusion.5), channel_id=1, source_target_pairs={{0,1},{1,0},{2,3},{3,2},{4,5},{5,4},{6,7},{7,6},{8,9},{9,8},{10,11... | collective-permute-start | bytes 786440 | tf_op jit(solution)/shard_map/ppermute | solution.py:577
  1321.7 22.4 %collective-permute-start.62 = (f32[2,128]{1,0:T(2,128)S(1)}, f32[2,128]{1,0:T(2,128)S(1)}, u32[]{:S(2)}, u32[]{:S(2)}) collective-permute-start(f32[2,128]{1,0:T(2,128)S(1)} %constant_dynamic-slice_fusion.6), channel_id=1, source_target_pairs={{0,2},{1,3},{2,0},{3,1},{4,6},{5,7},{6,4},{7,5},{8,10},{9,11},{10,... | collective-permute-start | bytes 3080 | tf_op jit(solution)/shard_map/ppermute | solution.py:577
  (213 other events, 2534.1 us)

commit v3 on v1

v3 whole, which is shorter than its diff:
```python
import functools

import jax
import jax.numpy as jnp
from jax import lax
from jax.experimental import pallas as pl
from jax.experimental.pallas import tpu as pltpu
from jax.sharding import PartitionSpec as P

HEADS = 32
KV_HEADS = 4
HD = 64
FF = 5632
STEP = 10


NORM_EPS = 1e-05
ROPE_BASE = 10000.0
CLIP_NORM = 1.0
BETA_ONE = 0.9
BETA_TWO = 0.999
ADAM_EPS = 1e-08
WEIGHT_DECAY = 0.1
MASKED = -1e30


def matmul(left, right):
    return jnp.dot(left, right, preferred_element_type=jnp.float32)


def contract(left, right, left_dim, right_dim):
    return lax.dot_general(
        left, right, (((left_dim,), (right_dim,)), ((), ())), preferred_element_type=jnp.float32
    )


def rope_tables(positions):
    half_dim = HD // 2
    inverse = jnp.exp(-(2.0 * jnp.arange(half_dim, dtype=jnp.float32) / HD) * jnp.log(ROPE_BASE))
    angles = inverse[:, None] * positions.astype(jnp.float32)[None, :]
    return (jnp.cos(angles), jnp.sin(angles))


def rotate(rows, cos_table, sin_table):
    tokens = rows.shape[1]
    split = rows.reshape(-1, 2, HD // 2, tokens)
    first, second = (split[:, 0], split[:, 1])
    return jnp.stack(
        [first * cos_table - second * sin_table, second * cos_table + first * sin_table], 1
    ).reshape(rows.shape)


def norm_forward(rows_in, gain_row):
    inv_rms = lax.rsqrt(jnp.mean(rows_in * rows_in, axis=-1, keepdims=True) + NORM_EPS)
    return (inv_rms, rows_in * inv_rms * gain_row)


def norm_backward(rows_in, inv_rms, gain_row, gradient):
    weighted = gain_row * gradient
    back_rows = inv_rms * weighted - rows_in * inv_rms**3 * jnp.mean(
        weighted * rows_in, axis=-1, keepdims=True
    )
    return (back_rows, jnp.sum(gradient * rows_in * inv_rms, axis=0))


LOG2E = 1.4426950408889634
SCORE_SCALE = HD ** (-0.5)
SHARE = HEADS // KV_HEADS


def transposed(block):
    return block.astype(jnp.float32).T.astype(block.dtype)


def causal(tokens, valid):
    key_ids = lax.broadcasted_iota(jnp.int32, (tokens, tokens), 0)
    row_ids = lax.broadcasted_iota(jnp.int32, (tokens, tokens), 1)
    return (key_ids == row_ids) | ((key_ids < row_ids) & (valid > 0))


def attend_head(head, blocks, reach, valid, q_ref, kv_ref, group, k_rows, o_ref, full_ref, lse_ref):
    tokens = q_ref.shape[1]
    rows = pl.ds(pl.multiple_of(head * HD, HD), HD)
    query = q_ref[rows, :]

    def scores_of(dist):
        return matmul(k_rows[dist], query) * (SCORE_SCALE * LOG2E)

    def values_of(dist):
        return kv_ref[dist, group, HD:, :]

    scores = jnp.where(causal(tokens, valid), scores_of(0), MASKED)
    top = jnp.max(scores, 0, keepdims=True)
    weights = jnp.exp2(scores - top)
    total = jnp.sum(weights, 0, keepdims=True)
    acc = matmul(values_of(0), weights.astype(jnp.bfloat16))

    def step(dist, carry):
        top, total, acc = carry
        scores = jnp.where(dist < reach, scores_of(dist), MASKED)
        new_top = jnp.maximum(top, jnp.max(scores, 0, keepdims=True))
        weights = jnp.exp2(scores - new_top)
        fade = jnp.exp2(top - new_top)
        total = total * fade + jnp.sum(weights, 0, keepdims=True)
        acc = acc * fade + matmul(values_of(dist), weights.astype(jnp.bfloat16))
        return (new_top, total, acc)

    top, total, acc = lax.fori_loop(1, blocks, step, (top, total, acc))
    out = acc / total
    o_ref[rows, :] = out.astype(jnp.bfloat16)
    full_ref[rows, :] = out
    lse_ref[head] = top + jnp.log2(total)


def sum_to_owner(parts):
    size = lax.axis_size("seq")
    total = parts[size - 1]
    for step in range(size - 1, 0, -1):
        total = parts[step - 1] + lax.ppermute(
            total.astype(jnp.bfloat16), "seq", [(i, i - 1) for i in range(step, size)]
        ).astype(jnp.float32)
    return total


def adam_update(weight, first_mom, second_mom, gradient, clip_factor, rate, decay):
    step_grad = gradient * clip_factor
    first_new = BETA_ONE * first_mom + (1.0 - BETA_ONE) * step_grad
    second_new = BETA_TWO * second_mom + (1.0 - BETA_TWO) * step_grad * step_grad
    mean_hat = first_new / (1.0 - BETA_ONE**STEP)
    square_hat = second_new / (1.0 - BETA_TWO**STEP)
    weight_new = weight - rate * (mean_hat / (jnp.sqrt(square_hat) + ADAM_EPS) + decay * weight)
    return (weight_new, first_new, second_new)


MESH = pl.DeviceIdType.MESH


def flipped(index, bit):
    return index + (1 << bit) * (1 - 2 * ((index // (1 << bit)) % 2))


WHOLE, ROWS, BLOCKS = range(3)


class Gather:
    ahead = 3

    def __init__(self, kinds, pieces, shards, fulls, local_sems, send_sems, recv_sems):
        self.kinds, self.pieces, self.shards, self.fulls = (kinds, pieces, shards, fulls)
        self.local_sems, self.send_sems, self.recv_sems = (local_sems, send_sems, recv_sems)
        self.dp, self.seq = (lax.axis_index("dp"), lax.axis_index("seq"))
        self.dp_size, self.seq_size = (lax.axis_size("dp"), lax.axis_size("seq"))
        self.bits = self.dp_size.bit_length() - 1
        up = list(range(1, self.bits))
        self.orders = (up + [0], up[::-1] + [0])
        self.started = []
        self.done = set()

    def along(self, step):
        return {"seq": lax.rem(self.seq + step, self.seq_size)}

    def across(self, bit):
        return {"dp": flipped(self.dp, bit)}

    def sides(self, piece):
        return range(len(self.pieces[piece][2]))

    def kind(self, piece):
        return self.kinds[self.pieces[piece][0]]

    def source(self, piece, side):
        shard, _, sides = self.pieces[piece]
        return self.shards[shard].at[:, pl.ds(sides[side][0], sides[side][2])]

    def target(self, piece, side, index, depth):
        _, result, sides = self.pieces[piece]
        rows = pl.ds(pl.multiple_of(index * depth, depth), depth)
        return self.fulls[result].at[rows, pl.ds(sides[side][1], sides[side][2])]

    def own_target(self, piece, side):
        index = {
            WHOLE: self.dp * self.seq_size + self.seq, ROWS: self.seq, BLOCKS: self.dp
        }[self.kind(piece)]
        return self.target(piece, side, index, self.shards[self.pieces[piece][0]].shape[0])

    def local_copy(self, piece, side):
        return pltpu.make_async_copy(
            self.source(piece, side), self.own_target(piece, side), self.local_sems.at[piece, side]
        )

    def seq_copy(self, piece, side, step):
        return pltpu.make_async_remote_copy(
            src_ref=self.source(piece, side),
            dst_ref=self.own_target(piece, side),
            send_sem=self.send_sems.at[piece, side, self.dp_size + step],
            recv_sem=self.recv_sems.at[piece, side, self.dp_size + step],
            device_id=self.along(step),
            device_id_type=MESH,
        )

    def block_copy(self, piece, side, held, bit):
        depth = self.fulls[self.pieces[piece][1]].shape[0] // self.dp_size
        owner = self.dp
        for position in range(self.bits):
            if held >> position & 1:
                owner = flipped(owner, position)
        target = self.target(piece, side, owner, depth)
        early = not held and self.kind(piece) == BLOCKS
        return pltpu.make_async_remote_copy(
            src_ref=self.source(piece, side) if early else target,
            dst_ref=target,
            send_sem=self.send_sems.at[piece, side, held | 1 << bit],
            recv_sem=self.recv_sems.at[piece, side, held | 1 << bit],
            device_id=self.across(bit),
            device_id_type=MESH,
        )

    def start(self, copy):
        copy.start()
        self.started.append(copy)

    def begin(self):
        for piece in range(len(self.pieces)):
            for side in self.sides(piece):
                self.local_copy(piece, side).start()
        for piece in range(min(self.ahead, len(self.pieces))):
            self.send_rows(piece)

    def send_rows(self, piece):
        if self.kind(piece) == BLOCKS:
            return
        for step in range(1, self.seq_size):
            for side in self.sides(piece):
                self.start(self.seq_copy(piece, side, step))

    def advance(self, piece, stage):
        if (piece, stage) in self.done:
            return
        self.done.add((piece, stage))
        kind = self.kind(piece)
        if stage and kind == ROWS:
            return
        for side in self.sides(piece):
            order = self.orders[side] if kind != ROWS else []
            if stage == 0:
                if kind == WHOLE:
                    self.local_copy(piece, side).wait()
                if kind != BLOCKS:
                    for step in range(1, self.seq_size):
                        self.seq_copy(piece, side, step).wait_recv()
                held = [0]
            else:
                reached = [0]
                for bit in order[: stage - 1]:
                    reached += [block | 1 << bit for block in reached]
                held = [block | 1 << order[stage - 1] for block in reached]
                for block in reached:
                    self.block_copy(piece, side, block, order[stage - 1]).wait_recv()
            for bit in order[stage:]:
                for block in held:
                    self.start(self.block_copy(piece, side, block, bit))
        if stage == 0 and piece + self.ahead < len(self.pieces):
            self.send_rows(piece + self.ahead)

    def finish(self):
        for turn in range(len(self.pieces) + self.bits):
            for piece in range(len(self.pieces)):
                if 0 <= turn - piece <= self.bits:
                    self.advance(piece, turn - piece)
        for piece in range(len(self.pieces)):
            if self.kind(piece) != WHOLE:
                for side in self.sides(piece):
                    self.local_copy(piece, side).wait()
        for copy in self.started:
            copy.wait_send()


def gather_scratch(pieces):
    slots = lax.axis_size("dp") + lax.axis_size("seq")
    return [
        pltpu.SemaphoreType.DMA((pieces, 2)),
        pltpu.SemaphoreType.DMA((pieces, 2, slots)),
        pltpu.SemaphoreType.DMA((pieces, 2, slots)),
    ]


def gather_kernel(kinds, pieces, *refs):
    count, sems = (len(kinds), len(refs) - 3)
    gather = Gather(kinds, pieces, refs[:count], refs[count:sems], *refs[sems:])
    greet()
    gather.begin()
    gather.finish()


def gather_all(kinds, shards, shapes, pieces, collective_id):
    hbm = pl.BlockSpec(memory_space=pl.ANY)
    return pl.pallas_call(
        functools.partial(gather_kernel, kinds, pieces),
        out_shape=[jax.ShapeDtypeStruct(shape, jnp.bfloat16) for shape in shapes],
        in_specs=[hbm] * len(shards),
        out_specs=[hbm] * len(shapes),
        scratch_shapes=gather_scratch(len(pieces)),
        compiler_params=pltpu.CompilerParams(collective_id=collective_id, has_side_effects=True),
        name="gather",
    )(*shards)


def attend_kernel(kinds, pieces, info, q_ref, kv_ref, *refs):
    count = len(kinds)
    shards = refs[:count]
    o_ref, full_ref, lse_ref, kv_all_ref = refs[count : count + 4]
    fulls = refs[count + 4 : -7]
    k_rows, slots, kv_send, kv_recv = refs[-7:-3]
    gather = Gather(kinds, pieces, shards, fulls, *refs[-3:])
    seq, seq_size = (gather.seq, gather.seq_size)
    reach, valid = (info[0], info[1])
    greet()

    def kv_copy(group, step):
        return pltpu.make_async_remote_copy(
            src_ref=kv_ref.at[group],
            dst_ref=slots.at[step, group],
            send_sem=kv_send.at[step, group],
            recv_sem=kv_recv.at[step, group],
            device_id=gather.along(step),
            device_id_type=MESH,
        )

    for group in range(KV_HEADS):
        for step in range(1, seq_size):

            @pl.when(seq + step < seq_size)
            def _():
                kv_copy(group, step).start()

    gather.begin()
    gather.advance(0, 0)
    slots[0] = kv_ref[...]
    beside = {1: [(0, 1)], 3: [(0, 2)], 5: [(1, 0)], 7: [(0, 3), (1, 1), (2, 0)]}
    for group in range(KV_HEADS):
        k_rows[0] = transposed(kv_ref[group, :HD, :])
        for step in range(1, seq_size):

            @pl.when(seq >= step)
            def _():
                kv_copy(group, step).wait_recv()
                k_rows[step] = transposed(slots[step, group, :HD, :])

        for part in range(2):

            @pl.loop(group * SHARE + part * SHARE // 2, group * SHARE + (part + 1) * SHARE // 2)
            def _(head):
                attend_head(
                    head, seq + 1, reach, valid, q_ref, slots, group, k_rows, o_ref, full_ref, lse_ref
                )

            for event in beside.get(group * 2 + part, []):
                gather.advance(*event)
    for step in range(seq_size):

        @pl.when(seq >= step)
        def _():
            kv_all_ref[step] = slots[step]

        @pl.when(seq < step)
        def _():
            kv_all_ref[step] = jnp.zeros_like(kv_ref)

    for group in range(KV_HEADS):
        for step in range(1, seq_size):

            @pl.when(seq + step < seq_size)
            def _():
                kv_copy(group, step).wait_send()

    gather.finish()


def attend_forward(info, query, kv, kinds, shards, shapes, pieces, collective_id):
    tokens = query.shape[1]
    seq_size = lax.axis_size("seq")
    count = len(shards)
    vmem = pl.BlockSpec(memory_space=pltpu.VMEM)
    hbm = pl.BlockSpec(memory_space=pl.ANY)
    out = pl.pallas_call(
        functools.partial(attend_kernel, kinds, pieces),
        out_shape=[
            jax.ShapeDtypeStruct(query.shape, jnp.bfloat16),
            jax.ShapeDtypeStruct(query.shape, jnp.float32),
            jax.ShapeDtypeStruct((HEADS, 1, tokens), jnp.float32),
            jax.ShapeDtypeStruct((seq_size, *kv.shape), kv.dtype),
            *[jax.ShapeDtypeStruct(shape, jnp.bfloat16) for shape in shapes],
        ],
        in_specs=[pl.BlockSpec(memory_space=pltpu.SMEM), vmem, vmem] + [hbm] * count,
        out_specs=[vmem] * 4 + [hbm] * len(shapes),
        scratch_shapes=[
            pltpu.VMEM((seq_size, tokens, HD), jnp.bfloat16),
            pltpu.VMEM((seq_size, *kv.shape), kv.dtype),
            pltpu.SemaphoreType.DMA((seq_size, KV_HEADS)),
            pltpu.SemaphoreType.DMA((seq_size, KV_HEADS)),
            *gather_scratch(len(pieces)),
        ],
        compiler_params=pltpu.CompilerParams(
            collective_id=collective_id, has_side_effects=True, vmem_limit_bytes=48 * 2**20
        ),
        name="attend_forward",
    )(info, query, kv, *shards)
    return (out[:4], out[4:])


def squares_of(value):
    return jnp.sum((value * value).reshape(-1, 8, 128), 0)


def apart(index, distance, bits):
    return sum(
        lax.rem(index // (1 << bit) + distance // (1 << bit), 2) * (1 << bit) for bit in range(bits)
    )


class Scatter:
    def __init__(self, tiles, shape, refs, deliver):
        self.tiles, (self.size, self.depth, self.columns) = (tiles, shape)
        self.half = self.columns // 2
        self.deliver = deliver
        self.dp, self.seq = (lax.axis_index("dp"), lax.axis_index("seq"))
        self.dp_size, self.seq_size = (lax.axis_size("dp"), lax.axis_size("seq"))
        self.hops = self.size.bit_length() - 1
        refs = list(refs)
        self.own, self.other, self.came = (refs.pop(0), refs.pop(0), refs.pop(0))
        self.sent, self.got, self.kept = ([None], [None], [None])
        for _ in range(self.hops):
            self.sent.append(refs.pop(0))
            self.got.append(refs.pop(0))
            self.kept.append(refs.pop(0))
        self.rows, self.rows_got, self.send_sems, self.recv_sems = refs
        self.steps = tiles + self.hops + 2

    @staticmethod
    def scratch(shape):
        size, depth, columns = shape
        half = columns // 2
        hops = size.bit_length() - 1
        seq_size = lax.axis_size("seq")
        low = jnp.bfloat16
        shapes = [
            pltpu.VMEM((size, depth, columns), low),
            pltpu.VMEM((size, depth, columns), low),
            pltpu.VMEM((2, size, depth, columns), low),
        ]
        for hop in range(1, hops + 1):
            shapes.append(pltpu.VMEM((2, 2, size >> hop, depth, half), low))
            shapes.append(pltpu.VMEM((2, 2, size >> hop, depth, half), low))
            shapes.append(pltpu.VMEM((2, size >> hop, depth, half), low))
        shapes.append(pltpu.VMEM((2, 2, depth, half), low))
        shapes.append(pltpu.VMEM((2, seq_size - 1, 2, depth // seq_size, half), low))
        lanes = max(2, seq_size - 1)
        shapes.append(pltpu.SemaphoreType.DMA((hops + 2, 2, lanes)))
        shapes.append(pltpu.SemaphoreType.DMA((hops + 2, 2, lanes)))
        return shapes

    def bit(self, hop, side):
        return hop if side == 0 else self.hops + 1 - hop

    def copy(self, kind, slot, lane, src, dst, device):
        return pltpu.make_async_remote_copy(
            src_ref=src,
            dst_ref=dst,
            send_sem=self.send_sems.at[kind, slot, lane],
            recv_sem=self.recv_sems.at[kind, slot, lane],
            device_id=device,
            device_id_type=MESH,
        )

    def copies(self, kind, slot):
        if kind == 0:
            return [
                self.copy(0, slot, 0, self.other, self.came.at[slot], {"dp": flipped(self.dp, 0)})
            ]
        if kind <= self.hops:
            return [
                self.copy(
                    kind,
                    slot,
                    side,
                    self.sent[kind].at[slot, side],
                    self.got[kind].at[slot, side],
                    {"dp": flipped(self.dp, self.bit(kind, side))},
                )
                for side in range(2)
            ]
        own = self.depth // self.seq_size
        result = []
        for step in range(1, self.seq_size):
            there = lax.rem(self.seq + step, self.seq_size)
            window = pl.ds(pl.multiple_of(there * own, own), own)
            result.append(
                self.copy(
                    kind,
                    slot,
                    step - 1,
                    self.rows.at[slot, :, window, :],
                    self.rows_got.at[slot, step - 1],
                    {"seq": there},
                )
            )
        return result

    def send(self, kind, tile):
        for copy in self.copies(kind, lax.rem(tile, 2)):
            copy.start()

    def sent_before(self, kind, tile, back):
        @pl.when(tile >= back)
        def _():
            for copy in self.copies(kind, lax.rem(tile + 2 - back, 2)):
                copy.wait_send()

    def plus(self, into, one, two):
        rows = 64 if self.depth % 64 == 0 else 16

        @pl.loop(0, self.depth // rows)
        def _(chunk):
            part = pl.ds(pl.multiple_of(chunk * rows, rows), rows)
            into[part, :] = one[part, :] + two[part, :]

    def stage(self, kind, tile):
        slot = lax.rem(tile, 2)
        for copy in self.copies(kind, slot):
            copy.wait_recv()
        if kind == self.hops + 1:
            own = self.depth // self.seq_size
            window = pl.ds(pl.multiple_of(self.seq * own, own), own)
            for side in range(2):
                total = self.rows[slot, side, window, :].astype(jnp.float32)
                for step in range(self.seq_size - 1):
                    total = total + self.rows_got[slot, step, side].astype(jnp.float32)
                self.deliver(tile, side, total)
            return
        self.sent_before(kind + 1, tile, 2)
        size = self.size >> kind
        for side in range(2):
            columns = pl.ds(side * self.half, self.half)
            for block in range(size):
                if kind == 0:
                    one, two = (self.own.at[block, :, columns], self.came.at[slot, block, :, columns])
                else:
                    one, two = (self.kept[kind].at[side, block], self.got[kind].at[slot, side, block])
                if kind == self.hops:
                    into = self.rows.at[slot, side]
                elif side == 0:
                    place = self.sent if block % 2 else self.kept
                    index = (block // 2,)
                    into = place[kind + 1].at[((slot, 0) if block % 2 else (0,)) + index]
                else:
                    away = block >= size // 2
                    place = self.sent if away else self.kept
                    index = (block - size // 2 if away else block,)
                    into = place[kind + 1].at[((slot, 1) if away else (1,)) + index]
                self.plus(into, one, two)
        self.send(kind + 1, tile)

    def step(self, now, begin):
        for kind in range(self.hops + 1, -1, -1):
            tile = now - kind - 1

            @pl.when((tile >= 0) & (tile < self.tiles))
            def _():
                self.stage(kind, tile)

        @pl.when((now >= 0) & (now < self.tiles))
        def _():
            self.sent_before(0, now, 1)
            begin(now)

    def finish(self):
        for kind in range(self.hops + 2):
            for tile in range(max(0, self.tiles - (1 if kind == 0 else 2)), self.tiles):
                for copy in self.copies(kind, tile % 2):
                    copy.wait_send()


def greet():
    dp, seq = (lax.axis_index("dp"), lax.axis_index("seq"))
    dp_size, seq_size = (lax.axis_size("dp"), lax.axis_size("seq"))
    barrier = pltpu.get_barrier_semaphore()
    others = [{"seq": lax.rem(seq + step, seq_size)} for step in range(1, seq_size)]
    others += [{"dp": flipped(dp, bit)} for bit in range(dp_size.bit_length() - 1)]
    for other in others:
        pl.semaphore_signal(barrier, inc=1, device_id=other, device_id_type=MESH)
    pl.semaphore_wait(barrier, len(others))


TILE = 512


def mlp_kernel(
    rows_ref, turned_ref, grad_hbm, gu_ref, down_ref,
    down_grad, inner_hbm, out_hbm, sum_ref,
    grad_ref, gu_buf, down_buf, hidden, d_gu, product, inner_ref, out_ref,
    load_sems, store_sems, *scratch
):
    tokens, model = rows_ref.shape
    tiles = FF // TILE
    size, depth, columns = scratch[0].shape

    def deliver(tile, side, total):
        sum_ref[:, pl.ds(pl.multiple_of(side * FF + tile * TILE, TILE), TILE)] = total

    scatter = Scatter(tiles, (size, depth, columns), scratch, deliver)
    bits = scatter.hops + 1

    def loads(tile, slot):
        start = pl.multiple_of(tile * TILE, TILE)
        return [
            pltpu.make_async_copy(
                gu_ref.at[:, pl.ds(start, TILE)], gu_buf.at[slot, 0], load_sems.at[slot, 0]
            ),
            pltpu.make_async_copy(
                gu_ref.at[:, pl.ds(pl.multiple_of(FF + start, TILE), TILE)],
                gu_buf.at[slot, 1],
                load_sems.at[slot, 1],
            ),
            pltpu.make_async_copy(
                down_ref.at[pl.ds(start, TILE), :], down_buf.at[slot], load_sems.at[slot, 2]
            ),
        ]

    def store(tile):
        start = pl.multiple_of(tile * TILE, TILE)
        return pltpu.make_async_copy(
            product, down_grad.at[pl.ds(start, TILE), :], store_sems.at[0]
        )

    grad_load = pltpu.make_async_copy(grad_hbm, grad_ref, store_sems.at[1])
    inner_store = pltpu.make_async_copy(inner_ref, inner_hbm, store_sems.at[2])
    out_store = pltpu.make_async_copy(out_ref, out_hbm, store_sems.at[3])
    grad_load.start()
    for copy in loads(0, 0):
        copy.start()
    inner_ref[...] = jnp.zeros_like(inner_ref)
    out_ref[...] = jnp.zeros_like(out_ref)
    greet()
    grad_load.wait()

    def begin(tile):
        slot = lax.rem(tile, 2)
        for copy in loads(tile, slot):
            copy.wait()

        @pl.when(tile + 1 < tiles)
        def _():
            for copy in loads(tile + 1, 1 - slot):
                copy.start()

        chunk_rows = min(256, tokens)

        @pl.loop(0, tokens // chunk_rows)
        def _(chunk):
            part = pl.ds(pl.multiple_of(chunk * chunk_rows, chunk_rows), chunk_rows)
            rows = rows_ref[part, :]
            gate = matmul(rows, gu_buf[slot, 0])
            up = matmul(rows, gu_buf[slot, 1])
            d_hidden = contract(grad_ref[part, :], down_buf[slot], 1, 1)
            sigmoid_gate = 1.0 / (1.0 + jnp.exp(-gate))
            silu = gate * sigmoid_gate
            hidden[part, :] = (silu * up).astype(jnp.bfloat16)
            d_gate = d_hidden * up * sigmoid_gate * (1.0 + gate * (1.0 - sigmoid_gate))
            d_gu[part, :TILE] = d_gate.astype(jnp.bfloat16)
            d_gu[part, TILE:] = (d_hidden * silu).astype(jnp.bfloat16)

        def blocks_of(core, into):
            @pl.loop(0, size)
            def _(block):
                owner = apart(scatter.dp, 2 * block + core, bits)
                part = pl.ds(pl.multiple_of(owner * depth, depth), depth)
                into[block] = matmul(turned_ref[part, :], d_gu[...]).astype(jnp.bfloat16)

        blocks_of(1, scatter.other)
        scatter.send(0, tile)
        blocks_of(0, scatter.own)

        @pl.when(tile >= 1)
        def _():
            store(tile - 1).wait()

        hidden_turned = transposed(hidden[...])

        @pl.loop(0, model // TILE)
        def _(chunk):
            part = pl.ds(pl.multiple_of(chunk * TILE, TILE), TILE)
            inner_ref[:, part] += contract(d_gu[:, :TILE], gu_buf[slot, 0, part, :], 1, 1) + contract(
                d_gu[:, TILE:], gu_buf[slot, 1, part, :], 1, 1
            )
            out_ref[:, part] += matmul(hidden[...], down_buf[slot, :, part])
            product[:, part] = matmul(hidden_turned, grad_ref[:, part]).astype(jnp.bfloat16)

        store(tile).start()

        @pl.when(tile == tiles - 1)
        def _():
            inner_store.start()
            out_store.start()

    @pl.loop(0, scatter.steps)
    def _(now):
        scatter.step(now, begin)

    store(tiles - 1).wait()
    inner_store.wait()
    out_store.wait()
    scatter.finish()


def feed_forward(rows, turned, grad, w_gu, w_down, collective_id):
    tokens, model = rows.shape
    dp_size, seq_size = (lax.axis_size("dp"), lax.axis_size("seq"))
    shape = (dp_size // 2, model // dp_size, 2 * TILE)
    vmem = pl.BlockSpec(memory_space=pltpu.VMEM)
    hbm = pl.BlockSpec(memory_space=pl.ANY)
    return pl.pallas_call(
        mlp_kernel,
        out_shape=[
            jax.ShapeDtypeStruct((FF, model), jnp.bfloat16),
            jax.ShapeDtypeStruct((tokens, model), jnp.float32),
            jax.ShapeDtypeStruct((tokens, model), jnp.float32),
            jax.ShapeDtypeStruct((model // (dp_size * seq_size), 2 * FF), jnp.float32),
        ],
        in_specs=[vmem, vmem, hbm, hbm, hbm],
        out_specs=[hbm, hbm, hbm, vmem],
        scratch_shapes=[
            pltpu.VMEM((tokens, model), jnp.bfloat16),
            pltpu.VMEM((2, 2, model, TILE), jnp.bfloat16),
            pltpu.VMEM((2, TILE, model), jnp.bfloat16),
            pltpu.VMEM((tokens, TILE), jnp.bfloat16),
            pltpu.VMEM((tokens, 2 * TILE), jnp.bfloat16),
            pltpu.VMEM((TILE, model), jnp.bfloat16),
            pltpu.VMEM((tokens, model), jnp.float32),
            pltpu.VMEM((tokens, model), jnp.float32),
            pltpu.SemaphoreType.DMA((2, 3)),
            pltpu.SemaphoreType.DMA((4,)),
            *Scatter.scratch(shape),
        ],
        compiler_params=pltpu.CompilerParams(
            collective_id=collective_id, has_side_effects=True, vmem_limit_bytes=60 * 2**20
        ),
        name="feed_forward",
    )(rows, turned, grad, w_gu, w_down)


def load_tile(scatter, source, load_sems):
    def copies(tile):
        columns = pl.ds(
            pl.multiple_of(tile * scatter.columns, scatter.columns), scatter.columns
        )
        result = []
        for block in range(2 * scatter.size):
            owner = apart(scatter.dp, block, scatter.hops + 1)
            into = scatter.other if block % 2 else scatter.own
            result.append(
                pltpu.make_async_copy(
                    source.at[owner, :, columns], into.at[block // 2], load_sems.at[block]
                )
            )
        return result

    def begin(tile):
        for copy in copies(tile):
            copy.start()

    def complete(now):
        @pl.when((now >= 0) & (now < scatter.tiles))
        def _():
            for copy in copies(now):
                copy.wait()
            scatter.send(0, now)

    return (begin, complete)


def delivered(ref, columns):
    def deliver(tile, side, total):
        start = pl.multiple_of(tile * columns + side * (columns // 2), columns // 2)
        ref[:, pl.ds(start, columns // 2)] = total

    return deliver


def backward_kernel(
    info, q_ref, kv_ref, full_ref, lse_ref, do_ref, down_ref, proj_ref,
    dq_ref, dkv_ref, down_sum, proj_sum,
    k_rows, v_rows, dk_acc, dv_acc, parts, parts_got, part_sends, part_recvs, load_sems, *scratch
):
    tokens = q_ref.shape[1]
    reach, valid = (info[0], info[1])
    count = len(scratch) // 2
    down = Scatter(
        down_ref.shape[2] // scratch[0].shape[2],
        scratch[0].shape,
        scratch[:count],
        delivered(down_sum, scratch[0].shape[2]),
    )
    proj = Scatter(
        proj_ref.shape[2] // scratch[count].shape[2],
        scratch[count].shape,
        scratch[count:],
        delivered(proj_sum, scratch[count].shape[2]),
    )
    seq, seq_size = (down.seq, down.seq_size)
    blocks = seq + 1
    greet()

    def part_copy(group, dist):
        return pltpu.make_async_remote_copy(
            src_ref=parts.at[dist, group],
            dst_ref=parts_got.at[dist, group],
            send_sem=part_sends.at[dist, group],
            recv_sem=part_recvs.at[dist, group],
            device_id={"seq": lax.rem(seq + seq_size - dist, seq_size)},
            device_id_type=MESH,
        )

    def one_head(head):
        group = head // SHARE
        rows = pl.ds(pl.multiple_of(head * HD, HD), HD)

        @pl.when(lax.rem(head, SHARE) == 0)
        def _():
            dk_acc[...] = jnp.zeros_like(dk_acc)
            dv_acc[...] = jnp.zeros_like(dv_acc)

            @pl.loop(0, blocks)
            def _(dist):
                k_rows[dist] = transposed(kv_ref[dist, group, :HD, :])
                v_rows[dist] = transposed(kv_ref[dist, group, HD:, :])

        query, grad = (q_ref[rows, :], do_ref[rows, :])
        query_rows, grad_rows = (transposed(query), transposed(grad))
        lse = lse_ref[head]
        centre = jnp.sum(grad.astype(jnp.float32) * full_ref[rows, :], 0, keepdims=True)

        def block(dist, mask):
            scores = matmul(k_rows[dist], query) * (SCORE_SCALE * LOG2E)
            prob = jnp.where(mask, jnp.exp2(scores - lse), 0.0)
            d_prob = matmul(v_rows[dist], grad)
            d_score = (prob * (d_prob - centre) * SCORE_SCALE).astype(jnp.bfloat16)
            dv_acc[dist] += matmul(prob.astype(jnp.bfloat16), grad_rows)
            dk_acc[dist] += matmul(d_score, query_rows)
            return matmul(kv_ref[dist, group, :HD, :], d_score)

        d_query = block(0, causal(tokens, valid))
        dq_ref[rows, :] = lax.fori_loop(
            1, blocks, lambda dist, acc: acc + block(dist, dist < reach), d_query
        )

        @pl.when(lax.rem(head, SHARE) == SHARE - 1)
        def _():
            dkv_ref[group, :HD, :] = dk_acc[0].T
            dkv_ref[group, HD:, :] = dv_acc[0].T
            for dist in range(1, seq_size):

                @pl.when(seq >= dist)
                def _():
                    parts[dist, group, :HD, :] = dk_acc[dist].T.astype(jnp.bfloat16)
                    parts[dist, group, HD:, :] = dv_acc[dist].T.astype(jnp.bfloat16)
                    part_copy(group, dist).start()

    begin_down, complete_down = load_tile(down, down_ref, load_sems.at[0])
    begin_proj, complete_proj = load_tile(proj, proj_ref, load_sems.at[1])
    steps = down.steps
    lag = steps - proj.steps

    @pl.loop(0, steps)
    def _(now):
        down.step(now, begin_down)
        proj.step(now - lag, begin_proj)
        complete_down(now)
        complete_proj(now - lag)

        @pl.loop(now * HEADS // steps, (now + 1) * HEADS // steps)
        def _(head):
            one_head(head)

    down.finish()
    proj.finish()
    for dist in range(1, seq_size):

        @pl.when(seq + dist < seq_size)
        def _():
            for group in range(KV_HEADS):
                part_copy(group, dist).wait_recv()
            dkv_ref[...] += parts_got[dist].astype(jnp.float32)

        @pl.when(seq >= dist)
        def _():
            for group in range(KV_HEADS):
                part_copy(group, dist).wait_send()


def attend_backward(info, query, kv, full, lse, grad, g_down, g_out, collective_id):
    tokens, reach = (query.shape[1], kv.shape[0])
    seq_size = lax.axis_size("seq")
    vmem = pl.BlockSpec(memory_space=pltpu.VMEM)
    hbm = pl.BlockSpec(memory_space=pl.ANY)
    down_shape = (g_down.shape[0] // 2, g_down.shape[1], 256)
    proj_shape = (g_out.shape[0] // 2, g_out.shape[1], 512)
    return pl.pallas_call(
        backward_kernel,
        out_shape=[
            jax.ShapeDtypeStruct(query.shape, jnp.float32),
            jax.ShapeDtypeStruct((KV_HEADS, 2 * HD, tokens), jnp.float32),
            jax.ShapeDtypeStruct((g_down.shape[1] // seq_size, g_down.shape[2]), jnp.float32),
            jax.ShapeDtypeStruct((g_out.shape[1] // seq_size, g_out.shape[2]), jnp.float32),
        ],
        in_specs=[pl.BlockSpec(memory_space=pltpu.SMEM)] + [vmem] * 5 + [hbm] * 2,
        out_specs=[vmem] * 4,
        scratch_shapes=[
            pltpu.VMEM((reach, tokens, HD), jnp.bfloat16),
            pltpu.VMEM((reach, tokens, HD), jnp.bfloat16),
            pltpu.VMEM((reach, tokens, HD), jnp.float32),
            pltpu.VMEM((reach, tokens, HD), jnp.float32),
            pltpu.VMEM((reach, KV_HEADS, 2 * HD, tokens), jnp.bfloat16),
            pltpu.VMEM((reach, KV_HEADS, 2 * HD, tokens), jnp.bfloat16),
            pltpu.SemaphoreType.DMA((reach, KV_HEADS)),
            pltpu.SemaphoreType.DMA((reach, KV_HEADS)),
            pltpu.SemaphoreType.DMA((2, g_down.shape[0])),
            *Scatter.scratch(down_shape),
            *Scatter.scratch(proj_shape),
        ],
        compiler_params=pltpu.CompilerParams(
            collective_id=collective_id, has_side_effects=True, vmem_limit_bytes=60 * 2**20
        ),
        name="attend_backward",
    )(info, query, kv, full, lse, grad, g_down, g_out)


def everyone():
    seq_size = lax.axis_size("seq")
    devices = lax.axis_size("dp") * seq_size
    me = lax.axis_index("dp") * seq_size + lax.axis_index("seq")

    def device(distance):
        other = lax.rem(me + distance, devices)
        return (other, (other // seq_size, lax.rem(other, seq_size)))

    return (me, devices, device)


def last_kernel(
    source, gains_ref, squares_ref,
    result, gains_sum, total_ref,
    load_sems, gains_got, mine, totals_got, tile_sends, tile_recvs, *scratch
):
    columns = scratch[0].shape[2]
    scatter = Scatter(
        source.shape[2] // columns, scratch[0].shape, scratch, delivered(result, columns)
    )
    me, devices, device = everyone()

    def copy(kind, distance):
        other, place = device(distance)
        return pltpu.make_async_remote_copy(
            src_ref=mine if kind else gains_ref.at[other],
            dst_ref=(totals_got if kind else gains_got).at[distance],
            send_sem=tile_sends.at[kind, distance],
            recv_sem=tile_recvs.at[kind, distance],
            device_id=place,
            device_id_type=MESH,
        )

    barrier = pltpu.get_barrier_semaphore()

    @pl.loop(1, devices)
    def _(distance):
        pl.semaphore_signal(barrier, inc=1, device_id=device(distance)[1], device_id_type=MESH)

    pl.semaphore_wait(barrier, devices - 1)

    @pl.loop(1, devices)
    def _(distance):
        copy(0, distance).start()

    begin, complete = load_tile(scatter, source, load_sems)

    @pl.loop(0, scatter.steps)
    def _(now):
        scatter.step(now, begin)
        complete(now)

    @pl.loop(1, devices)
    def _(distance):
        copy(0, distance).wait()

    gains = gains_ref[me] + jnp.sum(gains_got[1:], 0)
    gains_sum[...] = gains
    lanes = result.shape[1] // 128
    squares = squares_ref[...] + gains * gains
    for lane in range(lanes):
        block = result[:, lane * 128 : (lane + 1) * 128]
        squares = squares + jnp.sum((block * block).reshape(-1, 8, 128), 0)
    mine[...] = squares

    @pl.loop(1, devices)
    def _(distance):
        copy(1, distance).start()

    @pl.loop(1, devices)
    def _(distance):
        copy(1, distance).wait()

    total = jnp.sum(squares + jnp.sum(totals_got[1:], 0))
    total_ref[...] = jnp.full((8, 128), total, jnp.float32)
    scatter.finish()


def last_sums(parts, gains, squares, columns, collective_id):
    devices = gains.shape[0]
    shape = (parts.shape[0] // 2, parts.shape[1], columns)
    vmem = pl.BlockSpec(memory_space=pltpu.VMEM)
    return pl.pallas_call(
        last_kernel,
        out_shape=[
            jax.ShapeDtypeStruct(
                (parts.shape[1] // lax.axis_size("seq"), parts.shape[2]), jnp.float32
            ),
            jax.ShapeDtypeStruct((8, 128), jnp.float32),
            jax.ShapeDtypeStruct((8, 128), jnp.float32),
        ],
        in_specs=[pl.BlockSpec(memory_space=pl.ANY), vmem, vmem],
        out_specs=[vmem] * 3,
        scratch_shapes=[
            pltpu.SemaphoreType.DMA((parts.shape[0],)),
            pltpu.VMEM((devices, 8, 128), jnp.float32),
            pltpu.VMEM((8, 128), jnp.float32),
            pltpu.VMEM((devices, 8, 128), jnp.float32),
            pltpu.SemaphoreType.DMA((2, devices)),
            pltpu.SemaphoreType.DMA((2, devices)),
            *Scatter.scratch(shape),
        ],
        compiler_params=pltpu.CompilerParams(
            collective_id=collective_id, has_side_effects=True, vmem_limit_bytes=48 * 2**20
        ),
        name="last_sums",
    )(parts, gains, squares)


def per_device(
    hidden_in,
    out_grad,
    seq_lengths,
    seq_counts,
    segment_ids,
    qkv_weight,
    qkv_m,
    qkv_v,
    out_weight,
    out_m,
    out_v,
    gate_up_weight,
    gate_up_m,
    gate_up_v,
    down_weight,
    down_m,
    down_v,
    norm_gains,
    gain_m,
    gain_v,
):
    tok_dev = hidden_in.shape[0]
    q_width = HEADS * HD
    kv_width = KV_HEADS * HD
    seg_all = segment_ids[0]
    lengths = seq_lengths[0]
    seq_index = lax.axis_index("seq")
    offset = seq_index * tok_dev
    seg_local = lax.dynamic_slice_in_dim(seg_all, offset, tok_dev, 0)
    starts = jnp.cumsum(lengths, dtype=jnp.int32) - lengths
    slot_ids = jnp.arange(lengths.shape[0], dtype=jnp.int32)
    seq_start = jnp.sum(
        jnp.where(seg_local[:, None] == slot_ids[None, :], starts[None, :], 0),
        axis=1,
        dtype=jnp.int32,
    )
    positions = offset + jnp.arange(tok_dev, dtype=jnp.int32) - seq_start
    cos_table, sin_table = rope_tables(positions)
    valid = (seg_local[0] < seq_counts[0]).astype(jnp.int32)
    reach = jnp.where(valid > 0, seq_index - seq_start[0] // tok_dev + 1, 1)
    info = jnp.stack([reach, valid]).astype(jnp.int32)

    devices = lax.axis_size("dp") * lax.axis_size("seq")
    own = norm_gains.shape[1]
    gain_rows = jnp.pad(norm_gains.astype(jnp.bfloat16), ((0, 14), (0, 128 - own)))
    width = qkv_weight.shape[1] // 4
    model = out_weight.shape[1]
    seq_size = lax.axis_size("seq")
    gu_shard = gate_up_weight.astype(jnp.bfloat16)
    early = 3 * TILE
    w_qkv, gain_rows, gu_block = gather_all(
        [WHOLE, WHOLE, ROWS],
        [qkv_weight.astype(jnp.bfloat16), gain_rows, gu_shard],
        [
            (devices * qkv_weight.shape[0], 4 * width),
            (devices * 16, 128),
            (seq_size * gu_shard.shape[0], 2 * early),
        ],
        [
            (1, 1, ((0, 0, 128),)),
            (0, 0, ((0, 0, width), (width, width, width))),
            (0, 0, ((2 * width, 2 * width, width), (3 * width, 3 * width, width))),
            (2, 2, ((0, 0, early), (FF, early, early))),
        ],
        1,
    )
    w_gain = jnp.moveaxis(gain_rows.reshape(devices, 16, 128)[:, :2, :own], 1, 0).reshape(2, -1)
    gain_attn = w_gain[0].astype(jnp.float32)
    gain_mlp = w_gain[1].astype(jnp.float32)
    residual = hidden_in.astype(jnp.float32)
    inv_one, normed = norm_forward(residual, gain_attn)
    normed_low = normed.astype(jnp.bfloat16)
    qkv_out = contract(w_qkv, normed_low, 0, 1)
    query = rotate(qkv_out[:q_width], cos_table, sin_table).astype(jnp.bfloat16)
    key = rotate(qkv_out[q_width : q_width + kv_width], cos_table, sin_table).astype(jnp.bfloat16)
    value = qkv_out[q_width + kv_width :].astype(jnp.bfloat16)
    kv_own = jnp.concatenate(
        [key.reshape(KV_HEADS, HD, tok_dev), value.reshape(KV_HEADS, HD, tok_dev)], 1
    )
    down_depth = down_weight.shape[0]
    spare = -down_depth % 16
    shards = [
        out_weight.astype(jnp.bfloat16),
        jnp.pad(down_weight.astype(jnp.bfloat16), ((0, spare), (0, 0))),
        gu_shard,
        gu_block,
    ]
    shapes = [(devices * shard.shape[0], shard.shape[1]) for shard in shards[:3]]
    half, quarter = (model // 2, model // 4)
    pieces = [
        (3, 2, ((0, 0, early), (early, FF, early))),
        (0, 0, ((0, 0, half), (half, half, half))),
        (1, 1, ((0, 0, quarter), (quarter, quarter, quarter))),
        (1, 1, ((half, half, quarter), (half + quarter, half + quarter, quarter))),
    ]
    for low, high in ((3, 6), (6, 9), (9, 10), (10, 11)):
        low, high = (low * TILE, high * TILE)
        pieces.append((2, 2, ((low, low, high - low), (FF + low, FF + low, high - low))))
    (attended, attended_full, lse, kv_all), (w_out, w_down, w_gu) = attend_forward(
        info, query, kv_own, [WHOLE, WHOLE, WHOLE, BLOCKS], shards, shapes, pieces, 2
    )
    if spare:
        w_down = w_down.reshape(devices, -1, model)[:, :down_depth].reshape(-1, model)
    mid_rows = residual + contract(attended, w_out, 0, 0)
    inv_two, normed_two = norm_forward(mid_rows, gain_mlp)
    inner_rows = normed_two.astype(jnp.bfloat16)

    g_down, d_inner, out_rows, g_gu_own = feed_forward(
        inner_rows, inner_rows.T, out_grad, w_gu, w_down, 3
    )
    block_out = (mid_rows + out_rows).astype(jnp.bfloat16)
    back_two, g_gain_two = norm_backward(mid_rows, inv_two, gain_mlp, d_inner)
    d_mid = out_grad.astype(jnp.float32) + back_two
    d_branch = d_mid.astype(jnp.bfloat16)
    d_attended = contract(w_out, d_branch, 1, 1).astype(jnp.bfloat16)
    dp_size = lax.axis_size("dp")
    if spare:
        g_down = jnp.pad(
            g_down.reshape(devices, down_depth, model), ((0, 0), (0, spare), (0, 0))
        )
    g_down = g_down.reshape(dp_size, -1, model)
    g_out = matmul(attended, d_branch).astype(jnp.bfloat16).reshape(dp_size, -1, model)
    d_query, d_kv, g_down_own, g_out_own = attend_backward(
        info, query, kv_all, attended_full, lse, d_attended, g_down, g_out, 4
    )
    g_down_own = g_down_own[:down_depth]
    d_qkv = jnp.concatenate(
        [
            rotate(d_query, cos_table, -sin_table),
            rotate(d_kv[:, :HD].reshape(kv_width, tok_dev), cos_table, -sin_table),
            d_kv[:, HD:].reshape(kv_width, tok_dev),
        ],
        0,
    ).astype(jnp.bfloat16)
    d_normed = contract(d_qkv, w_qkv, 0, 1)
    back_one, g_gain_one = norm_backward(residual, inv_one, gain_attn, d_normed)
    input_grad = d_mid + back_one
    g_qkv = contract(normed_low, d_qkv, 0, 1).astype(jnp.bfloat16).reshape(dp_size, -1, 4 * width)
    g_gains = jnp.stack([g_gain_one, g_gain_two], 0).reshape(2, devices, own)
    g_gains = jnp.pad(jnp.moveaxis(g_gains, 0, 1), ((0, 0), (0, 6), (0, 128 - own)))
    squares = squares_of(g_gu_own) + squares_of(g_down_own) + squares_of(g_out_own)
    g_qkv_own, g_gains_own, total_sq = last_sums(g_qkv, g_gains, squares, 512, 5)
    g_gains_own = g_gains_own[:2, :own]
    grad_norm = jnp.sqrt(total_sq[0, 0])
    clip_factor = jnp.minimum(1.0, CLIP_NORM / (grad_norm + 1e-06))
    new_qkv, new_qkv_m, new_qkv_v = adam_update(
        qkv_weight, qkv_m, qkv_v, g_qkv_own, clip_factor, 0.06, WEIGHT_DECAY
    )
    new_out, new_out_m, new_out_v = adam_update(
        out_weight, out_m, out_v, g_out_own, clip_factor, 0.4, WEIGHT_DECAY
    )
    new_gu, new_gu_m, new_gu_v = adam_update(
        gate_up_weight, gate_up_m, gate_up_v, g_gu_own, clip_factor, 0.06, WEIGHT_DECAY
    )
    new_down, new_down_m, new_down_v = adam_update(
        down_weight, down_m, down_v, g_down_own, clip_factor, 0.06, WEIGHT_DECAY
    )
    new_gains, new_gain_m, new_gain_v = adam_update(
        norm_gains, gain_m, gain_v, g_gains_own, clip_factor, 0.6, 0.0
    )
    return (
        block_out,
        input_grad,
        grad_norm,
        new_qkv,
        new_qkv_m,
        new_qkv_v,
        new_out,
        new_out_m,
        new_out_v,
        new_gu,
        new_gu_m,
        new_gu_v,
        new_down,
        new_down_m,
        new_down_v,
        new_gains,
        new_gain_m,
        new_gain_v,
    )


def solution(mesh):
    in_specs = (
        P(("dp", "seq"), None),
        P(("dp", "seq"), None),
        P("dp", None),
        P("dp"),
        P("dp", None),
        P(("dp", "seq"), None),
        P(("dp", "seq"), None),
        P(("dp", "seq"), None),
        P(("dp", "seq"), None),
        P(("dp", "seq"), None),
        P(("dp", "seq"), None),
        P(("dp", "seq"), None),
        P(("dp", "seq"), None),
        P(("dp", "seq"), None),
        P(("dp", "seq"), None),
        P(("dp", "seq"), None),
        P(("dp", "seq"), None),
        P(None, ("dp", "seq")),
        P(None, ("dp", "seq")),
        P(None, ("dp", "seq")),
    )
    out_specs = (
        P(("dp", "seq"), None),
        P(("dp", "seq"), None),
        P(),
        P(("dp", "seq"), None),
        P(("dp", "seq"), None),
        P(("dp", "seq"), None),
        P(("dp", "seq"), None),
        P(("dp", "seq"), None),
        P(("dp", "seq"), None),
        P(("dp", "seq"), None),
        P(("dp", "seq"), None),
        P(("dp", "seq"), None),
        P(("dp", "seq"), None),
        P(("dp", "seq"), None),
        P(("dp", "seq"), None),
        P(None, ("dp", "seq")),
        P(None, ("dp", "seq")),
        P(None, ("dp", "seq")),
    )
    return jax.shard_map(
        per_device, mesh=mesh, in_specs=in_specs, out_specs=out_specs, check_vma=False
    )
```

time: 1790 us -> 1130 us (0.63)
  waiting for transfers between devices: 1290 us -> 0 us
  Pallas kernels: 55.8 us -> 953 us
  matrix products: 227 us -> 56.5 us
  blocking collectives: 111 us -> 0 us
  local copies, waits for them, and re-layouts: 17.9 us -> 42.9 us
    pallas_call x2 -> x5, Pallas kernels: 55.8 us -> 953 us  [the longest x1 341 us: attend_forward(): pl.pallas_call(functools.partial(attend_kernel, kinds, pieces), out_shape...]
    all_gather x4 -> x0, waiting for transfers between devices: 399 us -> none  [gathered(): lax.all_gather(shard.astype(jnp.bfloat16), ('dp', 'seq'), axis=0, tiled=T...]
    unnamed x15 -> x0, waiting for transfers between devices: 387 us -> none
    reduce_scatter x7 -> x0, waiting for transfers between devices: 374 us -> none  [the longest x4 212 us: scattered(): lax.psum_scatter(part, 'seq', scatter_dimension=0, tiled=True)]
    ppermute x6 -> x0, waiting for transfers between devices: 127 us -> none  [the longest x3 112 us: sum_to_owner(): lax.ppermute(total.astype(jnp.bfloat16), 'seq', [(i, i - 1) for i in rang...]
    dot_general x9 -> x5, matrix products: 167 us -> 49.7 us  [contract(): lax.dot_general(left, right, (((left_dim,), (right_dim,)), ((), ())), pre...]
    all_gather x1 -> x0, blocking collectives: 70 us -> none  [per_device(): lax.all_gather(norm_gains.astype(jnp.bfloat16), ('dp', 'seq'), axis=1, ti...]
    dot_general x3 -> x1, matrix products: 59.9 us -> 6.86 us  [matmul(): return jnp.dot(left, right, preferred_element_type=jnp.float32)]
  transfers between devices with their start and end apart: 19 -> 0, of which waited for: 14 -> 0; matrix products, arithmetic and copies ran while one was open for 10% -> 0% of each run, Pallas kernels for 3% -> 0%
where the time goes in v3:
time: 1130 us; the launch traced here: 1120 us
  Pallas kernels  953 us (84%)
  other arithmetic  59.1 us (5%)
  matrix products  56.5 us (5%)
  local copies, waits for them, and re-layouts  42.9 us (4%)
    pallas_call x1, Pallas kernels, attend_forward(): pl.pallas_call(functools.partial(attend_kernel, kinds, pieces), out_shape...  341 us
    pallas_call x1, Pallas kernels, feed_forward(): pl.pallas_call(mlp_kernel, out_shape=[jax.ShapeDtypeStruct((FF, model), j...  267 us
    pallas_call x1, Pallas kernels, attend_backward(): pl.pallas_call(backward_kernel, out_shape=[jax.ShapeDtypeStruct(query.sha...  198 us
    pallas_call x1, Pallas kernels, gather_all(): pl.pallas_call(functools.partial(gather_kernel, kinds, pieces), out_shape...  76.6 us
    pallas_call x1, Pallas kernels, last_sums(): pl.pallas_call(last_kernel, out_shape=[jax.ShapeDtypeStruct((parts.shape[...  71.1 us
    dot_general x5, matrix products, contract(): lax.dot_general(left, right, (((left_dim,), (right_dim,)), ((), ())), pre...  49.7 us

profile of v3, /device:TPU:0, one launch (start us, length us, event | category | flops | bytes accessed | tf_op | source)
XLA Modules:
  0.0 1118.9 jit_solution(13529632413527694657)
XLA Ops:
  0.7 0.8 reduce-window_clone.1
  1.5 0.7 subtract_bitcast_fusion
  7.4 2.9 copy.49
  11.4 3.1 convert_element_type.90.refs_2_
  14.4 0.8 convert_element_type.88.refs_0_
  15.2 0.6 pad.8.refs_1_
  15.8 76.6 %gather.1 = (bf16[2048,2560]{1,0:T(8,128)(2,1)}, bf16[512,128]{1,0:T(8,128)(2,1)}, bf16[256,3072]{1,0:T(8,128)(2,1)}) custom-call(bf16[64,2560]{1,0:T(8,128)(2,1)} %convert_element_type.88.refs_0_, bf16[16,128]{1,0:T(8,128)(2,1)} %pad.8.refs_1_, bf16[64,11264]{1,0:T(8,128)(2,1)} %convert_element_type.90.refs_2_), custom_call_target="tpu_custom_call" | custom-call | tf_op jit(solution)/shard_map/gather/pallas_call | solution.py:297
  92.4 0.9 slice_bitcast_fusion
  93.5 8.6 fusion.16
  103.1 0.7 subtract_convert_fusion.1
  103.9 1.5 pad_maximum_fusion.1
  107.1 340.8 %attend_forward.1 = (bf16[2048,512]{1,0:T(8,128)(2,1)}, f32[2048,512]{1,0:T(8,128)}, f32[32,1,512]{2,1,0:T(1,128)S(1)}, bf16[4,4,128,512]{3,2,1,0:T(8,128)(2,1)}...) custom-call(s32[2]{0:T(128)S(1)} %pad_add_fusion.info, ...), custom_call_target="tpu_custom_call" | custom-call | tf_op jit(solution)/shard_map/attend_forward/pallas_call | solution.py:385
  447.9 11.0 multiply_reduce_fusion.2
  458.9 4.1 fusion.37.turned_ref
  463.5 2.8 copy.51.rows_ref
  466.3 266.7 %feed_forward.1 = (bf16[5632,2048]{1,0:T(8,128)(2,1)}, f32[512,2048]{1,0:T(8,128)}, f32[512,2048]{1,0:T(8,128)}, f32[64,11264]{1,0:T(8,128)}) custom-call(bf16[512,2048]{1,0:T(8,128)(2,1)} %copy.51.rows_ref, bf16[2048,512]{1,0:T(8,128)(2,1)} %fusion.37.turned_ref, bf16[512,2048]{1,0:T(8,128)(2,1)} %grad_hbm.1, bf16[2048,11264]{1,0:T(8,128)(2,1)} %get-tuple-element.44.gu_ref, ...), custom_call_target="tpu_custom_call" | custom-call | tf_op jit(solution)/shard_map/feed_forward/pallas_call | solution.py:721
  732.9 5.3 copy.54
  738.2 4.7 multiply_reduce_fusion
  742.9 5.5 copy.52
  748.4 2.5 copy.53
  750.9 7.4 subtract_add_fusion
  758.3 6.9 convolution_convert_fusion.1
  765.2 5.7 convolution_convert_fusion.2.do_ref
  770.9 198.0 %attend_backward.1 = (f32[2048,512]{1,0:T(8,128)}, f32[4,128,512]{2,1,0:T(8,128)}, f32[176,2048]{1,0:T(8,128)}, f32[64,2048]{1,0:T(8,128)}) custom-call(s32[2]{0:T(128)} %copy-done.5, bf16[2048,512]{1,0:T(8,128)(2,1)} %bitcast.38, bf16[4,4,128,512]{3,2,1,0:T(8,128)(2,1)} %get-tuple-element.48.kv_ref, f32[2048,512]{1,0:T(8,128)} %get-tuple-element.49.full_ref, ...), custom_call_target="tpu_custom_call" | custom-call | tf_op jit(solution)/shard_map/attend_backward/pallas_call | solution.py:907
  969.0 2.0 mul.548
  971.0 1.3 reshape.268
  972.3 1.9 reduce_sum.98
  974.2 0.9 mul.549
  975.1 1.1 reshape.269
  976.2 0.7 reduce_sum.99
  976.9 1.9 mul.547
  978.8 4.1 reshape.267
  982.9 2.6 reduce_sum.97
  985.5 2.9 subtract_convert_fusion
  988.7 1.1 copy-done.28
  990.0 1.1 copy-done.9
  991.1 12.8 %fusion.8 = (f32[2048]{0:T(1024)S(1)}, f32[512]{0:T(512)}, f32[512,2048]{0,1:T(8,128)}) fusion(bf16[512,2048]{0,1:T(8,128)(2,1)S(1)} %copy-done.9, f32[512]{0:T(512)S(1)} %copy-done.35, f32[2048]{0:T(1024)S(1)} %reshape.270, bf16[2048,2560]{1,0:T(8,128)(2,1)} %get-tuple-element.39, bf16[256,512]{1,0:T(8,128)(2,1)S(1)} %bitcast.51, ...), kind=kOutput, calls=%fused_computation.17 | convolution fusion | flops 5383910912 | bytes 19419136 | tf_op jit(solution)/shard_map/dot_general | solution.py:32
  1004.2 11.5 %convolution_convert_fusion = bf16[2048,2560]{1,0:T(8,128)(2,1)} fusion(bf16[256,512]{1,0:T(8,128)(2,1)S(1)} %bitcast.52, bf16[256,512]{1,0:T(8,128)(2,1)S(1)} %bitcast.50, bf16[2048,512]{1,0:T(8,128)(2,1)} %bitcast.46, bf16[512,2048]{0,1:T(8,128)(2,1)} %copy-done.8, f32[2048]{0:T(1024)S(1)} %reshape.270, f32[512]{0:T(512)S(1)} %copy-done.35), kind=kOutput, calls=%fused_computation | convolution fusion | flops 5386010624 | bytes 15214592 | tf_op jit(solution)/shard_map/dot_general | solution.py:32
  1015.7 71.1 %last_sums.1 = (f32[64,2560]{1,0:T(8,128)S(1)}, f32[8,128]{1,0:T(8,128)S(1)}, f32[8,128]{1,0:T(8,128)S(1)}) custom-call(bf16[8,256,2560]{2,1,0:T(8,128)(2,1)} %bitcast.40, f32[32,8,128]{2,1,0:T(8,128)S(1)} %pad.9.gains_ref, f32[8,128]{1,0:T(8,128)S(1)} %add_add_fusion.squares_ref), custom_call_target="tpu_custom_call" | custom-call | tf_op jit(solution)/shard_map/last_sums/pallas_call | solution.py:1020
  1088.1 1.3 multiply_subtract_fusion.4
  1089.4 5.7 multiply_subtract_fusion.1
  1095.1 7.3 multiply_subtract_fusion
  1102.5 1.4 multiply_subtract_fusion.3
  1104.5 1.6 multiply_subtract_fusion.2
  1106.1 1.1 copy-done.10
  1107.2 2.5 fusion.5
  1109.7 5.5 copy.59
  1115.2 2.4 copy.58
  (119 shorter events, 7.5 us)
Async XLA Ops:
  7.4 98.8 %copy-start.5 = (s32[2]{0:T(128)}, s32[2]{0:T(128)S(1)}, u32[]{:S(2)}) copy-start(s32[2]{0:T(128)S(1)} %pad_add_fusion.info) | copy-start | bytes 28
  10.2 437.6 %copy-start.8 = (bf16[512,2048]{0,1:T(8,128)(2,1)}, bf16[512,2048]{0,1:T(8,128)(2,1)S(1)}, u32[]{:S(2)}) copy-start(bf16[512,2048]{0,1:T(8,128)(2,1)S(1)} %copy.49) | copy-start | bytes 6291460
  10.2 4.2 copy-start.21
  10.8 4.4 copy-start.38
  11.4 82.1 %copy-start.34 = (f32[512]{0:T(512)}, f32[512]{0:T(512)S(1)}, u32[]{:S(2)}) copy-start(f32[512]{0:T(512)S(1)} %get-tuple-element.131) | copy-start | bytes 6148
  103.9 1.8 copy-start.16
  103.9 2.2 copy-start.24
  103.9 2.7 copy-start.2
  103.9 3.2 copy-start.3
  447.9 11.0 copy-start.4
  458.9 4.1 copy-start.6
  742.9 5.5 copy-start.14
  750.9 7.4 copy-start.39
  750.9 14.3 %slice-start = ((s8[8388608]{0:T(1024)(128)(4,1)}), s8[4194304]{0:T(1024)(128)(4,1)S(1)}, s32[]{:S(2)}) async-start(s8[8388608]{0:T(1024)(128)(4,1)} %bitcast.55), calls=%async_computation | async-start | bytes 8388608
  758.3 6.9 copy-start.11
  758.3 6.9 slice-start.1
  971.0 3.2 copy-start.17
  972.3 4.6 copy-start.7
  982.9 2.6 copy-start.32
  988.4 1.4 copy-start.28
  988.4 2.7 copy-start.9
  988.4 2.7 copy-start.35
  988.6 15.3 %copy-start.23 = (bf16[32,2,32,512]{3,2,1,0:T(8,128)(2,1)}, bf16[32,2,32,512]{3,2,1,0:T(8,128)(2,1)S(1)}, u32[]{:S(2)}) copy-start(bf16[32,2,32,512]{3,2,1,0:T(8,128)(2,1)S(1)} %pad_maximum_fusion.2) | copy-start | bytes 6291460
  991.1 12.9 %copy-start.31 = (f32[2048]{0:T(1024)S(1)}, f32[2048]{0:T(1024)}, u32[]{:S(2)}) copy-start(f32[2048]{0:T(1024)} %get-tuple-element.96) | copy-start | bytes 24580
  1089.4 5.7 copy-start.13
  1089.4 5.7 copy-start.20
  1095.1 7.3 copy-start.18
  1095.1 7.3 copy-start.25
  1095.1 7.3 copy-start.29
  1095.1 7.3 copy-start.30
  1095.1 11.0 copy-start.19
  1102.4 1.5 copy-start.22
  1102.4 1.6 copy-start.26
  1102.4 2.0 copy-start.27
  1102.5 3.6 copy-start.12
  1103.9 2.2 copy-start.37
  1103.9 3.3 copy-start.10
  1103.9 3.3 copy-start.33
  1103.9 3.3 copy-start.36
  1109.7 5.5 copy-start.15
  1109.7 7.9 copy-start.1
  (1 other events, 0.0 us)

commit v4 on v3

--- a/solution.py
+++ b/solution.py
@@ -1,4 +1,5 @@
 import functools
+import math
 
 import jax
 import jax.numpy as jnp
@@ -32,35 +33,6 @@
     return lax.dot_general(
         left, right, (((left_dim,), (right_dim,)), ((), ())), preferred_element_type=jnp.float32
     )
-
-
-def rope_tables(positions):
-    half_dim = HD // 2
-    inverse = jnp.exp(-(2.0 * jnp.arange(half_dim, dtype=jnp.float32) / HD) * jnp.log(ROPE_BASE))
-    angles = inverse[:, None] * positions.astype(jnp.float32)[None, :]
-    return (jnp.cos(angles), jnp.sin(angles))
-
-
-def rotate(rows, cos_table, sin_table):
-    tokens = rows.shape[1]
-    split = rows.reshape(-1, 2, HD // 2, tokens)
-    first, second = (split[:, 0], split[:, 1])
-    return jnp.stack(
-        [first * cos_table - second * sin_table, second * cos_table + first * sin_table], 1
-    ).reshape(rows.shape)
-
-
-def norm_forward(rows_in, gain_row):
-    inv_rms = lax.rsqrt(jnp.mean(rows_in * rows_in, axis=-1, keepdims=True) + NORM_EPS)
-    return (inv_rms, rows_in * inv_rms * gain_row)
-
-
-def norm_backward(rows_in, inv_rms, gain_row, gradient):
-    weighted = gain_row * gradient
-    back_rows = inv_rms * weighted - rows_in * inv_rms**3 * jnp.mean(
-        weighted * rows_in, axis=-1, keepdims=True
-    )
-    return (back_rows, jnp.sum(gradient * rows_in * inv_rms, axis=0))
 
 
 LOG2E = 1.4426950408889634
@@ -112,16 +84,6 @@
     lse_ref[head] = top + jnp.log2(total)
 
 
-def sum_to_owner(parts):
-    size = lax.axis_size("seq")
-    total = parts[size - 1]
-    for step in range(size - 1, 0, -1):
-        total = parts[step - 1] + lax.ppermute(
-            total.astype(jnp.bfloat16), "seq", [(i, i - 1) for i in range(step, size)]
-        ).astype(jnp.float32)
-    return total
-
-
 def adam_update(weight, first_mom, second_mom, gradient, clip_factor, rate, decay):
     step_grad = gradient * clip_factor
     first_new = BETA_ONE * first_mom + (1.0 - BETA_ONE) * step_grad
@@ -143,7 +105,7 @@
 
 
 class Gather:
-    ahead = 3
+    ahead = 2
 
     def __init__(self, kinds, pieces, shards, fulls, local_sems, send_sems, recv_sems):
         self.kinds, self.pieces, self.shards, self.fulls = (kinds, pieces, shards, fulls)
@@ -154,7 +116,8 @@
         up = list(range(1, self.bits))
         self.orders = (up + [0], up[::-1] + [0])
         self.started = []
-        self.done = set()
+        self.done, self.begun = (set(), set())
+        self.hold = False
 
     def along(self, step):
         return {"seq": lax.rem(self.seq + step, self.seq_size)}
@@ -223,10 +186,11 @@
         for piece in range(len(self.pieces)):
             for side in self.sides(piece):
                 self.local_copy(piece, side).start()
-        for piece in range(min(self.ahead, len(self.pieces))):
-            self.send_rows(piece)
 
     def send_rows(self, piece):
+        if piece in self.begun or piece >= len(self.pieces):
+            return
+        self.begun.add(piece)
         if self.kind(piece) == BLOCKS:
             return
         for step in range(1, self.seq_size):
@@ -237,6 +201,7 @@
         if (piece, stage) in self.done:
             return
         self.done.add((piece, stage))
+        self.send_rows(piece)
         kind = self.kind(piece)
         if stage and kind == ROWS:
             return
@@ -259,14 +224,18 @@
             for bit in order[stage:]:
                 for block in held:
                     self.start(self.block_copy(piece, side, block, bit))
-        if stage == 0 and piece + self.ahead < len(self.pieces):
+        if stage == 0 and not self.hold:
             self.send_rows(piece + self.ahead)
 
-    def finish(self):
-        for turn in range(len(self.pieces) + self.bits):
-            for piece in range(len(self.pieces)):
-                if 0 <= turn - piece <= self.bits:
-                    self.advance(piece, turn - piece)
+    def events(self, lag):
+        for turn in range(len(self.pieces) + lag * self.bits):
+            for stage in range(self.bits, -1, -1):
+                if 0 <= turn - lag * stage < len(self.pieces):
+                    yield (turn - lag * stage, stage)
+
+    def finish(self, lag=1):
+        for event in self.events(lag):
+            self.advance(*event)
         for piece in range(len(self.pieces)):
             if self.kind(piece) != WHOLE:
                 for side in self.sides(piece):
@@ -284,37 +253,74 @@
     ]
 
 
-def gather_kernel(kinds, pieces, *refs):
-    count, sems = (len(kinds), len(refs) - 3)
-    gather = Gather(kinds, pieces, refs[:count], refs[count:sems], *refs[sems:])
+def gather_kernel(kinds, pieces, count, *refs):
+    shards, refs = (refs[:count], refs[count:])
+    rounded, fulls, sems = (refs[:count], refs[count:-3], refs[-3:])
+    for shard, result in zip(shards, rounded):
+        result[...] = shard[...].astype(jnp.bfloat16)
+    gather = Gather(kinds, pieces, rounded, fulls, *sems)
     greet()
     gather.begin()
+    for piece in range(gather.ahead):
+        gather.send_rows(piece)
     gather.finish()
 
 
 def gather_all(kinds, shards, shapes, pieces, collective_id):
+    vmem = pl.BlockSpec(memory_space=pltpu.VMEM)
     hbm = pl.BlockSpec(memory_space=pl.ANY)
-    return pl.pallas_call(
-        functools.partial(gather_kernel, kinds, pieces),
-        out_shape=[jax.ShapeDtypeStruct(shape, jnp.bfloat16) for shape in shapes],
-        in_specs=[hbm] * len(shards),
-        out_specs=[hbm] * len(shapes),
+    count = len(shards)
+    out = pl.pallas_call(
+        functools.partial(gather_kernel, kinds, pieces, count),
+        out_shape=[jax.ShapeDtypeStruct(shard.shape, jnp.bfloat16) for shard in shards]
+        + [jax.ShapeDtypeStruct(shape, jnp.bfloat16) for shape in shapes],
+        in_specs=[vmem] * count,
+        out_specs=[vmem] * count + [hbm] * len(shapes),
         scratch_shapes=gather_scratch(len(pieces)),
-        compiler_params=pltpu.CompilerParams(collective_id=collective_id, has_side_effects=True),
+        compiler_params=pltpu.CompilerParams(
+            collective_id=collective_id, has_side_effects=True, vmem_limit_bytes=32 * 2**20
+        ),
         name="gather",
     )(*shards)
-
-
-def attend_kernel(kinds, pieces, info, q_ref, kv_ref, *refs):
+    return (out[:count], out[count:])
+
+
+def token_layout(tokens, lengths, counts, segments):
+    seq = lax.axis_index("seq")
+    segment = segments[0, seq * tokens]
+    start = sum(
+        jnp.where(slot < segment, lengths[0, slot], 0) for slot in range(lengths.shape[1])
+    )
+    valid = (segment < counts[0]).astype(jnp.int32)
+    return (start, jnp.where(valid > 0, seq - start // tokens + 1, 1), valid)
+
+
+def rotated(value, cos, sin):
+    first, second = (value[: HD // 2], value[HD // 2 :])
+    return jnp.concatenate([first * cos - second * sin, second * cos + first * sin], 0).astype(
+        jnp.bfloat16
+    )
+
+
+def attend_kernel(kinds, pieces, lengths, counts, segments, x_ref, gains_ref, w_qkv, *refs):
     count = len(kinds)
     shards = refs[:count]
-    o_ref, full_ref, lse_ref, kv_all_ref = refs[count : count + 4]
-    fulls = refs[count + 4 : -7]
-    k_rows, slots, kv_send, kv_recv = refs[-7:-3]
+    q_ref, o_ref, full_ref, lse_ref, kv_all_ref, mid_ref, inner_ref, turned_ref = refs[count : count + 8]
+    normed_ref, gain_one, gain_two, cos_ref, sin_ref = refs[count + 8 : count + 13]
+    fulls = refs[count + 13 : -11]
+    kv_ref, k_rows, slots, kv_send, kv_recv, o_rows, w_buf, w_sems = refs[-11:-3]
     gather = Gather(kinds, pieces, shards, fulls, *refs[-3:])
     seq, seq_size = (gather.seq, gather.seq_size)
-    reach, valid = (info[0], info[1])
-    greet()
+    tokens, model = x_ref.shape
+    start, reach, valid = token_layout(tokens, lengths, counts, segments)
+
+    def qkv_load(tile, slot):
+        return pltpu.make_async_copy(
+            w_qkv.at[:, pl.ds(tile * TILE, TILE)], w_buf.at[slot], w_sems.at[slot]
+        )
+
+    def qkv_tile(slot):
+        return matmul(o_rows[...], w_buf[slot]).T
 
     def kv_copy(group, step):
         return pltpu.make_async_remote_copy(
@@ -326,17 +332,81 @@
             device_id_type=MESH,
         )
 
+    def send_kv(groups):
+        for group in groups:
+            for step in range(1, seq_size):
+
+                @pl.when(seq + step < seq_size)
+                def _():
+                    kv_copy(group, step).start()
+
+    last = w_qkv.shape[1] // TILE - 1
+    qkv_load(last, 0).start()
+    qkv_load(0, 1).start()
+    greet()
+    gather.begin()
+    gather.send_rows(1)
+    gather.send_rows(2)
+    gather.hold = True
+    gather.advance(0, 0)
+    half = lax.broadcasted_iota(jnp.int32, (HD // 2, tokens), 0).astype(jnp.float32)
+    inverse = jnp.exp(half * (-2.0 / HD * math.log(ROPE_BASE)))
+    place = seq * tokens - start + lax.broadcasted_iota(jnp.int32, (HD // 2, tokens), 1)
+    angles = place.astype(jnp.float32) * inverse
+    cos, sin = (jnp.cos(angles), jnp.sin(angles))
+    cos_ref[...] = cos
+    sin_ref[...] = sin
+    devices = gather.dp_size * seq_size
+    own = model // devices
+    for row, gain in enumerate((gain_one, gain_two)):
+        for chunk in range(model // 128):
+            gain[:, chunk * 128 : (chunk + 1) * 128] = sum(
+                pltpu.roll(
+                    gains_ref[16 * device + row : 16 * device + row + 1, :].astype(jnp.float32),
+                    device * own % 128,
+                    1,
+                )
+                for device in range(chunk * 128 // own, (chunk + 1) * 128 // own)
+            )
+
+    @pl.loop(0, tokens // 64)
+    def _(chunk):
+        part = pl.ds(pl.multiple_of(chunk * 64, 64), 64)
+        rows = x_ref[part, :].astype(jnp.float32)
+        inverse = lax.rsqrt(jnp.mean(rows * rows, axis=-1, keepdims=True) + NORM_EPS)
+        o_rows[part, :] = (rows * inverse * gain_one[...]).astype(jnp.bfloat16)
+
+    qkv_load(last, 0).wait()
+    value = qkv_tile(0)
+    qkv_load(1, 0).start()
     for group in range(KV_HEADS):
-        for step in range(1, seq_size):
-
-            @pl.when(seq + step < seq_size)
-            def _():
-                kv_copy(group, step).start()
-
-    gather.begin()
-    gather.advance(0, 0)
+        kv_ref[group, :HD, :] = rotated(value[group * HD : (group + 1) * HD], cos, sin)
+        rest = (KV_HEADS + group) * HD
+        kv_ref[group, HD:, :] = value[rest : rest + HD].astype(jnp.bfloat16)
     slots[0] = kv_ref[...]
-    beside = {1: [(0, 1)], 3: [(0, 2)], 5: [(1, 0)], 7: [(0, 3), (1, 1), (2, 0)]}
+    gather.advance(0, 1)
+    for tile in range(last):
+        slot = (tile + 1) % 2
+        qkv_load(tile, slot).wait()
+        value = qkv_tile(slot)
+        if tile + 2 < last:
+            qkv_load(tile + 2, slot).start()
+        for head in range(TILE // HD):
+            rows = slice(tile * TILE + head * HD, tile * TILE + (head + 1) * HD)
+            q_ref[rows, :] = rotated(value[head * HD : (head + 1) * HD], cos, sin)
+        part = slice(tile * TILE, (tile + 1) * TILE)
+        normed_ref[part, :] = transposed(o_rows[:, part])
+    gather.hold = False
+    events = [event for event in gather.events(2) if event not in gather.done]
+
+    def proceed(count):
+        for _ in range(min(count, len(events))):
+            gather.advance(*events.pop(0))
+
+    for group in range(KV_HEADS):
+        proceed(2)
+        send_kv([group])
+    proceed(2)
     for group in range(KV_HEADS):
         k_rows[0] = transposed(kv_ref[group, :HD, :])
         for step in range(1, seq_size):
@@ -346,16 +416,15 @@
                 kv_copy(group, step).wait_recv()
                 k_rows[step] = transposed(slots[step, group, :HD, :])
 
-        for part in range(2):
-
-            @pl.loop(group * SHARE + part * SHARE // 2, group * SHARE + (part + 1) * SHARE // 2)
+        for part in range(4):
+
+            @pl.loop(group * SHARE + part * SHARE // 4, group * SHARE + (part + 1) * SHARE // 4)
             def _(head):
                 attend_head(
                     head, seq + 1, reach, valid, q_ref, slots, group, k_rows, o_ref, full_ref, lse_ref
                 )
 
-            for event in beside.get(group * 2 + part, []):
-                gather.advance(*event)
+            proceed(1)
     for step in range(seq_size):
 
         @pl.when(seq >= step)
@@ -373,43 +442,86 @@
             def _():
                 kv_copy(group, step).wait_send()
 
-    gather.finish()
-
-
-def attend_forward(info, query, kv, kinds, shards, shapes, pieces, collective_id):
-    tokens = query.shape[1]
+    chunks = model // TILE
+
+    def w_load(chunk):
+        return pltpu.make_async_copy(
+            fulls[0].at[:, pl.ds(chunk * TILE, TILE)], w_buf.at[chunk % 2], w_sems.at[chunk % 2]
+        )
+
+    while (1, gather.bits) not in gather.done:
+        proceed(1)
+    w_load(0).start()
+    for row in range(model // TILE):
+        part = slice(row * TILE, (row + 1) * TILE)
+        o_rows[:, part] = transposed(o_ref[part, :])
+    for chunk in range(chunks):
+        w_load(chunk).wait()
+        if chunk + 1 < chunks:
+            w_load(chunk + 1).start()
+        part = slice(chunk * TILE, (chunk + 1) * TILE)
+        mid_ref[:, part] = x_ref[:, part].astype(jnp.float32) + matmul(o_rows[...], w_buf[chunk % 2])
+        proceed(1)
+
+    @pl.loop(0, tokens // 64)
+    def _(chunk):
+        part = pl.ds(pl.multiple_of(chunk * 64, 64), 64)
+        rows = mid_ref[part, :]
+        inverse = lax.rsqrt(jnp.mean(rows * rows, axis=-1, keepdims=True) + NORM_EPS)
+        inner_ref[part, :] = (rows * inverse * gain_two[...]).astype(jnp.bfloat16)
+
+    proceed(1)
+    for row in range(model // TILE):
+        part = slice(row * TILE, (row + 1) * TILE)
+        turned_ref[part, :] = transposed(inner_ref[:, part])
+    gather.finish(2)
+
+
+def attend_forward(layout, rows, gains, w_qkv, kinds, shards, shapes, pieces, collective_id):
+    tokens, model = rows.shape
     seq_size = lax.axis_size("seq")
-    count = len(shards)
+    low, wide = (jnp.bfloat16, jnp.float32)
     vmem = pl.BlockSpec(memory_space=pltpu.VMEM)
+    smem = pl.BlockSpec(memory_space=pltpu.SMEM)
     hbm = pl.BlockSpec(memory_space=pl.ANY)
+    results = [
+        ((HEADS * HD, tokens), low),
+        ((HEADS * HD, tokens), low),
+        ((HEADS * HD, tokens), wide),
+        ((HEADS, 1, tokens), wide),
+        ((seq_size, KV_HEADS, 2 * HD, tokens), low),
+        ((tokens, model), wide),
+        ((tokens, model), low),
+        ((model, tokens), low),
+        ((model, tokens), low),
+        ((1, model), wide),
+        ((1, model), wide),
+        ((HD // 2, tokens), wide),
+        ((HD // 2, tokens), wide),
+    ]
     out = pl.pallas_call(
         functools.partial(attend_kernel, kinds, pieces),
-        out_shape=[
-            jax.ShapeDtypeStruct(query.shape, jnp.bfloat16),
-            jax.ShapeDtypeStruct(query.shape, jnp.float32),
-            jax.ShapeDtypeStruct((HEADS, 1, tokens), jnp.float32),
-            jax.ShapeDtypeStruct((seq_size, *kv.shape), kv.dtype),
-            *[jax.ShapeDtypeStruct(shape, jnp.bfloat16) for shape in shapes],
-        ],
-        in_specs=[pl.BlockSpec(memory_space=pltpu.SMEM), vmem, vmem] + [hbm] * count,
-        out_specs=[vmem] * 4 + [hbm] * len(shapes),
+        out_shape=[jax.ShapeDtypeStruct(*result) for result in results]
+        + [jax.ShapeDtypeStruct(shape, low) for shape in shapes],
+        in_specs=[smem] * 3 + [vmem] * 2 + [hbm] * (1 + len(shards)),
+        out_specs=[vmem] * len(results) + [hbm] * len(shapes),
         scratch_shapes=[
-            pltpu.VMEM((seq_size, tokens, HD), jnp.bfloat16),
-            pltpu.VMEM((seq_size, *kv.shape), kv.dtype),
+            pltpu.VMEM((KV_HEADS, 2 * HD, tokens), low),
+            pltpu.VMEM((seq_size, tokens, HD), low),
+            pltpu.VMEM((seq_size, KV_HEADS, 2 * HD, tokens), low),
             pltpu.SemaphoreType.DMA((seq_size, KV_HEADS)),
             pltpu.SemaphoreType.DMA((seq_size, KV_HEADS)),
+            pltpu.VMEM((tokens, model), low),
+            pltpu.VMEM((2, model, TILE), low),
+            pltpu.SemaphoreType.DMA((2,)),
             *gather_scratch(len(pieces)),
         ],
         compiler_params=pltpu.CompilerParams(
-            collective_id=collective_id, has_side_effects=True, vmem_limit_bytes=48 * 2**20
+            collective_id=collective_id, has_side_effects=True, vmem_limit_bytes=58 * 2**20
         ),
         name="attend_forward",
-    )(info, query, kv, *shards)
-    return (out[:4], out[4:])
-
-
-def squares_of(value):
-    return jnp.sum((value * value).reshape(-1, 8, 128), 0)
+    )(*layout, rows, gains, w_qkv, *shards)
+    return (out[: len(results)], out[len(results) :])
 
 
 def apart(index, distance, bits):
@@ -594,11 +706,37 @@
 TILE = 512
 
 
+def squares_of(value):
+    return sum(
+        jnp.sum((part * part).reshape(-1, 8, 128), 0)
+        for part in (value[:, c * 128 : (c + 1) * 128] for c in range(value.shape[1] // 128))
+    )
+
+
+def norm_backward_rows(rows_of, gradient, gain_ref, give):
+    tokens, model = gradient.shape
+    chunk_rows = 64
+
+    def step(chunk, gain_sum):
+        part = pl.ds(pl.multiple_of(chunk * chunk_rows, chunk_rows), chunk_rows)
+        rows, grad = (rows_of(part), gradient[part, :])
+        inverse = lax.rsqrt(jnp.mean(rows * rows, axis=-1, keepdims=True) + NORM_EPS)
+        weighted = gain_ref[...] * grad
+        scaled = rows * inverse
+        mean = jnp.mean(weighted * rows, axis=-1, keepdims=True)
+        give(part, inverse * weighted - scaled * (inverse * inverse * mean))
+        return gain_sum + jnp.sum(grad * scaled, 0, keepdims=True)
+
+    return lax.fori_loop(
+        0, tokens // chunk_rows, step, jnp.zeros((1, model), jnp.float32)
+    )
+
+
 def mlp_kernel(
-    rows_ref, turned_ref, grad_hbm, gu_ref, down_ref,
-    down_grad, inner_hbm, out_hbm, sum_ref,
-    grad_ref, gu_buf, down_buf, hidden, d_gu, product, inner_ref, out_ref,
-    load_sems, store_sems, *scratch
+    rows_ref, turned_ref, gain_ref, grad_hbm, mid_hbm, gu_ref, down_ref, proj_ref,
+    down_grad, d_mid_hbm, branch_hbm, block_out_hbm, d_out_hbm, gain_sum, sum_ref, squares,
+    grad_ref, mid_ref, gu_buf, down_buf, hidden, d_gu, product, inner_ref, out_ref,
+    load_sems, store_sems, out_sems, *scratch
 ):
     tokens, model = rows_ref.shape
     tiles = FF // TILE
@@ -606,6 +744,7 @@
 
     def deliver(tile, side, total):
         sum_ref[:, pl.ds(pl.multiple_of(side * FF + tile * TILE, TILE), TILE)] = total
+        squares[...] += squares_of(total)
 
     scatter = Scatter(tiles, (size, depth, columns), scratch, deliver)
     bits = scatter.hops + 1
@@ -633,9 +772,36 @@
         )
 
     grad_load = pltpu.make_async_copy(grad_hbm, grad_ref, store_sems.at[1])
-    inner_store = pltpu.make_async_copy(inner_ref, inner_hbm, store_sems.at[2])
-    out_store = pltpu.make_async_copy(out_ref, out_hbm, store_sems.at[3])
+    mid_load = pltpu.make_async_copy(mid_hbm, mid_ref, store_sems.at[2])
+    d_mid_store = pltpu.make_async_copy(inner_ref, d_mid_hbm, store_sems.at[3])
+    low_stores = []
+    for place, result in enumerate((branch_hbm, block_out_hbm)):
+        for chunk in range(model // TILE):
+            low_stores.append(
+                pltpu.make_async_copy(
+                    gu_buf.at[0, place, pl.ds(chunk * tokens, tokens), :],
+                    result.at[:, pl.ds(chunk * TILE, TILE)],
+                    store_sems.at[4 + len(low_stores)],
+                )
+            )
+    chunks = model // TILE
+
+    def proj_load(chunk):
+        rows = pl.ds(chunk * TILE, TILE)
+        return pltpu.make_async_copy(
+            proj_ref.at[rows, :], down_buf.at[chunk % 2], out_sems.at[0, chunk % 2]
+        )
+
+    def d_out_store(chunk):
+        return pltpu.make_async_copy(
+            product.at[:, pl.ds(chunk * tokens, tokens)],
+            d_out_hbm.at[pl.ds(chunk * TILE, TILE), :],
+            out_sems.at[1, chunk],
+        )
+
     grad_load.start()
+    mid_load.start()
+    squares[...] = jnp.zeros_like(squares)
     for copy in loads(0, 0):
         copy.start()
     inner_ref[...] = jnp.zeros_like(inner_ref)
@@ -697,22 +863,60 @@
 
         store(tile).start()
 
-        @pl.when(tile == tiles - 1)
-        def _():
-            inner_store.start()
-            out_store.start()
+    def give(part, back):
+        start, count = (part.start, part.size)
+        d_mid = grad_ref[part, :].astype(jnp.float32) + back
+        inner_ref[part, :] = d_mid
+        block_out = mid_ref[part, :] + out_ref[part, :]
+        for chunk in range(model // TILE):
+            columns = slice(chunk * TILE, (chunk + 1) * TILE)
+            rows = pl.ds(pl.multiple_of(chunk * tokens + start, count), count)
+            gu_buf[0, 0, rows, :] = d_mid[:, columns].astype(jnp.bfloat16)
+            gu_buf[0, 1, rows, :] = block_out[:, columns].astype(jnp.bfloat16)
 
     @pl.loop(0, scatter.steps)
     def _(now):
         scatter.step(now, begin)
 
-    store(tiles - 1).wait()
-    inner_store.wait()
-    out_store.wait()
+        @pl.when(now == tiles)
+        def _():
+            mid_load.wait()
+            gain_sum[...] = norm_backward_rows(
+                lambda part: mid_ref[part, :], inner_ref, gain_ref, give
+            )
+            d_mid_store.start()
+            for copy in low_stores:
+                copy.start()
+            for chunk in range(2):
+                proj_load(chunk).start()
+
+        @pl.when(now == tiles + 1)
+        def _():
+            store(tiles - 1).wait()
+            for chunk in range(chunks):
+                proj_load(chunk).wait()
+                product[:, chunk * tokens : (chunk + 1) * tokens] = sum(
+                    contract(
+                        down_buf[chunk % 2, :, part * TILE : (part + 1) * TILE],
+                        gu_buf[0, 0, part * tokens : (part + 1) * tokens, :],
+                        1,
+                        1,
+                    )
+                    for part in range(chunks)
+                ).astype(jnp.bfloat16)
+                d_out_store(chunk).start()
+                if chunk + 2 < chunks:
+                    proj_load(chunk + 2).start()
+
+    d_mid_store.wait()
+    for copy in low_stores:
+        copy.wait()
+    for chunk in range(chunks):
+        d_out_store(chunk).wait()
     scatter.finish()
 
 
-def feed_forward(rows, turned, grad, w_gu, w_down, collective_id):
+def feed_forward(rows, turned, gain, grad, mid, w_gu, w_down, w_out, collective_id):
     tokens, model = rows.shape
     dp_size, seq_size = (lax.axis_size("dp"), lax.axis_size("seq"))
     shape = (dp_size // 2, model // dp_size, 2 * TILE)
@@ -723,13 +927,18 @@
         out_shape=[
             jax.ShapeDtypeStruct((FF, model), jnp.bfloat16),
             jax.ShapeDtypeStruct((tokens, model), jnp.float32),
-            jax.ShapeDtypeStruct((tokens, model), jnp.float32),
+            jax.ShapeDtypeStruct((tokens, model), jnp.bfloat16),
+            jax.ShapeDtypeStruct((tokens, model), jnp.bfloat16),
+            jax.ShapeDtypeStruct((model, tokens), jnp.bfloat16),
+            jax.ShapeDtypeStruct((1, model), jnp.float32),
             jax.ShapeDtypeStruct((model // (dp_size * seq_size), 2 * FF), jnp.float32),
+            jax.ShapeDtypeStruct((8, 128), jnp.float32),
         ],
-        in_specs=[vmem, vmem, hbm, hbm, hbm],
-        out_specs=[hbm, hbm, hbm, vmem],
+        in_specs=[vmem, vmem, vmem, hbm, hbm, hbm, hbm, hbm],
+        out_specs=[hbm, hbm, hbm, hbm, hbm, vmem, vmem, vmem],
         scratch_shapes=[
             pltpu.VMEM((tokens, model), jnp.bfloat16),
+            pltpu.VMEM((tokens, model), jnp.float32),
             pltpu.VMEM((2, 2, model, TILE), jnp.bfloat16),
             pltpu.VMEM((2, TILE, model), jnp.bfloat16),
             pltpu.VMEM((tokens, TILE), jnp.bfloat16),
@@ -738,14 +947,15 @@
             pltpu.VMEM((tokens, model), jnp.float32),
             pltpu.VMEM((tokens, model), jnp.float32),
             pltpu.SemaphoreType.DMA((2, 3)),
-            pltpu.SemaphoreType.DMA((4,)),
+            pltpu.SemaphoreType.DMA((4 + 2 * model // TILE,)),
+            pltpu.SemaphoreType.DMA((2, model // TILE)),
             *Scatter.scratch(shape),
         ],
         compiler_params=pltpu.CompilerParams(
             collective_id=collective_id, has_side_effects=True, vmem_limit_bytes=60 * 2**20
         ),
         name="feed_forward",
-    )(rows, turned, grad, w_gu, w_down)
+    )(rows, turned, gain, grad, mid, w_gu, w_down, w_out)
 
 
 def load_tile(scatter, source, load_sems):
@@ -778,37 +988,47 @@
     return (begin, complete)
 
 
-def delivered(ref, columns):
+def delivered(ref, columns, squares):
     def deliver(tile, side, total):
         start = pl.multiple_of(tile * columns + side * (columns // 2), columns // 2)
         ref[:, pl.ds(start, columns // 2)] = total
+        squares[...] += squares_of(total)
 
     return deliver
 
 
 def backward_kernel(
-    info, q_ref, kv_ref, full_ref, lse_ref, do_ref, down_ref, proj_ref,
-    dq_ref, dkv_ref, down_sum, proj_sum,
-    k_rows, v_rows, dk_acc, dv_acc, parts, parts_got, part_sends, part_recvs, load_sems, *scratch
+    lengths, counts, segments,
+    q_ref, kv_ref, full_ref, lse_ref, do_ref, o_ref, branch_ref, cos_ref, sin_ref, squares_in, down_ref,
+    d_qkv_ref, down_sum, proj_sum, squares,
+    k_rows, v_rows, dk_acc, dv_acc, dkv_ref, turned, parts, parts_got, part_sends, part_recvs, load_sems, *scratch
 ):
     tokens = q_ref.shape[1]
-    reach, valid = (info[0], info[1])
+    _, reach, valid = token_layout(tokens, lengths, counts, segments)
     count = len(scratch) // 2
     down = Scatter(
         down_ref.shape[2] // scratch[0].shape[2],
         scratch[0].shape,
         scratch[:count],
-        delivered(down_sum, scratch[0].shape[2]),
+        delivered(down_sum, scratch[0].shape[2], squares),
     )
     proj = Scatter(
-        proj_ref.shape[2] // scratch[count].shape[2],
+        branch_ref.shape[1] // scratch[count].shape[2],
         scratch[count].shape,
         scratch[count:],
-        delivered(proj_sum, scratch[count].shape[2]),
+        delivered(proj_sum, scratch[count].shape[2], squares),
     )
     seq, seq_size = (down.seq, down.seq_size)
     blocks = seq + 1
+    squares[...] = squares_in[...]
     greet()
+
+    def unrotated(value):
+        first, second = (value[: HD // 2], value[HD // 2 :])
+        cos, sin = (cos_ref[...], sin_ref[...])
+        return jnp.concatenate(
+            [first * cos + second * sin, second * cos - first * sin], 0
+        ).astype(jnp.bfloat16)
 
     def part_copy(group, dist):
         return pltpu.make_async_remote_copy(
@@ -849,9 +1069,10 @@
             return matmul(kv_ref[dist, group, :HD, :], d_score)
 
         d_query = block(0, causal(tokens, valid))
-        dq_ref[rows, :] = lax.fori_loop(
+        d_query = lax.fori_loop(
             1, blocks, lambda dist, acc: acc + block(dist, dist < reach), d_query
         )
+        turned[rows, :] = unrotated(d_query)
 
         @pl.when(lax.rem(head, SHARE) == SHARE - 1)
         def _():
@@ -865,8 +1086,45 @@
                     parts[dist, group, HD:, :] = dv_acc[dist].T.astype(jnp.bfloat16)
                     part_copy(group, dist).start()
 
-    begin_down, complete_down = load_tile(down, down_ref, load_sems.at[0])
-    begin_proj, complete_proj = load_tile(proj, proj_ref, load_sems.at[1])
+    def settle():
+        for dist in range(1, seq_size):
+
+            @pl.when(seq + dist < seq_size)
+            def _():
+                for group in range(KV_HEADS):
+                    part_copy(group, dist).wait_recv()
+                dkv_ref[...] += parts_got[dist].astype(jnp.float32)
+
+            @pl.when(seq >= dist)
+            def _():
+                for group in range(KV_HEADS):
+                    part_copy(group, dist).wait_send()
+
+        for group in range(KV_HEADS):
+            place = (HEADS + group) * HD
+            turned[place : place + HD, :] = unrotated(dkv_ref[group, :HD, :])
+            place += KV_HEADS * HD
+            turned[place : place + HD, :] = dkv_ref[group, HD:, :].astype(jnp.bfloat16)
+        for chunk in range(turned.shape[0] // TILE):
+            part = slice(chunk * TILE, (chunk + 1) * TILE)
+            d_qkv_ref[:, part] = transposed(turned[part, :])
+
+    begin_down, complete_down = load_tile(down, down_ref, load_sems)
+
+    def begin_proj(tile):
+        columns = pl.ds(pl.multiple_of(tile * proj.columns, proj.columns), proj.columns)
+
+        def blocks_of(core, into):
+            @pl.loop(0, proj.size)
+            def _(block):
+                owner = apart(proj.dp, 2 * block + core, proj.hops + 1)
+                part = pl.ds(pl.multiple_of(owner * proj.depth, proj.depth), proj.depth)
+                into[block] = matmul(o_ref[part, :], branch_ref[:, columns]).astype(jnp.bfloat16)
+
+        blocks_of(1, proj.other)
+        proj.send(0, tile)
+        blocks_of(0, proj.own)
+
     steps = down.steps
     lag = steps - proj.steps
 
@@ -875,55 +1133,54 @@
         down.step(now, begin_down)
         proj.step(now - lag, begin_proj)
         complete_down(now)
-        complete_proj(now - lag)
-
-        @pl.loop(now * HEADS // steps, (now + 1) * HEADS // steps)
+
+        busy = down.tiles
+
+        @pl.loop(jnp.minimum(now, busy) * HEADS // busy, jnp.minimum(now + 1, busy) * HEADS // busy)
         def _(head):
             one_head(head)
 
+        @pl.when(now == busy + 1)
+        def _():
+            settle()
+
     down.finish()
     proj.finish()
-    for dist in range(1, seq_size):
-
-        @pl.when(seq + dist < seq_size)
-        def _():
-            for group in range(KV_HEADS):
-                part_copy(group, dist).wait_recv()
-            dkv_ref[...] += parts_got[dist].astype(jnp.float32)
-
-        @pl.when(seq >= dist)
-        def _():
-            for group in range(KV_HEADS):
-                part_copy(group, dist).wait_send()
-
-
-def attend_backward(info, query, kv, full, lse, grad, g_down, g_out, collective_id):
+
+
+def attend_backward(
+    layout, query, kv, full, lse, grad, attended, branch, cos, sin, squares, g_down, collective_id
+):
     tokens, reach = (query.shape[1], kv.shape[0])
-    seq_size = lax.axis_size("seq")
+    model = branch.shape[1]
+    dp_size, seq_size = (lax.axis_size("dp"), lax.axis_size("seq"))
+    width = (HEADS + 2 * KV_HEADS) * HD
     vmem = pl.BlockSpec(memory_space=pltpu.VMEM)
     hbm = pl.BlockSpec(memory_space=pl.ANY)
-    down_shape = (g_down.shape[0] // 2, g_down.shape[1], 256)
-    proj_shape = (g_out.shape[0] // 2, g_out.shape[1], 512)
+    down_shape = (dp_size // 2, g_down.shape[1], 256)
+    proj_shape = (dp_size // 2, HEADS * HD // dp_size, 256)
     return pl.pallas_call(
         backward_kernel,
         out_shape=[
-            jax.ShapeDtypeStruct(query.shape, jnp.float32),
-            jax.ShapeDtypeStruct((KV_HEADS, 2 * HD, tokens), jnp.float32),
-            jax.ShapeDtypeStruct((g_down.shape[1] // seq_size, g_down.shape[2]), jnp.float32),
-            jax.ShapeDtypeStruct((g_out.shape[1] // seq_size, g_out.shape[2]), jnp.float32),
+            jax.ShapeDtypeStruct((tokens, width), jnp.bfloat16),
+            jax.ShapeDtypeStruct((g_down.shape[1] // seq_size, model), jnp.float32),
+            jax.ShapeDtypeStruct((HEADS * HD // (dp_size * seq_size), model), jnp.float32),
+            jax.ShapeDtypeStruct((8, 128), jnp.float32),
         ],
-        in_specs=[pl.BlockSpec(memory_space=pltpu.SMEM)] + [vmem] * 5 + [hbm] * 2,
+        in_specs=[pl.BlockSpec(memory_space=pltpu.SMEM)] * 3 + [vmem] * 10 + [hbm],
         out_specs=[vmem] * 4,
         scratch_shapes=[
             pltpu.VMEM((reach, tokens, HD), jnp.bfloat16),
             pltpu.VMEM((reach, tokens, HD), jnp.bfloat16),
             pltpu.VMEM((reach, tokens, HD), jnp.float32),
             pltpu.VMEM((reach, tokens, HD), jnp.float32),
+            pltpu.VMEM((KV_HEADS, 2 * HD, tokens), jnp.float32),
+            pltpu.VMEM((width, tokens), jnp.bfloat16),
             pltpu.VMEM((reach, KV_HEADS, 2 * HD, tokens), jnp.bfloat16),
             pltpu.VMEM((reach, KV_HEADS, 2 * HD, tokens), jnp.bfloat16),
             pltpu.SemaphoreType.DMA((reach, KV_HEADS)),
             pltpu.SemaphoreType.DMA((reach, KV_HEADS)),
-            pltpu.SemaphoreType.DMA((2, g_down.shape[0])),
+            pltpu.SemaphoreType.DMA((dp_size,)),
             *Scatter.scratch(down_shape),
             *Scatter.scratch(proj_shape),
         ],
@@ -931,7 +1188,7 @@
             collective_id=collective_id, has_side_effects=True, vmem_limit_bytes=60 * 2**20
         ),
         name="attend_backward",
-    )(info, query, kv, full, lse, grad, g_down, g_out)
+    )(*layout, query, kv, full, lse, grad, attended, branch, cos, sin, squares, g_down)
 
 
 def everyone():
@@ -947,20 +1204,32 @@
 
 
 def last_kernel(
-    source, gains_ref, squares_ref,
-    result, gains_sum, total_ref,
-    load_sems, gains_got, mine, totals_got, tile_sends, tile_recvs, *scratch
+    rows_ref, turned_ref, d_qkv_ref, gain_ref, mlp_gain_ref, squares_ref, w_hbm, d_mid_hbm,
+    result, gains_sum, total_ref, input_grad_hbm,
+    w_buf, d_normed, d_mid, gains, gains_got, mine, totals_got,
+    load_sems, tile_sends, tile_recvs, *scratch
 ):
-    columns = scratch[0].shape[2]
+    tokens, model = rows_ref.shape
+    size, depth, columns = scratch[0].shape
     scatter = Scatter(
-        source.shape[2] // columns, scratch[0].shape, scratch, delivered(result, columns)
-    )
+        d_qkv_ref.shape[1] // columns, scratch[0].shape, scratch, delivered(result, columns, mine)
+    )
+    bits = scatter.hops + 1
     me, devices, device = everyone()
+    own = model // devices
+    chunks = model // TILE
+
+    def w_load(chunk, slot):
+        rows = pl.ds(pl.multiple_of(chunk * TILE, TILE), TILE)
+        return pltpu.make_async_copy(w_hbm.at[rows, :], w_buf.at[slot], load_sems.at[slot])
+
+    mid_load = pltpu.make_async_copy(d_mid_hbm, d_mid, load_sems.at[2])
+    input_store = pltpu.make_async_copy(d_mid, input_grad_hbm, load_sems.at[3])
 
     def copy(kind, distance):
         other, place = device(distance)
         return pltpu.make_async_remote_copy(
-            src_ref=mine if kind else gains_ref.at[other],
+            src_ref=mine if kind else gains.at[other * own // 128],
             dst_ref=(totals_got if kind else gains_got).at[distance],
             send_sem=tile_sends.at[kind, distance],
             recv_sem=tile_recvs.at[kind, distance],
@@ -968,6 +1237,10 @@
             device_id_type=MESH,
         )
 
+    mid_load.start()
+    w_load(0, 0).start()
+    gains[...] = jnp.zeros_like(gains)
+    mine[...] = squares_ref[...]
     barrier = pltpu.get_barrier_semaphore()
 
     @pl.loop(1, devices)
@@ -976,29 +1249,67 @@
 
     pl.semaphore_wait(barrier, devices - 1)
 
-    @pl.loop(1, devices)
-    def _(distance):
-        copy(0, distance).start()
-
-    begin, complete = load_tile(scatter, source, load_sems)
+    def begin(tile):
+        part_columns = pl.ds(pl.multiple_of(tile * columns, columns), columns)
+
+        def blocks_of(core, into):
+            @pl.loop(0, size)
+            def _(block):
+                owner = apart(scatter.dp, 2 * block + core, bits)
+                part = pl.ds(pl.multiple_of(owner * depth, depth), depth)
+                into[block] = matmul(turned_ref[part, :], d_qkv_ref[:, part_columns]).astype(
+                    jnp.bfloat16
+                )
+
+        blocks_of(1, scatter.other)
+        scatter.send(0, tile)
+        blocks_of(0, scatter.own)
+
+    def give(part, back):
+        d_mid[part, :] += back
 
     @pl.loop(0, scatter.steps)
     def _(now):
         scatter.step(now, begin)
-        complete(now)
+
+        @pl.when(now < chunks)
+        def _():
+            slot = lax.rem(now, 2)
+            w_load(now, slot).wait()
+
+            @pl.when(now + 1 < chunks)
+            def _():
+                w_load(now + 1, 1 - slot).start()
+
+            part = pl.ds(pl.multiple_of(now * TILE, TILE), TILE)
+            d_normed[:, part] = contract(d_qkv_ref[...], w_buf[slot], 1, 1)
+
+        @pl.when(now == chunks)
+        def _():
+            mid_load.wait()
+            gain_sum = norm_backward_rows(
+                lambda part: rows_ref[part, :].astype(jnp.float32), d_normed, gain_ref, give
+            )
+            input_store.start()
+            for chunk in range(model // 128):
+                part = slice(chunk * 128, (chunk + 1) * 128)
+                gains[chunk, 0:1, :] = gain_sum[:, part]
+                gains[chunk, 1:2, :] = mlp_gain_ref[:, part]
+
+            @pl.loop(1, devices)
+            def _(distance):
+                copy(0, distance).start()
 
     @pl.loop(1, devices)
     def _(distance):
         copy(0, distance).wait()
 
-    gains = gains_ref[me] + jnp.sum(gains_got[1:], 0)
-    gains_sum[...] = gains
-    lanes = result.shape[1] // 128
-    squares = squares_ref[...] + gains * gains
-    for lane in range(lanes):
-        block = result[:, lane * 128 : (lane + 1) * 128]
-        squares = squares + jnp.sum((block * block).reshape(-1, 8, 128), 0)
-    mine[...] = squares
+    lane = lax.broadcasted_iota(jnp.int32, (8, 128), 1)
+    first = lax.rem(me * own, 128)
+    total_gains = gains[me * own // 128] + jnp.sum(gains_got[1:], 0)
+    total_gains = jnp.where((lane >= first) & (lane < first + own), total_gains, 0.0)
+    gains_sum[...] = total_gains
+    mine[...] += total_gains * total_gains
 
     @pl.loop(1, devices)
     def _(distance):
@@ -1008,40 +1319,49 @@
     def _(distance):
         copy(1, distance).wait()
 
-    total = jnp.sum(squares + jnp.sum(totals_got[1:], 0))
+    total = jnp.sum(mine[...] + jnp.sum(totals_got[1:], 0))
     total_ref[...] = jnp.full((8, 128), total, jnp.float32)
+    input_store.wait()
     scatter.finish()
 
 
-def last_sums(parts, gains, squares, columns, collective_id):
-    devices = gains.shape[0]
-    shape = (parts.shape[0] // 2, parts.shape[1], columns)
+def last_sums(
+    rows, turned, d_qkv, gain, mlp_gain, squares, weight, d_mid, columns, collective_id
+):
+    tokens, model = rows.shape
+    dp_size, seq_size = (lax.axis_size("dp"), lax.axis_size("seq"))
+    devices = dp_size * seq_size
+    shape = (dp_size // 2, model // dp_size, columns)
     vmem = pl.BlockSpec(memory_space=pltpu.VMEM)
+    hbm = pl.BlockSpec(memory_space=pl.ANY)
     return pl.pallas_call(
         last_kernel,
         out_shape=[
-            jax.ShapeDtypeStruct(
-                (parts.shape[1] // lax.axis_size("seq"), parts.shape[2]), jnp.float32
-            ),
+            jax.ShapeDtypeStruct((model // devices, d_qkv.shape[1]), jnp.float32),
             jax.ShapeDtypeStruct((8, 128), jnp.float32),
             jax.ShapeDtypeStruct((8, 128), jnp.float32),
+            jax.ShapeDtypeStruct((tokens, model), jnp.float32),
         ],
-        in_specs=[pl.BlockSpec(memory_space=pl.ANY), vmem, vmem],
-        out_specs=[vmem] * 3,
+        in_specs=[vmem] * 6 + [hbm] * 2,
+        out_specs=[vmem] * 3 + [hbm],
         scratch_shapes=[
-            pltpu.SemaphoreType.DMA((parts.shape[0],)),
+            pltpu.VMEM((2, TILE, d_qkv.shape[1]), jnp.bfloat16),
+            pltpu.VMEM((tokens, model), jnp.float32),
+            pltpu.VMEM((tokens, model), jnp.float32),
+            pltpu.VMEM((model // 128, 8, 128), jnp.float32),
             pltpu.VMEM((devices, 8, 128), jnp.float32),
             pltpu.VMEM((8, 128), jnp.float32),
             pltpu.VMEM((devices, 8, 128), jnp.float32),
+            pltpu.SemaphoreType.DMA((4,)),
             pltpu.SemaphoreType.DMA((2, devices)),
             pltpu.SemaphoreType.DMA((2, devices)),
             *Scatter.scratch(shape),
         ],
         compiler_params=pltpu.CompilerParams(
-            collective_id=collective_id, has_side_effects=True, vmem_limit_bytes=48 * 2**20
+            collective_id=collective_id, has_side_effects=True, vmem_limit_bytes=56 * 2**20
         ),
         name="last_sums",
-    )(parts, gains, squares)
+    )(rows, turned, d_qkv, gain, mlp_gain, squares, weight, d_mid)
 
 
 def per_device(
@@ -1067,71 +1387,34 @@
     gain_v,
 ):
     tok_dev = hidden_in.shape[0]
-    q_width = HEADS * HD
-    kv_width = KV_HEADS * HD
-    seg_all = segment_ids[0]
-    lengths = seq_lengths[0]
-    seq_index = lax.axis_index("seq")
-    offset = seq_index * tok_dev
-    seg_local = lax.dynamic_slice_in_dim(seg_all, offset, tok_dev, 0)
-    starts = jnp.cumsum(lengths, dtype=jnp.int32) - lengths
-    slot_ids = jnp.arange(lengths.shape[0], dtype=jnp.int32)
-    seq_start = jnp.sum(
-        jnp.where(seg_local[:, None] == slot_ids[None, :], starts[None, :], 0),
-        axis=1,
-        dtype=jnp.int32,
-    )
-    positions = offset + jnp.arange(tok_dev, dtype=jnp.int32) - seq_start
-    cos_table, sin_table = rope_tables(positions)
-    valid = (seg_local[0] < seq_counts[0]).astype(jnp.int32)
-    reach = jnp.where(valid > 0, seq_index - seq_start[0] // tok_dev + 1, 1)
-    info = jnp.stack([reach, valid]).astype(jnp.int32)
-
+    layout = (seq_lengths, seq_counts, segment_ids)
     devices = lax.axis_size("dp") * lax.axis_size("seq")
     own = norm_gains.shape[1]
-    gain_rows = jnp.pad(norm_gains.astype(jnp.bfloat16), ((0, 14), (0, 128 - own)))
-    width = qkv_weight.shape[1] // 4
+    gain_rows = jnp.pad(norm_gains, ((0, 14), (0, 128 - own)))
     model = out_weight.shape[1]
     seq_size = lax.axis_size("seq")
-    gu_shard = gate_up_weight.astype(jnp.bfloat16)
+    down_depth = down_weight.shape[0]
+    spare = -down_depth % 16
+    down_shard = jnp.pad(down_weight, ((0, spare), (0, 0))) if spare else down_weight
     early = 3 * TILE
-    w_qkv, gain_rows, gu_block = gather_all(
+    shards, (w_qkv, gain_rows, gu_block) = gather_all(
         [WHOLE, WHOLE, ROWS],
-        [qkv_weight.astype(jnp.bfloat16), gain_rows, gu_shard],
+        [qkv_weight, gain_rows, gate_up_weight, out_weight, down_shard],
         [
-            (devices * qkv_weight.shape[0], 4 * width),
+            (devices * qkv_weight.shape[0], qkv_weight.shape[1]),
             (devices * 16, 128),
-            (seq_size * gu_shard.shape[0], 2 * early),
+            (seq_size * gate_up_weight.shape[0], 2 * early),
         ],
         [
             (1, 1, ((0, 0, 128),)),
-            (0, 0, ((0, 0, width), (width, width, width))),
-            (0, 0, ((2 * width, 2 * width, width), (3 * width, 3 * width, width))),
+            (0, 0, ((0, 0, 512), (512, 512, 384))),
+            (0, 0, ((896, 896, 384), (1280, 1280, 512))),
+            (0, 0, ((1792, 1792, 384), (2176, 2176, 384))),
             (2, 2, ((0, 0, early), (FF, early, early))),
         ],
         1,
     )
-    w_gain = jnp.moveaxis(gain_rows.reshape(devices, 16, 128)[:, :2, :own], 1, 0).reshape(2, -1)
-    gain_attn = w_gain[0].astype(jnp.float32)
-    gain_mlp = w_gain[1].astype(jnp.float32)
-    residual = hidden_in.astype(jnp.float32)
-    inv_one, normed = norm_forward(residual, gain_attn)
-    normed_low = normed.astype(jnp.bfloat16)
-    qkv_out = contract(w_qkv, normed_low, 0, 1)
-    query = rotate(qkv_out[:q_width], cos_table, sin_table).astype(jnp.bfloat16)
-    key = rotate(qkv_out[q_width : q_width + kv_width], cos_table, sin_table).astype(jnp.bfloat16)
-    value = qkv_out[q_width + kv_width :].astype(jnp.bfloat16)
-    kv_own = jnp.concatenate(
-        [key.reshape(KV_HEADS, HD, tok_dev), value.reshape(KV_HEADS, HD, tok_dev)], 1
-    )
-    down_depth = down_weight.shape[0]
-    spare = -down_depth % 16
-    shards = [
-        out_weight.astype(jnp.bfloat16),
-        jnp.pad(down_weight.astype(jnp.bfloat16), ((0, spare), (0, 0))),
-        gu_shard,
-        gu_block,
-    ]
+    shards = [shards[3], shards[4], shards[2], gu_block]
     shapes = [(devices * shard.shape[0], shard.shape[1]) for shard in shards[:3]]
     half, quarter = (model // 2, model // 4)
     pieces = [
@@ -1143,51 +1426,41 @@
     for low, high in ((3, 6), (6, 9), (9, 10), (10, 11)):
         low, high = (low * TILE, high * TILE)
         pieces.append((2, 2, ((low, low, high - low), (FF + low, FF + low, high - low))))
-    (attended, attended_full, lse, kv_all), (w_out, w_down, w_gu) = attend_forward(
-        info, query, kv_own, [WHOLE, WHOLE, WHOLE, BLOCKS], shards, shapes, pieces, 2
+    forward, (w_out, w_down, w_gu) = attend_forward(
+        layout, hidden_in, gain_rows, w_qkv, [WHOLE, WHOLE, WHOLE, BLOCKS], shards, shapes, pieces, 2
     )
     if spare:
         w_down = w_down.reshape(devices, -1, model)[:, :down_depth].reshape(-1, model)
-    mid_rows = residual + contract(attended, w_out, 0, 0)
-    inv_two, normed_two = norm_forward(mid_rows, gain_mlp)
-    inner_rows = normed_two.astype(jnp.bfloat16)
-
-    g_down, d_inner, out_rows, g_gu_own = feed_forward(
-        inner_rows, inner_rows.T, out_grad, w_gu, w_down, 3
-    )
-    block_out = (mid_rows + out_rows).astype(jnp.bfloat16)
-    back_two, g_gain_two = norm_backward(mid_rows, inv_two, gain_mlp, d_inner)
-    d_mid = out_grad.astype(jnp.float32) + back_two
-    d_branch = d_mid.astype(jnp.bfloat16)
-    d_attended = contract(w_out, d_branch, 1, 1).astype(jnp.bfloat16)
+    query, attended, attended_full, lse, kv_all, mid_rows, inner_rows, turned = forward[:8]
+    normed, gain_one, gain_two, cos, sin = forward[8:]
+    g_down, d_mid, d_branch, block_out, d_attended, g_gain_two, g_gu_own, squares = feed_forward(
+        inner_rows, turned, gain_two, out_grad, mid_rows, w_gu, w_down, w_out, 3
+    )
     dp_size = lax.axis_size("dp")
     if spare:
         g_down = jnp.pad(
             g_down.reshape(devices, down_depth, model), ((0, 0), (0, spare), (0, 0))
         )
     g_down = g_down.reshape(dp_size, -1, model)
-    g_out = matmul(attended, d_branch).astype(jnp.bfloat16).reshape(dp_size, -1, model)
-    d_query, d_kv, g_down_own, g_out_own = attend_backward(
-        info, query, kv_all, attended_full, lse, d_attended, g_down, g_out, 4
+    d_qkv, g_down_own, g_out_own, squares = attend_backward(
+        layout, query, kv_all, attended_full, lse, d_attended,
+        attended, d_branch, cos, sin, squares, g_down, 4,
     )
     g_down_own = g_down_own[:down_depth]
-    d_qkv = jnp.concatenate(
-        [
-            rotate(d_query, cos_table, -sin_table),
-            rotate(d_kv[:, :HD].reshape(kv_width, tok_dev), cos_table, -sin_table),
-            d_kv[:, HD:].reshape(kv_width, tok_dev),
-        ],
-        0,
-    ).astype(jnp.bfloat16)
-    d_normed = contract(d_qkv, w_qkv, 0, 1)
-    back_one, g_gain_one = norm_backward(residual, inv_one, gain_attn, d_normed)
-    input_grad = d_mid + back_one
-    g_qkv = contract(normed_low, d_qkv, 0, 1).astype(jnp.bfloat16).reshape(dp_size, -1, 4 * width)
-    g_gains = jnp.stack([g_gain_one, g_gain_two], 0).reshape(2, devices, own)
-    g_gains = jnp.pad(jnp.moveaxis(g_gains, 0, 1), ((0, 0), (0, 6), (0, 128 - own)))
-    squares = squares_of(g_gu_own) + squares_of(g_down_own) + squares_of(g_out_own)
-    g_qkv_own, g_gains_own, total_sq = last_sums(g_qkv, g_gains, squares, 512, 5)
-    g_gains_own = g_gains_own[:2, :own]
+    g_qkv_own, g_gains_own, total_sq, input_grad = last_sums(
+        hidden_in,
+        normed,
+        d_qkv,
+        gain_one,
+        g_gain_two,
+        squares,
+        w_qkv,
+        d_mid,
+        512,
+        5,
+    )
+    place = (lax.axis_index("dp") * seq_size + lax.axis_index("seq")) * own % 128
+    g_gains_own = lax.dynamic_slice(g_gains_own, (0, place), (2, own))
     grad_norm = jnp.sqrt(total_sq[0, 0])
     clip_factor = jnp.minimum(1.0, CLIP_NORM / (grad_norm + 1e-06))
     new_qkv, new_qkv_m, new_qkv_v = adam_update(

time: 1130 us -> 949 us (0.84)
  matrix products: 56.5 us -> 0 us
  Pallas kernels: 953 us -> 897 us
  other arithmetic: 59.1 us -> 16.3 us
  local copies, waits for them, and re-layouts: 42.9 us -> 23.2 us
    dot_general x6 -> x0, matrix products: 56.5 us -> none  [the longest x5 49.7 us: contract(): lax.dot_general(left, right, (((left_dim,), (right_dim,)), ((), ())), pre...]
    pallas_call x1, Pallas kernels: 267 us -> 224 us  [feed_forward(): pl.pallas_call(mlp_kernel, out_shape=[jax.ShapeDtypeStruct((FF, model), j...]
    pallas_call x3, Pallas kernels: 346 us -> 328 us  [the longest x1 185 us: attend_backward(): pl.pallas_call(backward_kernel, out_shape=[jax.ShapeDtypeStruct((tokens,...]
where the time goes in v4:
time: 949 us; the launch traced here: 940 us
  Pallas kernels  897 us (95%)
  local copies, waits for them, and re-layouts  23.2 us (2%)
  other arithmetic  16.3 us (2%)
    pallas_call x1, Pallas kernels, attend_forward(): pl.pallas_call(functools.partial(attend_kernel, kinds, pieces), out_shape...  345 us
    pallas_call x1, Pallas kernels, feed_forward(): pl.pallas_call(mlp_kernel, out_shape=[jax.ShapeDtypeStruct((FF, model), j...  224 us
    pallas_call x1, Pallas kernels, attend_backward(): pl.pallas_call(backward_kernel, out_shape=[jax.ShapeDtypeStruct((tokens,...  185 us
    pallas_call x1, Pallas kernels, last_sums(): pl.pallas_call(last_kernel, out_shape=[jax.ShapeDtypeStruct((model // dev...  77.6 us
    pallas_call x1, Pallas kernels, gather_all(): pl.pallas_call(functools.partial(gather_kernel, kinds, pieces, count), ou...  66.1 us
    unnamed x58, local copies, waits for them, and re-layouts  21.3 us

profile of v4, /device:TPU:0, one launch (start us, length us, event | category | flops | bytes accessed | tf_op | source)
XLA Modules:
  0.0 940.3 jit_solution(13582086280915714068)
XLA Ops:
  0.7 0.7 pad.4.refs_1_
  1.3 1.8 copy-done.1
  3.2 1.4 copy-done.3
  4.5 1.1 copy-done.5
  5.6 1.0 copy-done.7
  6.6 66.1 %gather.1 = (bf16[64,2560]{1,0:T(8,128)(2,1)}, bf16[16,128]{1,0:T(8,128)(2,1)}, bf16[64,11264]{1,0:T(8,128)(2,1)S(1)}, bf16[64,2048]{1,0:T(8,128)(2,1)S(1)}, bf1...) custom-call(f32[64,2560]{1,0:T(8,128)S(1)} %copy-done.5, ...), custom_call_target="tpu_custom_call" | custom-call | tf_op jit(solution)/shard_map/gather/pallas_call | solution.py:273
  72.8 0.0 copy-start
  72.8 4.0 copy-done
  76.8 1.1 copy-done.9
  77.9 1.1 copy-done.10
  79.0 0.9 copy-done.11
  79.9 0.7 copy-done.12
  80.6 0.7 copy-done.13
  81.9 344.7 %attend_forward.1 = (bf16[2048,512]{1,0:T(8,128)(2,1)}, bf16[2048,512]{1,0:T(8,128)(2,1)}, f32[2048,512]{1,0:T(8,128)}, f32[32,1,512]{2,1,0:T(1,128)}, bf16[4,4,...) custom-call(s32[1,2]{1,0:T(1,128)} %lengths.3, ...), custom_call_target="tpu_custom_call" | custom-call | tf_op jit(solution)/shard_map/attend_forward/pallas_call | solution.py:502
  426.6 224.2 %feed_forward.1 = (bf16[5632,2048]{1,0:T(8,128)(2,1)}, f32[512,2048]{1,0:T(8,128)}, bf16[512,2048]{1,0:T(8,128)(2,1)}, bf16[512,2048]{1,0:T(8,128)(2,1)}, bf16[2...) custom-call(bf16[512,2048]{1,0:T(8,128)(2,1)} %get-tuple-element.62.rows_ref, ...), custom_call_target="tpu_custom_call" | custom-call | tf_op jit(solution)/shard_map/feed_forward/pallas_call | solution.py:925
  650.8 184.6 %attend_backward.1 = (bf16[512,2560]{1,0:T(8,128)(2,1)}, f32[176,2048]{1,0:T(8,128)}, f32[64,2048]{1,0:T(8,128)}, f32[8,128]{1,0:T(8,128)}) custom-call(s32[1,2]{1,0:T(1,128)} %lengths.3, s32[1]{0:T(128)S(6)} %copy.40.counts, s32[1,2048]{1,0:T(1,128)} %segments.3, bf16[2048,512]{1,0:T(8,128)(2,1)} %get-tuple-element.71.q_ref, ...), custom_call_target="tpu_custom_call" | custom-call | tf_op jit(solution)/shard_map/attend_backward/pallas_call | solution.py:1162
  835.4 0.0 copy-start.25
  835.4 0.0 copy-start.26
  835.4 0.0 copy-start.27
  835.4 0.0 copy-start.4
  835.4 0.0 copy-start.18
  835.4 77.6 %last_sums.1 = (f32[64,2560]{1,0:T(8,128)}, f32[8,128]{1,0:T(8,128)}, f32[8,128]{1,0:T(8,128)}, f32[512,2048]{1,0:T(8,128)}) custom-call(bf16[512,2048]{1,0:T(8,128)(2,1)} %rows_ref.1, bf16[2048,512]{1,0:T(8,128)(2,1)} %get-tuple-element.70.turned_ref, bf16[512,2560]{1,0:T(8,128)(2,1)} %get-tuple-element.82.d_qkv_ref, f32[1,2048]{1,0:T(1,128)} %get-tuple-element.83.gain_ref, ...), custom_call_target="tpu_custom_call" | custom-call | tf_op jit(solution)/shard_map/last_sums/pallas_call | solution.py:1337
  913.1 1.2 slice.3
  915.0 0.0 copy-done.25
  915.0 0.0 copy-done.26
  915.0 0.0 copy-done.27
  915.0 1.3 multiply_subtract_fusion.4
  916.4 0.0 copy-done.4
  916.4 0.0 copy-done.18
  916.4 0.0 copy-start.15
  916.4 0.0 copy-start.16
  916.4 4.9 multiply_subtract_fusion.1
  921.3 0.0 copy-done.2
  921.3 0.0 copy-done.15
  921.3 1.1 copy-done.16
  922.4 7.1 multiply_subtract_fusion
  929.5 0.0 copy-done.8
  929.5 0.0 copy-done.22
  929.5 0.0 copy-done.23
  929.5 1.4 multiply_subtract_fusion.3
  931.0 0.1 copy-done.19
  931.1 0.4 copy-done.20
  931.5 0.2 copy-done.21
  931.7 1.6 multiply_subtract_fusion.2
  933.3 0.7 copy-done.17
  934.0 1.3 copy.41
  935.3 1.6 copy-done.14
  937.0 2.0 copy.42
  (22 shorter events, 0.0 us)
Async XLA Ops:
  1.3 1.8 copy-start.1
  3.2 1.4 copy-start.3
  4.5 1.1 copy-start.5
  5.6 1.0 copy-start.7
  72.8 4.0 copy-start
  76.8 1.1 copy-start.9
  77.9 1.1 copy-start.10
  79.0 0.9 copy-start.11
  79.9 0.7 copy-start.12
  80.6 0.7 copy-start.13
  835.4 79.6 %copy-start.25 = (f32[2,64]{1,0:T(2,128)S(1)}, f32[2,64]{1,0:T(2,128)}, u32[]{:S(2)}) copy-start(f32[2,64]{1,0:T(2,128)} %param.37) | copy-start | bytes 1540
  835.4 79.6 %copy-start.26 = (f32[2,64]{1,0:T(2,128)S(1)}, f32[2,64]{1,0:T(2,128)}, u32[]{:S(2)}) copy-start(f32[2,64]{1,0:T(2,128)} %param.38) | copy-start | bytes 1540
  835.4 79.6 %copy-start.27 = (f32[2,64]{1,0:T(2,128)S(1)}, f32[2,64]{1,0:T(2,128)}, u32[]{:S(2)}) copy-start(f32[2,64]{1,0:T(2,128)} %param.39) | copy-start | bytes 1540
  835.4 81.0 %copy-start.4 = (f32[176,2048]{1,0:T(8,128)S(1)}, f32[176,2048]{1,0:T(8,128)}, u32[]{:S(2)}) copy-start(f32[176,2048]{1,0:T(8,128)} %refs_4_.1) | copy-start | bytes 4325380
  835.4 81.0 %copy-start.18 = (f32[176,2048]{1,0:T(8,128)S(1)}, f32[176,2048]{1,0:T(8,128)}, u32[]{:S(2)}) copy-start(f32[176,2048]{1,0:T(8,128)} %param.35) | copy-start | bytes 4325380
  916.4 4.9 copy-start.2
  916.4 4.9 copy-start.15
  916.4 6.0 copy-start.16
  922.4 7.1 copy-start.8
  922.4 7.1 copy-start.22
  922.4 7.1 copy-start.23
  922.4 7.1 copy-start.24
  929.5 1.5 copy-start.6
  929.5 1.6 copy-start.19
  929.5 2.0 copy-start.20
  929.5 2.2 copy-start.21
  931.7 2.3 copy-start.17
  934.0 2.9 copy-start.14

commit v5 on v4

--- a/solution.py
+++ b/solution.py
@@ -278,7 +278,7 @@
         out_specs=[vmem] * count + [hbm] * len(shapes),
         scratch_shapes=gather_scratch(len(pieces)),
         compiler_params=pltpu.CompilerParams(
-            collective_id=collective_id, has_side_effects=True, vmem_limit_bytes=32 * 2**20
+            collective_id=collective_id, has_side_effects=True, vmem_limit_bytes=60 * 2**20
         ),
         name="gather",
     )(*shards)
@@ -1134,13 +1134,16 @@
         proj.step(now - lag, begin_proj)
         complete_down(now)
 
-        busy = down.tiles
-
-        @pl.loop(jnp.minimum(now, busy) * HEADS // busy, jnp.minimum(now + 1, busy) * HEADS // busy)
+        busy, first = (down.tiles, 2)
+
+        def heads_before(step):
+            return jnp.minimum(jnp.maximum(step - first, 0), busy) * HEADS // busy
+
+        @pl.loop(heads_before(now), heads_before(now + 1))
         def _(head):
             one_head(head)
 
-        @pl.when(now == busy + 1)
+        @pl.when(now == first + busy)
         def _():
             settle()
 

time: 949 us -> 934 us (0.984)
  local copies, waits for them, and re-layouts: 23.2 us -> 10 us
    unnamed x58 -> x38, local copies, waits for them, and re-layouts: 21.3 us -> 7.55 us
    pallas_call x1, Pallas kernels: 185 us -> 175 us  [attend_backward(): pl.pallas_call(backward_kernel, out_shape=[jax.ShapeDtypeStruct((tokens,...]
where the time goes in v5:
time: 934 us; the launch traced here: 924 us
  Pallas kernels  894 us (96%)
  other arithmetic  16.3 us (2%)
  local copies, waits for them, and re-layouts  10 us (1%)
    pallas_call x1, Pallas kernels, attend_forward(): pl.pallas_call(functools.partial(attend_kernel, kinds, pieces), out_shape...  345 us
    pallas_call x1, Pallas kernels, feed_forward(): pl.pallas_call(mlp_kernel, out_shape=[jax.ShapeDtypeStruct((FF, model), j...  225 us
    pallas_call x1, Pallas kernels, attend_backward(): pl.pallas_call(backward_kernel, out_shape=[jax.ShapeDtypeStruct((tokens,...  175 us
    pallas_call x1, Pallas kernels, last_sums(): pl.pallas_call(last_kernel, out_shape=[jax.ShapeDtypeStruct((model // dev...  80.1 us
    pallas_call x1, Pallas kernels, gather_all(): pl.pallas_call(functools.partial(gather_kernel, kinds, pieces, count), ou...  69.9 us

profile of v5, /device:TPU:0, one launch (start us, length us, event | category | flops | bytes accessed | tf_op | source)
XLA Modules:
  0.0 923.9 jit_solution(8431933870653382102)
XLA Ops:
  0.7 1.3 pad.4.refs_1_
  1.9 69.9 %gather.1 = (bf16[64,2560]{1,0:T(8,128)(2,1)}, bf16[16,128]{1,0:T(8,128)(2,1)}, bf16[64,11264]{1,0:T(8,128)(2,1)}, bf16[64,2048]{1,0:T(8,128)(2,1)}, bf16[176,20...) custom-call(f32[64,2560]{1,0:T(8,128)} %refs_0_.1, ...), custom_call_target="tpu_custom_call" | custom-call | tf_op jit(solution)/shard_map/gather/pallas_call | solution.py:273
  72.5 344.7 %attend_forward.1 = (bf16[2048,512]{1,0:T(8,128)(2,1)}, bf16[2048,512]{1,0:T(8,128)(2,1)}, f32[2048,512]{1,0:T(8,128)}, f32[32,1,512]{2,1,0:T(1,128)}, bf16[4,4,...) custom-call(s32[1,2]{1,0:T(1,128)} %lengths.3, ...), custom_call_target="tpu_custom_call" | custom-call | tf_op jit(solution)/shard_map/attend_forward/pallas_call | solution.py:502
  417.2 224.6 %feed_forward.1 = (bf16[5632,2048]{1,0:T(8,128)(2,1)}, f32[512,2048]{1,0:T(8,128)}, bf16[512,2048]{1,0:T(8,128)(2,1)}, bf16[512,2048]{1,0:T(8,128)(2,1)}, bf16[2...) custom-call(bf16[512,2048]{1,0:T(8,128)(2,1)} %get-tuple-element.62.rows_ref, ...), custom_call_target="tpu_custom_call" | custom-call | tf_op jit(solution)/shard_map/feed_forward/pallas_call | solution.py:925
  641.8 174.7 %attend_backward.1 = (bf16[512,2560]{1,0:T(8,128)(2,1)}, f32[176,2048]{1,0:T(8,128)}, f32[64,2048]{1,0:T(8,128)}, f32[8,128]{1,0:T(8,128)}) custom-call(s32[1,2]{1,0:T(1,128)} %lengths.3, s32[1]{0:T(128)S(6)} %copy.40.counts, s32[1,2048]{1,0:T(1,128)} %segments.3, bf16[2048,512]{1,0:T(8,128)(2,1)} %get-tuple-element.71.q_ref, ...), custom_call_target="tpu_custom_call" | custom-call | tf_op jit(solution)/shard_map/attend_backward/pallas_call | solution.py:1165
  816.5 0.0 copy-start.15
  816.5 0.0 copy-start.16
  816.5 0.0 copy-start.17
  816.5 0.0 copy-start.1
  816.5 0.0 copy-start.8
  816.6 80.1 %last_sums.1 = (f32[64,2560]{1,0:T(8,128)}, f32[8,128]{1,0:T(8,128)}, f32[8,128]{1,0:T(8,128)}, f32[512,2048]{1,0:T(8,128)}) custom-call(bf16[512,2048]{1,0:T(8,128)(2,1)} %rows_ref.1, bf16[2048,512]{1,0:T(8,128)(2,1)} %get-tuple-element.70.turned_ref, bf16[512,2560]{1,0:T(8,128)(2,1)} %get-tuple-element.82.d_qkv_ref, f32[1,2048]{1,0:T(1,128)} %get-tuple-element.83.gain_ref, ...), custom_call_target="tpu_custom_call" | custom-call | tf_op jit(solution)/shard_map/last_sums/pallas_call | solution.py:1340
  896.7 1.2 slice.3
  898.7 0.0 copy-done.15
  898.7 0.0 copy-done.16
  898.7 0.0 copy-done.17
  898.7 1.3 multiply_subtract_fusion.4
  900.0 0.0 copy-done.1
  900.0 0.0 copy-done.8
  900.0 0.0 copy-start
  900.0 0.0 copy-start.3
  900.1 0.0 copy-start.4
  900.1 4.9 multiply_subtract_fusion.1
  904.9 0.0 copy-done
  904.9 0.0 copy-done.3
  904.9 1.1 copy-done.4
  906.0 0.0 copy-start.7
  906.0 0.0 copy-start.12
  906.0 0.0 copy-start.13
  906.0 0.0 copy-start.14
  906.0 7.1 multiply_subtract_fusion
  913.1 0.0 copy-start.5
  913.1 0.0 copy-start.9
  913.1 0.0 copy-start.10
  913.1 0.0 copy-start.11
  913.1 0.0 copy-done.7
  913.1 0.0 copy-done.12
  913.1 0.0 copy-done.13
  913.2 0.0 copy-done.14
  913.2 1.4 multiply_subtract_fusion.3
  914.6 0.0 copy-done.5
  914.6 0.1 copy-done.9
  914.7 0.4 copy-done.10
  915.2 0.2 copy-done.11
  915.4 1.6 multiply_subtract_fusion.2
  917.0 0.7 copy-done.6
  917.7 1.3 copy.41
  919.0 1.6 copy-done.2
  920.6 2.0 copy.42
  (2 shorter events, 0.0 us)
Async XLA Ops:
  816.5 82.2 %copy-start.15 = (f32[2,64]{1,0:T(2,128)S(1)}, f32[2,64]{1,0:T(2,128)}, u32[]{:S(2)}) copy-start(f32[2,64]{1,0:T(2,128)} %param.37) | copy-start | bytes 1540
  816.5 82.2 %copy-start.16 = (f32[2,64]{1,0:T(2,128)S(1)}, f32[2,64]{1,0:T(2,128)}, u32[]{:S(2)}) copy-start(f32[2,64]{1,0:T(2,128)} %param.38) | copy-start | bytes 1540
  816.5 82.2 %copy-start.17 = (f32[2,64]{1,0:T(2,128)S(1)}, f32[2,64]{1,0:T(2,128)}, u32[]{:S(2)}) copy-start(f32[2,64]{1,0:T(2,128)} %param.39) | copy-start | bytes 1540
  816.5 83.5 %copy-start.1 = (f32[176,2048]{1,0:T(8,128)S(1)}, f32[176,2048]{1,0:T(8,128)}, u32[]{:S(2)}) copy-start(f32[176,2048]{1,0:T(8,128)} %refs_4_.1) | copy-start | bytes 4325380
  816.5 83.5 %copy-start.8 = (f32[176,2048]{1,0:T(8,128)S(1)}, f32[176,2048]{1,0:T(8,128)}, u32[]{:S(2)}) copy-start(f32[176,2048]{1,0:T(8,128)} %param.35) | copy-start | bytes 4325380
  900.0 4.9 copy-start
  900.0 4.9 copy-start.3
  900.1 6.0 copy-start.4
  906.0 7.1 copy-start.7
  906.0 7.1 copy-start.12
  906.0 7.1 copy-start.13
  906.0 7.1 copy-start.14
  913.1 1.5 copy-start.5
  913.1 1.6 copy-start.9
  913.1 2.0 copy-start.10
  913.1 2.2 copy-start.11
  915.4 2.3 copy-start.6
  917.7 2.9 copy-start.2

commit v6 on v5

--- a/solution.py
+++ b/solution.py
@@ -964,7 +964,7 @@
             pl.multiple_of(tile * scatter.columns, scatter.columns), scatter.columns
         )
         result = []
-        for block in range(2 * scatter.size):
+        for block in (*range(1, 2 * scatter.size, 2), *range(0, 2 * scatter.size, 2)):
             owner = apart(scatter.dp, block, scatter.hops + 1)
             into = scatter.other if block % 2 else scatter.own
             result.append(
@@ -981,11 +981,17 @@
     def complete(now):
         @pl.when((now >= 0) & (now < scatter.tiles))
         def _():
-            for copy in copies(now):
+            for copy in copies(now)[: scatter.size]:
                 copy.wait()
             scatter.send(0, now)
 
-    return (begin, complete)
+    def settle_own(now):
+        @pl.when((now >= 0) & (now < scatter.tiles))
+        def _():
+            for copy in copies(now)[scatter.size :]:
+                copy.wait()
+
+    return (begin, complete, settle_own)
 
 
 def delivered(ref, columns, squares):
@@ -1109,7 +1115,7 @@
             part = slice(chunk * TILE, (chunk + 1) * TILE)
             d_qkv_ref[:, part] = transposed(turned[part, :])
 
-    begin_down, complete_down = load_tile(down, down_ref, load_sems)
+    begin_down, complete_down, own_down = load_tile(down, down_ref, load_sems)
 
     def begin_proj(tile):
         columns = pl.ds(pl.multiple_of(tile * proj.columns, proj.columns), proj.columns)
@@ -1142,6 +1148,8 @@
         @pl.loop(heads_before(now), heads_before(now + 1))
         def _(head):
             one_head(head)
+
+        own_down(now)
 
         @pl.when(now == first + busy)
         def _():

time: 934 us -> 934 us (level)
  no operation moved by 1% of the time
where the time goes in v6:
time: 934 us; the launch traced here: 924 us
  Pallas kernels  894 us (96%)
  other arithmetic  16.3 us (2%)
  local copies, waits for them, and re-layouts  10 us (1%)
    pallas_call x1, Pallas kernels, attend_forward(): pl.pallas_call(functools.partial(attend_kernel, kinds, pieces), out_shape...  345 us
    pallas_call x1, Pallas kernels, feed_forward(): pl.pallas_call(mlp_kernel, out_shape=[jax.ShapeDtypeStruct((FF, model), j...  225 us
    pallas_call x1, Pallas kernels, attend_backward(): pl.pallas_call(backward_kernel, out_shape=[jax.ShapeDtypeStruct((tokens,...  175 us
    pallas_call x1, Pallas kernels, last_sums(): pl.pallas_call(last_kernel, out_shape=[jax.ShapeDtypeStruct((model // dev...  80.2 us
    pallas_call x1, Pallas kernels, gather_all(): pl.pallas_call(functools.partial(gather_kernel, kinds, pieces, count), ou...  69.9 us

profile of v6, /device:TPU:0, one launch (start us, length us, event | category | flops | bytes accessed | tf_op | source)
XLA Modules:
  0.0 924.0 jit_solution(4463336530946517168)
XLA Ops:
  0.7 1.3 pad.4.refs_1_
  1.9 69.9 %gather.1 = (bf16[64,2560]{1,0:T(8,128)(2,1)}, bf16[16,128]{1,0:T(8,128)(2,1)}, bf16[64,11264]{1,0:T(8,128)(2,1)}, bf16[64,2048]{1,0:T(8,128)(2,1)}, bf16[176,20...) custom-call(f32[64,2560]{1,0:T(8,128)} %refs_0_.1, ...), custom_call_target="tpu_custom_call" | custom-call | tf_op jit(solution)/shard_map/gather/pallas_call | solution.py:273
  72.5 344.7 %attend_forward.1 = (bf16[2048,512]{1,0:T(8,128)(2,1)}, bf16[2048,512]{1,0:T(8,128)(2,1)}, f32[2048,512]{1,0:T(8,128)}, f32[32,1,512]{2,1,0:T(1,128)}, bf16[4,4,...) custom-call(s32[1,2]{1,0:T(1,128)} %lengths.3, ...), custom_call_target="tpu_custom_call" | custom-call | tf_op jit(solution)/shard_map/attend_forward/pallas_call | solution.py:502
  417.2 224.6 %feed_forward.1 = (bf16[5632,2048]{1,0:T(8,128)(2,1)}, f32[512,2048]{1,0:T(8,128)}, bf16[512,2048]{1,0:T(8,128)(2,1)}, bf16[512,2048]{1,0:T(8,128)(2,1)}, bf16[2...) custom-call(bf16[512,2048]{1,0:T(8,128)(2,1)} %get-tuple-element.62.rows_ref, ...), custom_call_target="tpu_custom_call" | custom-call | tf_op jit(solution)/shard_map/feed_forward/pallas_call | solution.py:925
  641.8 174.7 %attend_backward.1 = (bf16[512,2560]{1,0:T(8,128)(2,1)}, f32[176,2048]{1,0:T(8,128)}, f32[64,2048]{1,0:T(8,128)}, f32[8,128]{1,0:T(8,128)}) custom-call(s32[1,2]{1,0:T(1,128)} %lengths.3, s32[1]{0:T(128)S(6)} %copy.40.counts, s32[1,2048]{1,0:T(1,128)} %segments.3, bf16[2048,512]{1,0:T(8,128)(2,1)} %get-tuple-element.71.q_ref, ...), custom_call_target="tpu_custom_call" | custom-call | tf_op jit(solution)/shard_map/attend_backward/pallas_call | solution.py:1173
  816.5 0.0 copy-start.15
  816.5 0.0 copy-start.16
  816.5 0.0 copy-start.17
  816.5 0.0 copy-start.1
  816.5 0.0 copy-start.8
  816.6 80.2 %last_sums.1 = (f32[64,2560]{1,0:T(8,128)}, f32[8,128]{1,0:T(8,128)}, f32[8,128]{1,0:T(8,128)}, f32[512,2048]{1,0:T(8,128)}) custom-call(bf16[512,2048]{1,0:T(8,128)(2,1)} %rows_ref.1, bf16[2048,512]{1,0:T(8,128)(2,1)} %get-tuple-element.70.turned_ref, bf16[512,2560]{1,0:T(8,128)(2,1)} %get-tuple-element.82.d_qkv_ref, f32[1,2048]{1,0:T(1,128)} %get-tuple-element.83.gain_ref, ...), custom_call_target="tpu_custom_call" | custom-call | tf_op jit(solution)/shard_map/last_sums/pallas_call | solution.py:1348
  896.8 1.2 slice.3
  898.8 0.0 copy-done.15
  898.8 0.0 copy-done.16
  898.8 0.0 copy-done.17
  898.8 1.3 multiply_subtract_fusion.4
  900.1 0.0 copy-done.1
  900.1 0.0 copy-done.8
  900.1 0.0 copy-start
  900.1 0.0 copy-start.3
  900.1 0.0 copy-start.4
  900.2 4.9 multiply_subtract_fusion.1
  905.0 0.0 copy-done
  905.0 0.0 copy-done.3
  905.0 1.1 copy-done.4
  906.1 0.0 copy-start.7
  906.1 0.0 copy-start.12
  906.1 0.0 copy-start.13
  906.1 7.1 multiply_subtract_fusion
  913.2 0.0 copy-start.5
  913.2 0.0 copy-start.9
  913.2 0.0 copy-start.10
  913.2 0.0 copy-start.11
  913.2 0.0 copy-done.7
  913.2 0.0 copy-done.12
  913.2 0.0 copy-done.13
  913.2 0.0 copy-done.14
  913.3 1.4 multiply_subtract_fusion.3
  914.7 0.0 copy-done.5
  914.7 0.1 copy-done.9
  914.8 0.4 copy-done.10
  915.3 0.2 copy-done.11
  915.5 0.0 copy-start.6
  915.5 1.6 multiply_subtract_fusion.2
  917.1 0.7 copy-done.6
  917.8 1.3 copy.41
  919.1 1.6 copy-done.2
  920.7 2.0 copy.42
  (2 shorter events, 0.0 us)
Async XLA Ops:
  816.5 82.3 %copy-start.15 = (f32[2,64]{1,0:T(2,128)S(1)}, f32[2,64]{1,0:T(2,128)}, u32[]{:S(2)}) copy-start(f32[2,64]{1,0:T(2,128)} %param.37) | copy-start | bytes 1540
  816.5 82.3 %copy-start.16 = (f32[2,64]{1,0:T(2,128)S(1)}, f32[2,64]{1,0:T(2,128)}, u32[]{:S(2)}) copy-start(f32[2,64]{1,0:T(2,128)} %param.38) | copy-start | bytes 1540
  816.5 82.3 %copy-start.17 = (f32[2,64]{1,0:T(2,128)S(1)}, f32[2,64]{1,0:T(2,128)}, u32[]{:S(2)}) copy-start(f32[2,64]{1,0:T(2,128)} %param.39) | copy-start | bytes 1540
  816.5 83.6 %copy-start.1 = (f32[176,2048]{1,0:T(8,128)S(1)}, f32[176,2048]{1,0:T(8,128)}, u32[]{:S(2)}) copy-start(f32[176,2048]{1,0:T(8,128)} %refs_4_.1) | copy-start | bytes 4325380
  816.5 83.6 %copy-start.8 = (f32[176,2048]{1,0:T(8,128)S(1)}, f32[176,2048]{1,0:T(8,128)}, u32[]{:S(2)}) copy-start(f32[176,2048]{1,0:T(8,128)} %param.35) | copy-start | bytes 4325380
  900.1 4.9 copy-start
  900.1 4.9 copy-start.3
  900.1 6.0 copy-start.4
  906.1 7.1 copy-start.7
  906.1 7.1 copy-start.12
  906.1 7.1 copy-start.13
  906.1 7.1 copy-start.14
  913.2 1.5 copy-start.5
  913.2 1.6 copy-start.9
  913.2 2.0 copy-start.10
  913.2 2.2 copy-start.11
  915.5 2.3 copy-start.6
  917.8 2.9 copy-start.2
